TPU v7x, 32 devices: a whole 2x2x4 slice. The times are simulated.
32 devices in a mesh: dp: 4 (over y, x), ctx: 2 (over core), head: 4 (over z).
Axes of the slice: x: 2, y: 2, z: 4, core: 2. Of those that a mesh axis runs over, the one named last changes fastest.
Arguments:
- queries: bfloat16 [4, 1024, 2048], P('dp', 'ctx', 'head'), may hold values from -6 to 6
- keys: bfloat16 [4, 1024, 2048], P('dp', 'ctx', 'head'), may hold values from -6 to 6
- values: bfloat16 [4, 1024, 2048], P('dp', 'ctx', 'head'), may hold values from -6 to 6
- decay: float32 [4, 16, 1024], P('dp', 'head', 'ctx'), may hold values from 0.4 to 1
- beta: float32 [4, 16, 1024], P('dp', 'head', 'ctx'), may hold values from 0 to 1
- inputs: bfloat16 [4, 1024, 4096], P('dp', 'ctx'), may hold values from -6 to 6
- probe: bfloat16 [4096, 2048], P(('dp', 'ctx'), 'head'), may hold values from -0.09375 to 0.09375
Outputs:
- mixed: bfloat16 [4, 1024, 2048], P('dp', 'ctx', 'head')
- curvature: float32 [4096, 2048], P(('dp', 'ctx'), 'head')
All inputs are finite; a program needn't handle non-finite values.
Results may differ from a plain program's by a relative error of at most 0.006.
Values may be sent and summed in bfloat16 or wider, within the bound.
No kernel may reach another device: no remote copies, remote signals or barrier semaphores. Data moves between devices by JAX's collectives and lax.ppermute only.
A program may use at most 128 MiB of HBM per device.

v0:
```python
import math

import jax
import jax.numpy as jnp
from jax import lax
from jax.sharding import PartitionSpec as P

D = 4096
DK = 128
SPAN = 64


EPSILON = 1e-06
EXACT = lax.Precision.HIGHEST


def contract(form, left, right):
    return jnp.einsum(form, left, right, precision=EXACT)


def narrow_contract(form, left, right):
    return jnp.einsum(form, left, right, preferred_element_type=jnp.float32)


def normalize(block):
    return block * lax.rsqrt(jnp.sum(block * block, -1, keepdims=True) + EPSILON)


def split_heads(block, head_count, span_count):
    return block.reshape(span_count, SPAN, head_count, -1).transpose(2, 0, 1, 3)


def join_heads(block):
    head_count, span_count, length_span, width = block.shape
    return block.transpose(1, 2, 0, 3).reshape(span_count * length_span, head_count * width)


def leading(block):
    return jnp.moveaxis(block, 1, 0)


def chain_pair(earlier, later):
    product = contract("...ij,...jk->...ik", earlier[0], later[0])
    carried = contract("...vj,...jk->...vk", earlier[1], later[0]) + later[1]
    return (product, carried)


def identity_pair(head_count, width):
    eye_block = jnp.broadcast_to(jnp.eye(DK, dtype=jnp.float32), (head_count, DK, DK))
    return (eye_block, jnp.zeros((head_count, width, DK), jnp.float32))


def compose(transit, summary, backwards):

    def advance(carried, element):
        return (chain_pair(carried, element), None)

    result, unused = lax.scan(
        advance,
        identity_pair(summary.shape[0], summary.shape[2]),
        (leading(transit), leading(summary)),
        reverse=backwards,
    )
    return result


def local(queries, keys, values, decay, beta, inputs, probe):
    length_dev = queries.shape[1]
    head_count = queries.shape[2] // DK
    span_count = length_dev // SPAN
    weighting = math.sqrt(D) / (lax.axis_size("dp") * lax.axis_size("ctx") * length_dev)
    input_rows = inputs[0]
    columns = input_rows
    tangent_full = jnp.dot(
        columns,
        lax.all_gather(probe, ("dp", "ctx"), axis=0, tiled=True),
        preferred_element_type=jnp.float32,
    )
    rounded = lax.optimization_barrier(
        (
            normalize(split_heads(queries[0].astype(jnp.float32), head_count, span_count)).astype(
                jnp.bfloat16
            ),
            normalize(split_heads(keys[0].astype(jnp.float32), head_count, span_count)).astype(
                jnp.bfloat16
            ),
            tangent_full.astype(jnp.bfloat16),
        )
    )
    queries_narrow = rounded[0]
    keys_narrow = rounded[1]
    tangent = rounded[2]
    queries_unit = queries_narrow.astype(jnp.float32)
    keys_unit = keys_narrow.astype(jnp.float32)
    paired = jnp.concatenate(
        [
            split_heads(values[0].astype(jnp.float32), head_count, span_count),
            split_heads(tangent.astype(jnp.float32), head_count, span_count),
        ],
        -1,
    )
    growth_log = jnp.cumsum(jnp.log(decay[0]).reshape(head_count, span_count, SPAN), -1)
    growth = jnp.exp(growth_log)
    strength = beta[0].reshape(head_count, span_count, SPAN)
    rows_index = lax.broadcasted_iota(jnp.int32, (SPAN, SPAN), 0)
    cols_index = lax.broadcasted_iota(jnp.int32, (SPAN, SPAN), 1)
    inclusive = rows_index >= cols_index
    strict = rows_index > cols_index
    spread = growth_log[..., :, None] - growth_log[..., None, :]
    ratios = jnp.where(inclusive, jnp.exp(jnp.where(inclusive, spread, 0.0)), 0.0)
    key_inner = narrow_contract("hnti,hnsi->hnts", keys_narrow, keys_narrow)
    coupling = jnp.where(strict, strength[..., :, None] * ratios * key_inner, 0.0)
    identity_span = jnp.eye(SPAN, dtype=jnp.float32)
    inverse = identity_span - coupling
    powers = coupling
    for degree in range(1, SPAN.bit_length() - 1):
        powers = contract("hnts,hnsu->hntu", powers, powers)
        inverse = contract("hnts,hnsu->hntu", inverse, identity_span + powers)
    right_side = jnp.concatenate(
        [strength[..., None] * paired, (strength * growth)[..., None] * keys_unit], -1
    )
    solved = contract("hnts,hnsw->hntw", inverse, right_side)
    new_values = solved[..., : 2 * DK]
    new_keys = solved[..., 2 * DK :]
    tail_keys = jnp.exp(growth_log[..., -1:] - growth_log)[..., None] * keys_unit
    identity_key = jnp.eye(DK, dtype=jnp.float32)
    transit = growth[..., -1, None, None] * identity_key - contract(
        "hnci,hncj->hnij", new_keys, tail_keys
    )
    summary = contract("hncv,hncj->hnvj", new_values, tail_keys)
    mixing = jnp.where(
        inclusive, ratios * narrow_contract("hnti,hnsi->hnts", queries_narrow, keys_narrow), 0.0
    )
    device_transit, device_summary = compose(transit, summary, False)
    position = lax.axis_index("ctx")
    all_transit, all_summary = (
        lax.all_gather(device_transit[None].astype(jnp.bfloat16), "ctx", axis=0, tiled=True).astype(
            jnp.float32
        ),
        lax.all_gather(device_summary[None].astype(jnp.bfloat16), "ctx", axis=0, tiled=True).astype(
            jnp.float32
        ),
    )

    def forward_fold(offset, carried):
        shifted = contract("hvi,hij->hvj", carried, all_transit[offset]) + all_summary[offset]
        return jnp.where(offset < position, shifted, carried)

    entry_state = lax.fori_loop(
        0, all_transit.shape[0], forward_fold, jnp.zeros_like(device_summary)
    )

    def forward_step(carried, element):
        (
            values_span,
            keys_span,
            queries_span,
            mixing_span,
            growth_span,
            transit_span,
            summary_span,
        ) = element
        fresh_values = values_span - contract("hcj,hvj->hcv", keys_span, carried)
        produced = growth_span[..., None] * contract(
            "hcj,hvj->hcv", queries_span, carried
        ) + contract("hts,hsv->htv", mixing_span, fresh_values)
        advanced = contract("hvi,hij->hvj", carried, transit_span) + summary_span
        return (advanced, produced)

    forward_items = (
        leading(new_values),
        leading(new_keys),
        leading(queries_unit),
        leading(mixing),
        leading(growth),
        leading(transit),
        leading(summary),
    )
    unused, produced_all = lax.scan(forward_step, entry_state, forward_items)
    outputs = jnp.moveaxis(produced_all, 0, 1)
    mixed = join_heads(outputs[..., :DK]).astype(jnp.bfloat16)
    grad_out = weighting * outputs[..., DK:]
    grad_fresh = contract("hnts,hntv->hnsv", mixing, grad_out)
    grads = contract("hncv,hncj->hnvj", grad_out, growth[..., None] * queries_unit) - contract(
        "hncv,hncj->hnvj", grad_fresh, new_keys
    )
    device_back, device_grad = compose(jnp.swapaxes(transit, -1, -2), grads, True)
    all_grads = lax.all_gather(
        device_grad[None].astype(jnp.bfloat16), "ctx", axis=0, tiled=True
    ).astype(jnp.float32)
    device_total = all_grads.shape[0]

    def reverse_fold(offset, carried):
        source = device_total - 1 - offset
        shifted = contract("hvj,hij->hvi", carried, all_transit[source]) + all_grads[source]
        return jnp.where(source > position, shifted, carried)

    exit_grad = lax.fori_loop(0, device_total, reverse_fold, jnp.zeros_like(device_grad))

    def reverse_step(grad_state, element):
        fresh_span, tail_span, inverse_span, strength_span, transit_span, grads_span = element
        grad_solved = fresh_span + contract("hcj,hvj->hcv", tail_span, grad_state)
        grad_span_values = strength_span[..., None] * contract(
            "hts,htv->hsv", inverse_span, grad_solved
        )
        previous = contract("hvj,hij->hvi", grad_state, transit_span) + grads_span
        return (previous, grad_span_values)

    reverse_items = (
        leading(grad_fresh),
        leading(tail_keys),
        leading(inverse),
        leading(strength),
        leading(transit),
        leading(grads),
    )
    unused_grad, grad_all = lax.scan(reverse_step, exit_grad, reverse_items, reverse=True)
    grad_values = join_heads(jnp.moveaxis(grad_all, 0, 1)).astype(jnp.bfloat16)
    columns = input_rows
    curvature = lax.psum_scatter(
        lax.dot_general(
            columns, grad_values, (((0,), (0,)), ((), ())), preferred_element_type=jnp.float32
        ),
        ("dp", "ctx"),
        scatter_dimension=0,
        tiled=True,
    )
    return (mixed[None], curvature)


def solution(mesh):
    return jax.shard_map(
        local,
        mesh=mesh,
        in_specs=(
            P("dp", "ctx", "head"),
            P("dp", "ctx", "head"),
            P("dp", "ctx", "head"),
            P("dp", "head", "ctx"),
            P("dp", "head", "ctx"),
            P("dp", "ctx", None),
            P(("dp", "ctx"), "head"),
        ),
        out_specs=(P("dp", "ctx", "head"), P(("dp", "ctx"), "head")),
        check_vma=False,
    )
```

profile of v0, /device:TPU:0, one launch (start us, length us, event | category | flops | bytes accessed | tf_op | source)
XLA Modules:
  0.0 351.1 jit_solution(12567347797043579141)
XLA Ops:
  22.9 26.4 %all-gather.5.cloned.1.call-done = bf16[4096,512]{1,0:T(8,128)(2,1)} async-done(((bf16[512,512]{1,0:T(8,128)(2,1)}), bf16[4096,512]{1,0:T(8,128)(2,1)}) %all-gather.5.cloned.1.call-update) | async-done | bytes 4194320 | tf_op jit(solution)/shard_map/all_gather | solution.py:76
  49.3 6.6 %fusion.72 = bf16[512,512]{1,0:T(8,128)(2,1)} fusion(bf16[4096,512]{1,0:T(8,128)(2,1)} %all-gather.5.cloned.1.call-done, bf16[1,512,4096]{2,1,0:T(8,128)(2,1)} %param.24), kind=kOutput, calls=%fused_computation.103 | convolution fusion | flops 2147745792 | bytes 8912896 | tf_op jit(solution)/shard_map/dot_general | solution.py:74
  66.2 2.7 fusion.85
  70.1 2.4 fusion.125
  74.7 3.1 fusion.64
  77.8 9.3 %convolution_bitcast_fusion.8 = f32[8,4,256,128]{3,2,0,1:T(8,128)} fusion(f32[4,8,64,384]{3,2,1,0:T(8,128)S(1)} %fusion.64, bf16[4,8,64,128]{3,2,1,0:T(8,128)(2,1)S(1)} %copy-done.6, f32[4,8,64]{2,1,0:T(8,128)S(1)} %get-tuple-element.923), kind=kOutput, calls=%fused_computation.87 | convolution fusion | flops 805830656 | bytes 6832128 | tf_op jit(solution)/shard_map/hncv,hncj->hnvj/dot_general | solution.py:18
  87.1 3.8 %fusion.71 = f32[4,8,128,128]{3,2,1,0:T(8,128)S(1)} fusion(bf16[4,8,64,128]{3,2,1,0:T(8,128)(2,1)S(1)} %copy-done.7, f32[4,8,64,384]{3,2,1,0:T(8,128)S(1)} %fusion.64, f32[4,8,64]{2,1,0:T(8,128)S(1)} %get-tuple-element.923), kind=kOutput, calls=%fused_computation.102 | convolution fusion | flops 403177472 | bytes 3686400 | tf_op jit(solution)/shard_map/hnci,hncj->hnij/dot_general | solution.py:18
  93.6 5.3 %copy.193 = f32[8,4,256,128]{2,3,1,0:T(8,128)} copy(f32[8,4,256,128]{3,2,0,1:T(8,128)} %convolution_bitcast_fusion.8) | data formatting | bytes 8388608
  100.8 3.5 bitcast_subtract_fusion
  106.3 22.9 %while.88 = (s32[]{:T(128)}, f32[4,128,128]{1,2,0:T(8,128)}, f32[4,256,128]{1,2,0:T(8,128)S(1)}, f32[8,4,128,128]{2,3,1,0:T(8,128)S(1)}, f32[8,4,256,128]{2,3,1,0:T(8,128)}, /*index=5*/s32[]{:T(128)}, s32[]{:T(128)}) while((s32[]{:T(128)}, f32[4,128,128]{1,2,0:T(8,128)}, f32[4,256,128]{1,2,0:T(8,128)S(1)}, ...), condition=%wide.region_4.5_spmd.clone, body=%wide.region_3.4_spmd.clone.sunk | while | flops 302252032 | bytes 5244023 | solution.py:58
  130.2 2.5 all-gather.1
  136.0 4.1 %while.89 = (s32[]{:T(128)}, f32[4,256,128]{1,2,0:T(8,128)S(1)}, s32[]{:T(128)}, f32[2,4,128,128]{3,2,1,0:T(8,128)S(1)}, f32[2,4,256,128]{3,2,1,0:T(8,128)}, /*index=5*/s32[]{:T(128)}, s32[]{:T(128)}) while((s32[]{:T(128)}, f32[4,256,128]{1,2,0:T(8,128)S(1)}, s32[]{:T(128)}, f32[2,4,128,128]{3,2,1,0:T(8,128)S(1)}, ...), condition=%wide.region_6.7_spmd.clone, body=%wide.region_5.6_spmd.clone.sunk | while | flops 201850880 | bytes 5506663 | solution.py:149
  142.0 51.5 %while.86 = (s32[]{:T(128)}, f32[4,256,128]{1,2,0:T(8,128)S(1)}, f32[8,4,64,256]{3,2,0,1:T(8,128)}, f32[8,4,128,128]{2,3,1,0:T(8,128)}, f32[8,4,256,128]{2,3,1,0...) while((s32[]{:T(128)}, f32[4,256,128]{1,2,0:T(8,128)S(1)}, ...), condition=%wide.region_8.9_spmd, body=%wide.region_7.8_spmd.sunk | while | flops 453312512 | bytes 6166645 | solution.py:179
  151.2 2.0 fusion.194
  189.6 2.0 fusion.194
  194.2 3.7 %fusion.82 = f32[4,8,64,128]{3,2,1,0:T(8,128)S(1)} fusion(f32[4,8,64,64]{3,2,1,0:T(8,128)} %get-tuple-element.927, f32[4,8,64,256]{3,2,1,0:T(8,128)} %bitcast.291, f32[4,8,64]{2,1,0:T(8,128)S(1)} %reduce_window_sum.11, pred[64,64]{1,0:T(8,128)(4,1)S(1)} %copy-done.18), kind=kOutput, calls=%fused_computation.118 | convolution fusion | flops 202244096 | bytes 3186688 | tf_op jit(solution)/shard_map/hnts,hntv->hnsv/dot_general | solution.py:18
  198.0 3.5 %fusion.80 = f32[4,8,128,128]{3,2,1,0:T(8,128)S(1)} fusion(f32[4,8,64,128]{3,0,2,1:T(4,128)S(1)} %convert_multiply_fusion.1, f32[4,8,64,256]{3,2,1,0:T(8,128)S(1)} %bitcast.293), kind=kOutput, calls=%fused_computation.116 | convolution fusion | flops 402915328 | bytes 4194304 | tf_op jit(solution)/shard_map/hncv,hncj->hnvj/dot_general | solution.py:18
  201.5 6.2 %subtract_bitcast_fusion = f32[8,4,128,128]{3,2,0,1:T(8,128)} fusion(f32[4,8,128,128]{3,2,1,0:T(8,128)S(1)} %fusion.80, f32[4,8,64,128]{3,2,1,0:T(8,128)S(1)} %fusion.82, f32[4,8,64,384]{3,2,1,0:T(8,128)} %copy-done), kind=kOutput, calls=%fused_computation.90 | convolution fusion | flops 403177472 | bytes 6291456 | tf_op jit(solution)/shard_map/hncv,hncj->hnvj/dot_general | solution.py:18
  209.7 11.2 %while.90 = (s32[]{:T(128)}, f32[4,128,128]{1,2,0:T(8,128)S(1)}, f32[8,4,128,128]{2,3,0,1:T(8,128)}, f32[8,4,128,128]{2,3,1,0:T(8,128)S(1)}, s32[]{:T(128)}, /*index=5*/s32[]{:T(128)}, s32[]{:T(128)}) while((s32[]{:T(128)}, f32[4,128,128]{1,2,0:T(8,128)S(1)}, f32[8,4,128,128]{2,3,0,1:T(8,128)}, ...), condition=%wide.region_10.11_spmd.clone, body=%wide.region_9.10_spmd.clone.sunk | while | flops 100794368 | bytes 1574498 | solution.py:58
  223.9 3.4 while.91
  227.4 34.4 %while.87 = (s32[]{:T(128)}, f32[4,128,128]{1,2,0:T(8,128)S(1)}, bf16[8,4,64,128]{3,2,1,0:T(8,128)(2,1)S(1)}, f32[8,4,128,128]{2,3,0,1:T(8,128)}, f32[8,4,128,12...) while((s32[]{:T(128)}, f32[4,128,128]{1,2,0:T(8,128)S(1)}, ...), condition=%wide.region_14.15_spmd, body=%wide.region_13.14_spmd.sunk | while | flops 176291840 | bytes 2628733 | solution.py:217
  262.2 7.8 %convolution_bitcast_fusion.7 = f32[4096,512]{0,1:T(8,128)} fusion(bf16[1,512,4096]{2,1,0:T(8,128)(2,1)} %param.24, bf16[64,8,4,128]{3,2,1,0:T(4,128)(2,1)S(1)} %bitcast.295), kind=kOutput, calls=%fused_computation.79 | convolution fusion | flops 2147483648 | bytes 13107200 | tf_op jit(solution)/shard_map/dot_general | solution.py:221
  272.8 68.7 %reduce-scatter.2.cloned.1.call-done = f32[512,512]{0,1:T(8,128)} async-done(((f32[4096,512]{0,1:T(8,128)}), f32[512,512]{0,1:T(8,128)}) %reduce-scatter.2.cloned.1.call-update) | async-done | bytes 1048592 | tf_op jit(solution)/shard_map/reduce_scatter | solution.py:220
  341.5 2.5 copy.222
  (285 shorter events, 172.1 us)
Async XLA Ops:
  7.2 42.2 %all-gather.5.cloned.1.call-start = ((), (), s32[]{:S(2)}) async-start(), calls=%async_computation.1 | async-start | bytes 4718592 | tf_op jit(solution)/shard_map/all_gather | solution.py:76
  7.9 333.6 %reduce-scatter.2.cloned.1.call-start = ((), (), s32[]{:S(2)}) async-start(), calls=%async_computation.2 | async-start | bytes 9437184 | tf_op jit(solution)/shard_map/reduce_scatter | solution.py:220
  9.4 3.0 copy-start.21
  9.4 3.1 copy-start.20
  17.1 4.1 %copy-start.15 = (f32[4,8,64]{0,2,1:T(8,128)S(1)}, f32[4,8,64]{0,2,1:T(8,128)}, u32[]{:S(2)}) copy-start(f32[4,8,64]{0,2,1:T(8,128)} %copy.187) | copy-start | bytes 24580
  22.9 33.1 %copy-start.6 = (bf16[4,8,64,128]{3,2,1,0:T(8,128)(2,1)S(1)}, bf16[4,8,64,128]{3,2,1,0:T(8,128)(2,1)}, u32[]{:S(2)}) copy-start(bf16[4,8,64,128]{3,2,1,0:T(8,128)(2,1)} %fusion.77) | copy-start | bytes 1572868
  22.9 33.0 %copy-start.17 = (pred[64,64]{1,0:T(8,128)(4,1)S(1)}, pred[64,64]{1,0:T(8,128)(4,1)}, u32[]{:S(2)}) copy-start(pred[64,64]{1,0:T(8,128)(4,1)} %get-tuple-element.928) | copy-start | bytes 12292
  22.9 33.0 %copy-start.22 = (pred[64,64]{1,0:T(8,128)(4,1)S(1)}, pred[64,64]{1,0:T(8,128)(4,1)}, u32[]{:S(2)}) copy-start(pred[64,64]{1,0:T(8,128)(4,1)} %get-tuple-element.929) | copy-start | bytes 12292
  68.9 3.6 %copy-start.16 = (f32[4,8,64]{2,1,0:T(8,128)S(1)}, f32[4,8,64]{2,1,0:T(8,128)}, u32[]{:S(2)}) copy-start(f32[4,8,64]{2,1,0:T(8,128)} %get-tuple-element.922) | copy-start | bytes 24580
  72.5 2.2 copy-start.9
  77.8 14.7 %copy-start = (f32[4,8,64,384]{3,2,1,0:T(8,128)}, f32[4,8,64,384]{3,2,1,0:T(8,128)S(1)}, u32[]{:S(2)}) copy-start(f32[4,8,64,384]{3,2,1,0:T(8,128)S(1)} %fusion.64) | copy-start | bytes 9437188
  77.8 9.3 %copy-start.7 = (bf16[4,8,64,128]{3,2,1,0:T(8,128)(2,1)S(1)}, bf16[4,8,64,128]{3,2,1,0:T(8,128)(2,1)}, u32[]{:S(2)}) copy-start(bf16[4,8,64,128]{3,2,1,0:T(8,128)(2,1)} %fusion.77) | copy-start | bytes 1572868
  98.9 1.8 copy-start.19
  112.0 1.7 copy-start.3
  126.3 1.7 copy-start.3
  129.2 6.7 %copy-start.1 = (f32[8,4,128,128]{2,3,1,0:T(8,128)}, f32[8,4,128,128]{2,3,1,0:T(8,128)S(1)}, u32[]{:S(2)}) copy-start(f32[8,4,128,128]{2,3,1,0:T(8,128)S(1)} %get-tuple-element.1327) | copy-start | bytes 6291460
  130.2 3.6 %copy-start.4 = (f32[4,128,128]{1,2,0:T(8,128)S(1)}, f32[4,128,128]{1,2,0:T(8,128)}, u32[]{:S(2)}) copy-start(f32[4,128,128]{1,2,0:T(8,128)} %get-tuple-element.576) | copy-start | bytes 786436
  135.9 4.2 %copy-start.11 = (bf16[4,8,64,128]{3,0,2,1:T(4,128)(2,1)S(1)}, bf16[4,8,64,128]{3,0,2,1:T(4,128)(2,1)}, u32[]{:S(2)}) copy-start(bf16[4,8,64,128]{3,0,2,1:T(4,128)(2,1)} %fusion.79) | copy-start | bytes 1572868
  135.9 4.3 %copy-start.8 = (bf16[4,8,64,128]{3,2,1,0:T(8,128)(2,1)S(1)}, bf16[4,8,64,128]{3,2,1,0:T(8,128)(2,1)}, u32[]{:S(2)}) copy-start(bf16[4,8,64,128]{3,2,1,0:T(8,128)(2,1)} %fusion.77) | copy-start | bytes 1572868
  136.0 4.3 %copy-start.18 = (pred[64,64]{1,0:T(8,128)(4,1)S(1)}, pred[64,64]{1,0:T(8,128)(4,1)}, u32[]{:S(2)}) copy-start(pred[64,64]{1,0:T(8,128)(4,1)} %get-tuple-element.928) | copy-start | bytes 12292
  142.0 51.6 %copy-start.14 = (f32[4,8,64]{0,2,1:T(8,128)S(1)}, f32[4,8,64]{0,2,1:T(8,128)}, u32[]{:S(2)}) copy-start(f32[4,8,64]{0,2,1:T(8,128)} %copy.208) | copy-start | bytes 24580
  193.6 4.4 %copy-start.12 = (f32[8,4,64,256]{3,2,0,1:T(8,128)S(1)}, f32[8,4,64,256]{3,2,0,1:T(8,128)}, u32[]{:S(2)}) copy-start(f32[8,4,64,256]{3,2,0,1:T(8,128)} %get-tuple-element.580) | copy-start | bytes 6291460
  198.0 3.5 %copy-start.10 = (f32[4,8,64,128]{3,2,1,0:T(8,128)}, f32[4,8,64,128]{3,2,1,0:T(8,128)S(1)}, u32[]{:S(2)}) copy-start(f32[4,8,64,128]{3,2,1,0:T(8,128)S(1)} %fusion.82) | copy-start | bytes 3145732
  207.7 2.0 copy-start.5
  (8 other events, 13.3 us)
Sparse Core Ops, SparseCore 0:
  9.9 39.4 all-gather.4
  270.2 71.2 reduce-scatter.1
where the time goes:
time: 356 us; the launch traced here: 351 us
  matrix products  175 us (49%)
  waiting for transfers between devices  95.8 us (27%)
  local copies, waits for them, and re-layouts  42.6 us (12%)
  between operations  14.9 us (4%)
  other arithmetic  14.5 us (4%)
  blocking collectives  6.5 us (2%)
    dot_general x100, matrix products, contract(): return jnp.einsum(form, left, right, precision=EXACT)  158 us
    reduce_scatter x1, waiting for transfers between devices, local(): lax.psum_scatter(lax.dot_general(columns, grad_values, (((0,), (0,)), (()...  68.7 us
    all_gather x1, waiting for transfers between devices, local(): lax.all_gather(probe, ('dp', 'ctx'), axis=0, tiled=True)  26.4 us
    unnamed x48, local copies, waits for them, and re-layouts  11.3 us
    dot_general x1, matrix products, local(): lax.dot_general(columns, grad_values, (((0,), (0,)), ((), ())), preferred...  7.83 us
  transfers between devices with their start and end apart: 2, of which 2 were waited for; matrix products, arithmetic and copies ran while one was open for 5% of the time, Pallas kernels for 0%

commit v1 on v0

v1 whole, which is shorter than its diff:
```python
import functools
import math

import jax
import jax.numpy as jnp
from jax import lax
from jax.experimental import pallas as pl
from jax.experimental.pallas import tpu as pltpu
from jax.sharding import PartitionSpec as P

D = 4096
DK = 128
SPAN = 128
EPSILON = 1e-06
GROUP = ("dp", "ctx")
BF16 = jnp.bfloat16
F32 = jnp.float32
VMEM_BYTES = 48 * 1024 * 1024


def dot(left, right):
    return jnp.dot(left, right, preferred_element_type=F32)


def dot_nt(left, right):
    return lax.dot_general(left, right, (((1,), (1,)), ((), ())), preferred_element_type=F32)


def dot_tn(left, right):
    return lax.dot_general(left, right, (((0,), (0,)), ((), ())), preferred_element_type=F32)


def halves(block):
    high = block.astype(BF16)
    return high, (block - high.astype(F32)).astype(BF16)


def fine_dot(left, right):
    left_high, left_low = halves(left)
    right_high, right_low = halves(right)
    wide = jnp.concatenate([right_high, right_low], 1)
    both = dot(jnp.concatenate([left_high, left_low], 1), jnp.concatenate([wide, wide], 0))
    width = right.shape[1]
    return both[:, :width] + both[:, width:]


def unit(block):
    block = block.astype(F32)
    return (block * lax.rsqrt(jnp.sum(block * block, -1, keepdims=True) + EPSILON)).astype(BF16)


def prepare_kernel(with_state, heads, chunks, *refs):
    if with_state:
        place, *refs = refs
        (qm, km, vm, qt, kt, vt, decay_m, beta_m, decay_t, beta_t, first, mixed, forth, back, last, state) = refs
    else:
        place, *refs = refs
        (qm, km, vm, qt, kt, vt, decay_m, beta_m, decay_t, beta_t, mixed, forth, back, last, state) = refs
    step = pl.program_id(0)
    core = place[0]
    is_mine = (step // (pl.num_programs(0) // 2)) == core

    @pl.when(step == 0)
    def _():
        if with_state:
            state[...] = first[...]
        else:
            state[...] = jnp.zeros_like(state)

    rows = lax.broadcasted_iota(jnp.int32, (SPAN, SPAN), 0)
    cols = lax.broadcasted_iota(jnp.int32, (SPAN, SPAN), 1)
    inclusive = rows >= cols
    strict = rows > cols
    diagonal = rows == cols

    def pick(mine, theirs):
        return jnp.where(is_mine, mine, theirs)

    def gates(mine, theirs):
        block = pick(mine[0], theirs[0])
        return jnp.where(core == 0, block[:heads], block[heads:])

    decay_log = jnp.log(gates(decay_m, decay_t))
    strengths = gates(beta_m, beta_t)
    queries, keys, values = (
        pick(mine[0], theirs[0]) for mine, theirs in ((qm, qt), (km, kt), (vm, vt))
    )
    items = [(chunk, head) for chunk in range(chunks) for head in range(heads)]

    def cut(block, item):
        chunk, head = item
        return block[chunk * SPAN : (chunk + 1) * SPAN, head * DK : (head + 1) * DK]

    def cut_row(block, item):
        chunk, head = item
        return block[head : head + 1, chunk * SPAN : (chunk + 1) * SPAN]

    def column_of(row):
        return jnp.sum(jnp.where(diagonal, row, 0.0), 1, keepdims=True)

    def row_of(column):
        return jnp.sum(jnp.where(diagonal, column, 0.0), 0, keepdims=True)

    q = [unit(cut(queries, item)) for item in items]
    k = [unit(cut(keys, item)) for item in items]
    v = [cut(values, item) for item in items]
    growth_log = [
        jnp.sum(jnp.where(inclusive, cut_row(decay_log, item), 0.0), 1, keepdims=True) for item in items
    ]
    strength_row = [cut_row(strengths, item) for item in items]
    inner = [dot_nt(jnp.concatenate([kk, qq], 0), kk) for kk, qq in zip(k, q)]
    ratios = [
        jnp.where(inclusive, jnp.exp(jnp.where(inclusive, log - row_of(log), 0.0)), 0.0)
        for log in growth_log
    ]
    coupling = [
        jnp.where(strict, column_of(row) * ratio * both[:SPAN], 0.0)
        for row, ratio, both in zip(strength_row, ratios, inner)
    ]
    mixing = [ratio * both[SPAN:] for ratio, both in zip(ratios, inner)]

    def lower_left(size):
        return (rows // (2 * size) == cols // (2 * size)) & (
            (rows // size) % 2 == 1
        ) & ((cols // size) % 2 == 0)

    identity = jnp.where(diagonal, 1.0, 0.0)
    corner = lower_left(1)
    inverse = [identity - jnp.where(corner, block, 0.0) for block in coupling]
    size = 2
    while size < SPAN:
        corner = lower_left(size)
        narrow = [block.astype(BF16) for block in inverse]
        part = [dot(x, jnp.where(corner, a, 0.0).astype(BF16)) for x, a in zip(narrow, coupling)]
        step_back = [dot(y.astype(BF16), x) for y, x in zip(part, narrow)]
        inverse = [x - z for x, z in zip(inverse, step_back)]
        size *= 2
    residual = [identity - x - fine_dot(a, x) for a, x in zip(coupling, inverse)]
    inverse = [
        x + dot(x.astype(BF16), e.astype(BF16)) for x, e in zip(inverse, residual)
    ]
    scaled = [x * row for x, row in zip(inverse, strength_row)]
    growth = [jnp.exp(log) for log in growth_log]
    grown_keys = [g * kk.astype(F32) for g, kk in zip(growth, k)]
    grown_queries = [g * qq.astype(F32) for g, qq in zip(growth, q)]
    tails = [
        (jnp.exp(log[SPAN - 1 :] - log) * kk.astype(F32)).T for log, kk in zip(growth_log, k)
    ]
    upper = [
        fine_dot(jnp.concatenate([tail, mix], 0), b) for tail, mix, b in zip(tails, mixing, scaled)
    ]
    removed = [fine_dot(up, gk) for up, gk in zip(upper, grown_keys)]
    maps = []
    for g, up, rem, gq in zip(growth, upper, removed, grown_queries):
        kept = jnp.where(diagonal, g[SPAN - 1 :], 0.0)
        maps.append(jnp.concatenate([jnp.concatenate([kept, gq], 0) - rem, up], 1))
    for item, whole in zip(items, maps):
        chunk, head = item
        forth[chunk, head] = whole.astype(BF16)
        back[chunk, head] = whole.T.astype(BF16)
    for chunk in range(chunks):
        for head in range(heads):
            index = chunk * heads + head
            high, low = halves(maps[index])
            x_high, x_low = halves(state[head])
            zero = jnp.zeros_like(v[index])
            wide = jnp.concatenate(
                [jnp.concatenate([x_high, x_low], 1), jnp.concatenate([v[index], zero], 1)], 0
            )
            both = dot(high, wide)
            result = both[:, :DK] + both[:, DK:] + dot(low, wide[:, :DK])
            state[head] = result[:DK]
            mixed[chunk * SPAN : (chunk + 1) * SPAN, head * DK : (head + 1) * DK] = result[DK:].astype(BF16)

    @pl.when(step == pl.num_programs(0) - 1)
    def _():
        last[...] = state[...]


def prepare(core, own, other, first):
    tokens = own[0].shape[1]
    width = own[0].shape[2] // 2
    heads = width // DK
    chunks = 2
    length = chunks * SPAN
    per_device = tokens // length
    steps = 2 * per_device
    total = 2 * tokens // SPAN
    wide = pl.BlockSpec((1, length, width), lambda i, place: (0, i % per_device, place[0]))
    gate = pl.BlockSpec((1, 2 * heads, length), lambda i, place: (0, 0, i % per_device))
    states = pl.BlockSpec((heads, DK, DK), lambda i, place: (0, 0, 0))
    maps = pl.BlockSpec((chunks, heads, 2 * DK, 2 * DK), lambda i, place: (i, 0, 0, 0))
    extra = () if first is None else (first,)
    return pl.pallas_call(
        functools.partial(prepare_kernel, first is not None, heads, chunks),
        grid_spec=pltpu.PrefetchScalarGridSpec(
            num_scalar_prefetch=1,
            grid=(steps,),
            in_specs=[wide] * 6 + [gate] * 4 + [states] * len(extra),
            out_specs=[pl.BlockSpec((length, width), lambda i, place: (i, 0)), maps, maps, states],
            scratch_shapes=[pltpu.VMEM((heads, DK, DK), F32)],
        ),
        out_shape=[
            jax.ShapeDtypeStruct((2 * tokens, width), BF16),
            jax.ShapeDtypeStruct((total, heads, 2 * DK, 2 * DK), BF16),
            jax.ShapeDtypeStruct((total, heads, 2 * DK, 2 * DK), BF16),
            jax.ShapeDtypeStruct((heads, DK, DK), F32),
        ],
        compiler_params=pltpu.CompilerParams(vmem_limit_bytes=VMEM_BYTES),
        name="prepare",
    )(core, *own[:3], *other[:3], own[3], own[4], other[3], other[4], *extra)


def column_copies(place, first, count, rows, mine, theirs, buffer, sems):
    copies = []
    for index in range(count):
        start = pl.multiple_of(place[first + index] * rows, rows)
        for which, source in enumerate((mine, theirs)):
            copies.append(
                pltpu.make_async_copy(
                    source.at[:, pl.ds(start, rows)], buffer.at[index, which], sems.at[index, which]
                )
            )
    return copies


def tangent_kernel(count, place, mine, theirs, *refs):
    pieces, (total, buffer, sems) = refs[:count], refs[count:]
    tokens = mine.shape[0]
    rows = pieces[0].shape[0]
    copies = column_copies(place, 1, count, rows, mine, theirs, buffer, sems)
    for copy in copies:
        copy.start()
    core = place[0]
    offsets = [pl.multiple_of(core * tokens, tokens), pl.multiple_of((1 - core) * tokens, tokens)]
    for index in range(count):
        for which in range(2):
            copies[2 * index + which].wait()
            part = dot(buffer[index, which], pieces[index][...])
            place_rows = pl.ds(offsets[which], tokens)
            if index == 0:
                total[place_rows, :] = part
            else:
                total[place_rows, :] += part


def tangent(core, mine, theirs, blocks, pieces):
    count = len(pieces)
    rows, width = pieces[0].shape
    tokens = mine.shape[0]
    any_spec = pl.BlockSpec(memory_space=pl.ANY)
    vmem_spec = pl.BlockSpec(memory_space=pltpu.VMEM)
    return pl.pallas_call(
        functools.partial(tangent_kernel, count),
        grid_spec=pltpu.PrefetchScalarGridSpec(
            num_scalar_prefetch=1,
            grid=(),
            in_specs=[any_spec] * 2 + [vmem_spec] * count,
            out_specs=vmem_spec,
            scratch_shapes=[
                pltpu.VMEM((count, 2, tokens, rows), BF16),
                pltpu.SemaphoreType.DMA((count, 2)),
            ],
        ),
        out_shape=jax.ShapeDtypeStruct((2 * tokens, width), F32),
        compiler_params=pltpu.CompilerParams(vmem_limit_bytes=VMEM_BYTES),
        name="tangent",
    )(jnp.stack([core] + list(blocks)), mine, theirs, *pieces)


def recur_kernel(weighting, with_state, count, place, mine, theirs, total, forth, back, *refs):
    pieces, refs = refs[:count], refs[count:]
    if with_state:
        (first, final, *refs) = refs
    (grads, last, start, buffer, forth_in, back_in, tangent_in, up, sems, map_sems) = refs
    tokens = mine.shape[0]
    rows = pieces[0].shape[0]
    spans, heads = forth.shape[:2]
    copies = column_copies(place, 1, count, rows, mine, theirs, buffer, sems)
    for copy in copies:
        copy.start()
    forth_copy = pltpu.make_async_copy(forth, forth_in, map_sems.at[0])
    back_copy = pltpu.make_async_copy(back, back_in, map_sems.at[1])
    forth_copy.start()
    back_copy.start()
    core = place[0]
    for which, owner in enumerate((core, 1 - core)):
        place_rows = pl.ds(pl.multiple_of(owner * tokens, tokens), tokens)
        part = total[place_rows, :]
        for index in range(count):
            copies[2 * index + which].wait()
            part += dot(buffer[index, which], pieces[index][...])
        tangent_in[place_rows, :] = part.astype(BF16)
    forth_copy.wait()
    back_copy.wait()
    zero = jnp.zeros((DK, DK), F32)
    states = [first[head] if with_state else zero for head in range(heads)]
    for span in range(spans):
        for head in range(heads):
            block = tangent_in[span * SPAN : (span + 1) * SPAN, head * DK : (head + 1) * DK]
            fresh = dot(forth_in[span, head, :, DK:], block)
            result = dot(forth_in[span, head, :, :DK], states[head].astype(BF16)) + fresh
            states[head] = result[:DK]
            grad = (weighting * result[DK:]).astype(BF16)
            up[span, head] = dot(back_in[span, head, :, DK:], grad)
    for head in range(heads):
        last[head] = states[head]
    states = [final[head] if with_state else zero for head in range(heads)]
    for span in reversed(range(spans)):
        for head in range(heads):
            result = dot(back_in[span, head, :, :DK], states[head].astype(BF16)) + up[span, head]
            states[head] = result[:DK]
            grads[span * SPAN : (span + 1) * SPAN, head * DK : (head + 1) * DK] = result[DK:].astype(BF16)
    for head in range(heads):
        start[head] = states[head]


def recur(weighting, core, mine, theirs, total, forth, back, blocks, pieces, states):
    count = len(pieces)
    rows, width = pieces[0].shape
    tokens = mine.shape[0]
    spans, heads = forth.shape[:2]
    any_spec = pl.BlockSpec(memory_space=pl.ANY)
    vmem_spec = pl.BlockSpec(memory_space=pltpu.VMEM)
    extra = () if states is None else states
    return pl.pallas_call(
        functools.partial(recur_kernel, weighting, states is not None, count),
        grid_spec=pltpu.PrefetchScalarGridSpec(
            num_scalar_prefetch=1,
            grid=(),
            in_specs=[any_spec] * 2
            + [vmem_spec]
            + [any_spec] * 2
            + [vmem_spec] * (count + len(extra)),
            out_specs=[vmem_spec] * 3,
            scratch_shapes=[
                pltpu.VMEM((count, 2, tokens, rows), BF16),
                pltpu.VMEM(forth.shape, BF16),
                pltpu.VMEM(back.shape, BF16),
                pltpu.VMEM((2 * tokens, width), BF16),
                pltpu.VMEM((spans, heads, 2 * DK, DK), F32),
                pltpu.SemaphoreType.DMA((count, 2)),
                pltpu.SemaphoreType.DMA((2,)),
            ],
        ),
        out_shape=[
            jax.ShapeDtypeStruct((2 * tokens, width), BF16),
            jax.ShapeDtypeStruct((heads, DK, DK), F32),
            jax.ShapeDtypeStruct((heads, DK, DK), F32),
        ],
        compiler_params=pltpu.CompilerParams(vmem_limit_bytes=VMEM_BYTES),
        name="recur",
    )(jnp.stack([core] + list(blocks)), mine, theirs, total, forth, back, *pieces, *extra)


ROWS = 256


def curvature_kernel(counts, place, mine, theirs, grads, *refs):
    outs, (buffer, sems) = refs[: len(counts)], refs[len(counts) :]
    count = sum(counts)
    tokens = mine.shape[0]
    copies = column_copies(place, 1, count, ROWS, mine, theirs, buffer, sems)
    for copy in copies:
        copy.start()
    core = place[0]
    both = [
        grads[pl.ds(pl.multiple_of(owner * tokens, tokens), tokens), :] for owner in (core, 1 - core)
    ]
    index = 0
    for out, length in zip(outs, counts):
        for slot in range(length):
            copies[2 * index].wait()
            copies[2 * index + 1].wait()
            part = dot_tn(buffer[index, 0], both[0]) + dot_tn(buffer[index, 1], both[1])
            out[slot] = part.astype(out.dtype)
            index += 1


def curvature(core, mine, theirs, grads, blocks, types):
    counts = tuple(len(part) for part in blocks)
    tokens = mine.shape[0]
    width = grads.shape[1]
    any_spec = pl.BlockSpec(memory_space=pl.ANY)
    vmem_spec = pl.BlockSpec(memory_space=pltpu.VMEM)
    return pl.pallas_call(
        functools.partial(curvature_kernel, counts),
        grid_spec=pltpu.PrefetchScalarGridSpec(
            num_scalar_prefetch=1,
            grid=(),
            in_specs=[any_spec] * 2 + [vmem_spec],
            out_specs=[vmem_spec] * len(counts),
            scratch_shapes=[
                pltpu.VMEM((sum(counts), 2, tokens, ROWS), BF16),
                pltpu.SemaphoreType.DMA((sum(counts), 2)),
            ],
        ),
        out_shape=[
            jax.ShapeDtypeStruct((count, ROWS, width), kind) for count, kind in zip(counts, types)
        ],
        compiler_params=pltpu.CompilerParams(vmem_limit_bytes=VMEM_BYTES),
        name="curvature",
    )(jnp.stack([core] + [index for part in blocks for index in part]), mine, theirs, grads)


def local(square, dp_size, ctx_size, queries, keys, values, decay, beta, inputs, probe):
    tokens = queries.shape[1]
    width = queries.shape[2] // 2
    weighting = math.sqrt(D) / (dp_size * ctx_size * tokens)
    ctx = lax.axis_index("ctx")
    chip = lax.axis_index("dp")
    core = lax.rem(ctx, 2)
    groups = ctx_size // 2
    partner = [(index, index ^ 1) for index in range(ctx_size)]
    mine = inputs[0]

    def swap(block):
        return lax.ppermute(block, "ctx", partner)

    def send(block, chips, cores):
        pairs = [
            (2 * index + which, 2 * (index ^ chips) + (which ^ cores))
            for index in range(dp_size)
            for which in range(2)
        ]
        return lax.ppermute(block, GROUP, pairs)

    def part(block, index):
        return lax.dynamic_slice_in_dim(block, index * width, width, 1)

    own = (queries, keys, values, decay, beta)
    if square:
        kept = part(probe, core)
        given = part(probe, 1 - core)
        x_one = send(kept, 1, 0)
        y_one = send(given, 2, 1)
        other = tuple(swap(block) for block in own)
        inside = swap(given)
        x_two = send(given, 1, 1)
        y_two = send(kept, 2, 0)
        theirs = swap(mine)
        far_one = send(x_one, 2, 0)
        far_two = send(y_one, 1, 0)
        pieces = [kept, inside, x_one, y_one, x_two, y_two, far_one, far_two]

        def block_at(chips, cores):
            return 2 * (chip ^ chips) + (core ^ cores)

        places = [
            block_at(0, 0),
            block_at(0, 1),
            block_at(1, 0),
            block_at(2, 1),
            block_at(1, 1),
            block_at(2, 0),
            block_at(3, 0),
            block_at(3, 1),
        ]
    else:
        other = tuple(swap(block) for block in own)
        theirs = swap(mine)
        gathered = part(lax.all_gather(probe, GROUP, axis=0, tiled=True), core)
        places = list(range(8))
        rows = D // len(places)
        pieces = [gathered[index * rows : (index + 1) * rows] for index in places]
    places = [jnp.asarray(index, jnp.int32) for index in places]

    def shift(block, by):
        pairs = [
            (index, index + 2 * by)
            for index in range(ctx_size)
            if 0 <= index + 2 * by < ctx_size
        ]
        return lax.ppermute(block, "ctx", pairs)

    early = len(pieces) - 2
    entry = None
    if groups > 1:
        entry = jnp.zeros((width // DK, DK, DK), F32)
        for _ in range(groups - 1):
            entry = shift(prepare(core[None], own, other, entry)[3], 1)
    read, forth, back, unused = prepare(core[None], own, other, entry)
    read_swapped = swap(lax.dynamic_slice_in_dim(read, (1 - core) * tokens, tokens, 0))
    read_kept = lax.dynamic_slice_in_dim(read, core * tokens, tokens, 0)
    mixed = jnp.where(
        core == 0,
        jnp.concatenate([read_kept, read_swapped], 1),
        jnp.concatenate([read_swapped, read_kept], 1),
    )
    total = tangent(core, mine, theirs, places[:early], pieces[:early])
    run = functools.partial(
        recur, weighting, core, mine, theirs, total, forth, back, places[early:], pieces[early:]
    )
    states = None
    if groups > 1:
        states = (jnp.zeros((width // DK, DK, DK), F32),) * 2
        for _ in range(groups - 1):
            states = (shift(run(states)[1], 1), states[1])
        for _ in range(groups - 1):
            states = (states[0], shift(run(states)[2], -1))
    grads = run(states)[0]
    build = functools.partial(curvature, core, mine, theirs, grads)
    if not square:
        everything = build([[jnp.int32(index) for index in range(D // ROWS)]], [F32])[0]
        flat = everything.reshape(D, width)
        zero = jnp.zeros_like(flat)
        both = jnp.where(
            core == 0, jnp.concatenate([flat, zero], 1), jnp.concatenate([zero, flat], 1)
        )
        return mixed[None], lax.psum_scatter(both, GROUP, scatter_dimension=0, tiled=True)

    def rows_at(chips, half):
        return [4 * (chip ^ chips) + 2 * which + half for which in range(2)]

    far_x, far_y = build([rows_at(3, 0), rows_at(3, 1)], [BF16] * 2)
    far_x = send(far_x, 1, 0)
    far_y = send(far_y, 2, 0)
    near_x, near_y = build([rows_at(1, 0), rows_at(2, 1)], [BF16] * 2)
    near_x = send(near_x, 1, 0)
    near_y = send(near_y, 2, 0)
    keep_y, keep_x, own_top, own_low = build(
        [rows_at(2, 0), rows_at(1, 1), rows_at(0, 0), rows_at(0, 1)], [F32] * 4
    )

    def at(block, index):
        return lax.dynamic_index_in_dim(block, index, 0, keepdims=False)

    relay_y = (keep_y + far_x.astype(F32)).astype(BF16)
    relay_x = (keep_x + far_y.astype(F32)).astype(BF16)
    top_same = send(at(relay_y, core), 2, 0)
    low_same = send(at(relay_x, core), 1, 0)
    top_cross = send(at(relay_y, 1 - core), 2, 1)
    low_cross = send(at(relay_x, 1 - core), 1, 1)
    sum_top = own_top + near_x.astype(F32)
    sum_low = own_low + near_y.astype(F32)
    sums = jnp.concatenate([sum_top, sum_low], 1)
    across = swap(at(sums, 1 - core))
    near = at(sums, core) + jnp.concatenate([top_same, low_same], 0).astype(F32)
    distant = across + jnp.concatenate([top_cross, low_cross], 0).astype(F32)
    result = jnp.where(
        core == 0, jnp.concatenate([near, distant], 1), jnp.concatenate([distant, near], 1)
    )
    return mixed[None], result


def solution(mesh):
    dp_size, ctx_size = mesh.shape["dp"], mesh.shape["ctx"]
    square = dp_size == 4 and ctx_size == 2
    return jax.shard_map(
        functools.partial(local, square, dp_size, ctx_size),
        mesh=mesh,
        in_specs=(
            P("dp", "ctx", "head"),
            P("dp", "ctx", "head"),
            P("dp", "ctx", "head"),
            P("dp", "head", "ctx"),
            P("dp", "head", "ctx"),
            P("dp", "ctx", None),
            P(("dp", "ctx"), "head"),
        ),
        out_specs=(P("dp", "ctx", "head"), P(("dp", "ctx"), "head")),
        check_vma=False,
    )
```

time: 356 us -> 93.4 us (0.26); the launches traced: 351 us -> 92.9 us
  matrix products: 175 us -> 0 us
  waiting for transfers between devices: 95.8 us -> 18 us
  Pallas kernels: 0 us -> 42.9 us
  local copies, waits for them, and re-layouts: 42.6 us -> 10.2 us
  starting transfers between devices: 0.08 us -> 17.6 us
  between operations: 14.9 us -> 0.82 us
  other arithmetic: 14.5 us -> 3.42 us
  blocking collectives: 6.5 us -> 0 us
    dot_general x104 -> x0, matrix products: 175 us -> none  [the longest x100 158 us: contract(): return jnp.einsum(form, left, right, precision=EXACT)]
    reduce_scatter x1 -> x0, waiting for transfers between devices: 68.7 us -> none  [local(): lax.psum_scatter(lax.dot_general(columns, grad_values, (((0,), (0,)), (()...]
    pallas_call x0 -> x6, Pallas kernels: none -> 42.9 us  [the longest x1 13.4 us: prepare(): pl.pallas_call(functools.partial(prepare_kernel, first is not None, heads...]
    all_gather x1 -> x0, waiting for transfers between devices: 26.4 us -> none  [local(): lax.all_gather(probe, ('dp', 'ctx'), axis=0, tiled=True)]
    ppermute x0 -> x23, waiting for transfers between devices: none -> 18 us  [the longest x14 15.9 us: send(): return lax.ppermute(block, GROUP, pairs)]
    ppermute x0 -> x23, starting transfers between devices: none -> 17.6 us  [the longest x14 15.5 us: send(): return lax.ppermute(block, GROUP, pairs)]
    dynamic_slice x32 -> x1, local copies, waits for them, and re-layouts: 10.9 us -> 1.76 us  [part(): return lax.dynamic_slice_in_dim(block, index * width, width, 1)]
    all_gather x3 -> x0, blocking collectives: 6.5 us -> none  [the longest x1 2.51 us: local(): lax.all_gather(device_summary[None].astype(jnp.bfloat16), 'ctx', axis=0,...]
  transfers between devices with their start and end apart: 2 -> 23, of which waited for: 2 -> 9; matrix products, arithmetic and copies ran while one was open for 5% -> 6% of each run, Pallas kernels for 0% -> 32%
where the time goes in v1:
time: 93.4 us; the launch traced here: 92.9 us
  Pallas kernels  42.9 us (46%)
  waiting for transfers between devices  18 us (19%)
  starting transfers between devices  17.6 us (19%)
  local copies, waits for them, and re-layouts  10.2 us (11%)
  other arithmetic  3.42 us (4%)
    ppermute x14, waiting for transfers between devices, send(): return lax.ppermute(block, GROUP, pairs)  15.9 us
    ppermute x14, starting transfers between devices, send(): return lax.ppermute(block, GROUP, pairs)  15.5 us
    pallas_call x1, Pallas kernels, prepare(): pl.pallas_call(functools.partial(prepare_kernel, first is not None, heads...  13.4 us
    pallas_call x3, Pallas kernels, curvature(): pl.pallas_call(functools.partial(curvature_kernel, counts), grid_spec=plt...  12 us
    pallas_call x1, Pallas kernels, recur(): pl.pallas_call(functools.partial(recur_kernel, weighting, states is not N...  9.66 us
    pallas_call x1, Pallas kernels, tangent(): pl.pallas_call(functools.partial(tangent_kernel, count), grid_spec=pltpu....  7.78 us
    unnamed x14, local copies, waits for them, and re-layouts  6.71 us
    ppermute x9, waiting for transfers between devices, swap(): return lax.ppermute(block, 'ctx', partner)  2.13 us
  transfers between devices with their start and end apart: 23, of which 9 were waited for; matrix products, arithmetic and copies ran while one was open for 6% of the time, Pallas kernels for 32%

profile of v1, /device:TPU:0, one launch (start us, length us, event | category | flops | bytes accessed | tf_op | source)
XLA Modules:
  0.0 92.9 jit_solution(11129344387665932286)
XLA Ops:
  1.1 1.8 %constant_dynamic-slice_fusion = (bf16[512,256]{1,0:T(8,128)(2,1)}, bf16[512,256]{1,0:T(8,128)(2,1)S(1)}) fusion(bf16[512,512]{1,0:T(8,128)(2,1)} %param.13, s32[]{:T(128)S(6)} %select_n.53, s32[]{:T(128)S(6)} %select_n.52), kind=kLoop, calls=%fused_computation.21 | loop fusion | bytes 1048584 | tf_op jit(solution)/shard_map/dynamic_slice | solution.py:429
  3.5 2.9 %collective-permute-start.8 = (bf16[512,256]{1,0:T(8,128)(2,1)S(1)}, bf16[512,256]{1,0:T(8,128)(2,1)S(1)}, u32[]{:S(2)}, u32[]{:S(2)}) collective-permute-start(bf16[512,256]{1,0:T(8,128)(2,1)S(1)} %get-tuple-element.27.refs_0_), channel_id=1, source_target_pairs={{0,8},{4,12},{8,0},{12,4},{16,24},{20,28},{24,16},{28,20},{1,9},{5... | collective-permute-start | bytes 786440 | tf_op jit(solution)/shard_map/ppermute | solution.py:426
  6.4 2.1 %collective-permute-done.3.refs_9_ = f32[1,4,512]{2,1,0:T(4,128)S(1)} collective-permute-done((f32[1,4,512]{2,1,0:T(4,128)}, f32[1,4,512]{2,1,0:T(4,128)S(1)}, u32[]{:S(2)}, u32[]{:S(2)}) %collective-permute-start.3) | collective-permute-done | bytes 8224 | tf_op jit(solution)/shard_map/ppermute | solution.py:418
  9.4 3.5 %collective-permute-done.8.refs_2_ = bf16[512,256]{1,0:T(8,128)(2,1)S(1)} collective-permute-done((bf16[512,256]{1,0:T(8,128)(2,1)S(1)}, bf16[512,256]{1,0:T(8,128)(2,1)S(1)}, u32[]{:S(2)}, u32[]{:S(2)}) %collective-permute-start.8) | collective-permute-done | bytes 262176 | tf_op jit(solution)/shard_map/ppermute | solution.py:426
  13.5 7.9 %collective-permute-done.9.refs_3_ = bf16[512,256]{1,0:T(8,128)(2,1)S(1)} collective-permute-done((bf16[512,256]{1,0:T(8,128)(2,1)}, bf16[512,256]{1,0:T(8,128)(2,1)S(1)}, u32[]{:S(2)}, u32[]{:S(2)}) %collective-permute-start.9) | collective-permute-done | bytes 262176 | tf_op jit(solution)/shard_map/ppermute | solution.py:426
  21.4 1.7 %collective-permute-start.10 = (bf16[512,256]{1,0:T(8,128)(2,1)}, bf16[512,256]{1,0:T(8,128)(2,1)}, u32[]{:S(2)}, u32[]{:S(2)}) collective-permute-start(bf16[512,256]{1,0:T(8,128)(2,1)} %get-tuple-element.26), channel_id=1, source_target_pairs={{0,12},{4,8},{8,4},{12,0},{16,28},{20,24},{24,20},{28,16},{1,13},{... | collective-permute-start | bytes 786440 | tf_op jit(solution)/shard_map/ppermute | solution.py:426
  23.5 1.6 %collective-permute-start.12 = (bf16[512,256]{1,0:T(8,128)(2,1)S(1)}, bf16[512,256]{1,0:T(8,128)(2,1)S(1)}, u32[]{:S(2)}, u32[]{:S(2)}) collective-permute-start(bf16[512,256]{1,0:T(8,128)(2,1)S(1)} %collective-permute-done.8.refs_2_), channel_id=1, source_target_pairs={{0,16},{4,20},{8,24},{12,28},{16,0},{20,4},{24,8},{28,12},{1,17},{... | collective-permute-start | bytes 786440 | tf_op jit(solution)/shard_map/ppermute | solution.py:426
  25.7 1.0 %copy-done.2 = bf16[1,512,512]{2,1,0:T(8,128)(2,1)S(1)} copy-done((bf16[1,512,512]{2,1,0:T(8,128)(2,1)S(1)}, bf16[1,512,512]{2,1,0:T(8,128)(2,1)}, u32[]{:S(2)}) %copy-start.2) | copy-done | bytes 524312
  26.7 1.0 %copy-done.3 = bf16[1,512,512]{2,1,0:T(8,128)(2,1)S(1)} copy-done((bf16[1,512,512]{2,1,0:T(8,128)(2,1)S(1)}, bf16[1,512,512]{2,1,0:T(8,128)(2,1)}, u32[]{:S(2)}) %copy-start.3) | copy-done | bytes 524312
  27.8 1.0 %copy-done.4 = bf16[1,512,512]{2,1,0:T(8,128)(2,1)S(1)} copy-done((bf16[1,512,512]{2,1,0:T(8,128)(2,1)S(1)}, bf16[1,512,512]{2,1,0:T(8,128)(2,1)}, u32[]{:S(2)}) %copy-start.4) | copy-done | bytes 524312
  30.2 13.4 %prepare.1 = (bf16[1024,256]{1,0:T(8,128)(2,1)S(1)}, bf16[8,2,256,256]{3,2,1,0:T(8,128)(2,1)S(1)}, bf16[8,2,256,256]{3,2,1,0:T(8,128)(2,1)}, f32[2,128,128]{2,1,0:T(8,128)}) custom-call(s32[1]{0:T(128)} %bitcast.refs_0_, bf16[1,512,512]{2,1,0:T(8,128)(2,1)S(1)} %copy-done.2, bf16[1,512,512]{2,1,0:T(8,128)(2,1)S(1)} %copy-done.3, ...), custom_call_target="tpu_custom_call" | custom-call | tf_op jit(solution)/shard_map/prepare/pallas_call | solution.py:194
  43.7 7.8 %tangent.1.total = f32[1024,256]{1,0:T(8,128)S(1)} custom-call(s32[7]{0:T(128)S(1)} %stack.110.place, bf16[512,4096]{1,0:T(8,128)(2,1)} %bitcast.44, bf16[512,4096]{1,0:T(8,128)(2,1)} %collective-permute-done.6.theirs, bf16[512,256]{1,0:T(8,128)(2,1)S(1)} %get-tuple-element.27.refs_0_, bf16[512,256]{1,0:T(8,128)(2,1)S(1)} %collective-permute-done.7.refs_1_, ...), custom_call_target="tpu_custom_call" | custom-call | tf_op jit(solution)/shard_map/tangent/pallas_call | solution.py:253
  51.5 9.7 %recur.1 = (bf16[1024,256]{1,0:T(8,128)(2,1)S(1)}, f32[2,128,128]{2,1,0:T(8,128)}, f32[2,128,128]{2,1,0:T(8,128)}) custom-call(s32[3]{0:T(128)S(1)} %pad_add_fusion.place, bf16[512,4096]{1,0:T(8,128)(2,1)} %bitcast.45, bf16[512,4096]{1,0:T(8,128)(2,1)} %collective-permute-done.6.theirs, f32[1024,256]{1,0:T(8,128)S(1)} %tangent.1.total, ...), custom_call_target="tpu_custom_call" | custom-call | tf_op jit(solution)/shard_map/recur/pallas_call | solution.py:326
  61.2 3.4 %curvature.4 = (bf16[2,256,256]{2,1,0:T(8,128)(2,1)S(1)}, bf16[2,256,256]{2,1,0:T(8,128)(2,1)S(1)}) custom-call(s32[5]{0:T(128)S(1)} %stack.115.place, bf16[512,4096]{1,0:T(8,128)(2,1)S(1)} %bitcast.47, bf16[512,4096]{1,0:T(8,128)(2,1)} %collective-permute-done.6.theirs, bf16[1024,256]{1,0:T(8,128)(2,1)S(1)} %get-tuple-element.17.grads), custom_call_target="tpu_custom_call" | custom-call | tf_op jit(solution)/shard_map/curvature/pallas_call | solution.py:386
  64.6 1.8 %collective-permute-start.14 = (bf16[2,256,256]{2,1,0:T(8,128)(2,1)S(1)}, bf16[2,256,256]{2,1,0:T(8,128)(2,1)S(1)}, u32[]{:S(2)}, u32[]{:S(2)}) collective-permute-start(bf16[2,256,256]{2,1,0:T(8,128)(2,1)S(1)} %get-tuple-element.19), channel_id=1, source_target_pairs={{0,8},{4,12},{8,0},{12,4},{16,24},{20,28},{24,16},{28,20},{1,9},{5... | collective-permute-start | bytes 786440 | tf_op jit(solution)/shard_map/ppermute | solution.py:426
  67.0 2.2 %copy-done.1 = bf16[1,512,4096]{2,1,0:T(8,128)(2,1)S(1)} copy-done((bf16[1,512,4096]{2,1,0:T(8,128)(2,1)S(1)}, bf16[1,512,4096]{2,1,0:T(8,128)(2,1)}, u32[]{:S(2)}) %copy-start.1) | copy-done | bytes 4194328
  69.2 3.4 %curvature.5 = (bf16[2,256,256]{2,1,0:T(8,128)(2,1)S(1)}, bf16[2,256,256]{2,1,0:T(8,128)(2,1)S(1)}) custom-call(s32[5]{0:T(128)S(1)} %stack.120.place, bf16[512,4096]{1,0:T(8,128)(2,1)S(1)} %bitcast.48, bf16[512,4096]{1,0:T(8,128)(2,1)} %collective-permute-done.6.theirs, bf16[1024,256]{1,0:T(8,128)(2,1)S(1)} %get-tuple-element.17.grads), custom_call_target="tpu_custom_call" | custom-call | tf_op jit(solution)/shard_map/curvature/pallas_call | solution.py:386
  72.6 1.7 %collective-permute-start.18 = (bf16[2,256,256]{2,1,0:T(8,128)(2,1)S(1)}, bf16[2,256,256]{2,1,0:T(8,128)(2,1)S(1)}, u32[]{:S(2)}, u32[]{:S(2)}) collective-permute-start(bf16[2,256,256]{2,1,0:T(8,128)(2,1)S(1)} %get-tuple-element.25), channel_id=1, source_target_pairs={{0,16},{4,20},{8,24},{12,28},{16,0},{20,4},{24,8},{28,12},{1,17},{... | collective-permute-start | bytes 786440 | tf_op jit(solution)/shard_map/ppermute | solution.py:426
  74.6 5.3 %curvature.3 = (f32[2,256,256]{2,1,0:T(8,128)S(1)}, f32[2,256,256]{2,1,0:T(8,128)S(1)}, f32[2,256,256]{2,1,0:T(8,128)S(1)}, f32[2,256,256]{2,1,0:T(8,128)S(1)}) custom-call(s32[9]{0:T(128)S(1)} %stack.100.place, bf16[512,4096]{1,0:T(8,128)(2,1)} %bitcast.46, bf16[512,4096]{1,0:T(8,128)(2,1)} %collective-permute-done.6.theirs, ...), custom_call_target="tpu_custom_call" | custom-call | tf_op jit(solution)/shard_map/curvature/pallas_call | solution.py:386
  80.1 1.2 %collective-permute-done.18 = bf16[2,256,256]{2,1,0:T(8,128)(2,1)S(1)} collective-permute-done((bf16[2,256,256]{2,1,0:T(8,128)(2,1)S(1)}, bf16[2,256,256]{2,1,0:T(8,128)(2,1)S(1)}, u32[]{:S(2)}, u32[]{:S(2)}) %collective-permute-start.18) | collective-permute-done | bytes 262176 | tf_op jit(solution)/shard_map/ppermute | solution.py:426
  81.4 1.4 %collective-permute-done.16 = bf16[2,256,256]{2,1,0:T(8,128)(2,1)S(1)} collective-permute-done((bf16[2,256,256]{2,1,0:T(8,128)(2,1)S(1)}, bf16[2,256,256]{2,1,0:T(8,128)(2,1)S(1)}, u32[]{:S(2)}, u32[]{:S(2)}) %collective-permute-start.16) | collective-permute-done | bytes 262176 | tf_op jit(solution)/shard_map/ppermute | solution.py:426
  84.5 1.0 %collective-permute-start.17 = (bf16[256,256]{1,0:T(8,128)(2,1)S(1)}, bf16[256,256]{1,0:T(8,128)(2,1)}, u32[]{:S(2)}, u32[]{:S(2)}) collective-permute-start(bf16[256,256]{1,0:T(8,128)(2,1)S(1)} %get-tuple-element.30), channel_id=1, source_target_pairs={{0,16},{4,20},{8,24},{12,28},{16,0},{20,4},{24,8},{28,12},{1,17},{... | collective-permute-start | bytes 393224 | tf_op jit(solution)/shard_map/ppermute | solution.py:426
  85.5 2.5 %collective-permute-start.21 = (bf16[256,256]{1,0:T(8,128)(2,1)}, bf16[256,256]{1,0:T(8,128)(2,1)S(1)}, u32[]{:S(2)}, u32[]{:S(2)}) collective-permute-start(bf16[256,256]{1,0:T(8,128)(2,1)} %get-tuple-element.31), channel_id=1, source_target_pairs={{0,20},{4,16},{8,28},{12,24},{16,4},{20,0},{24,12},{28,8},{1,21},{... | collective-permute-start | bytes 393224 | tf_op jit(solution)/shard_map/ppermute | solution.py:426
  91.7 1.1 %maximum_select_fusion = f32[512,512]{1,0:T(8,128)} fusion(f32[512,256]{1,0:T(8,128)S(1)} %convert_add_fusion, f32[512,256]{1,0:T(8,128)S(1)} %fusion.4, pred[]{:T(512)S(6)} %eq.4), kind=kLoop, calls=%fused_computation.4 | loop fusion | flops 786432 | bytes 2097153 | tf_op jit(solution)/shard_map/jit(_where)/select_n | solution.py:540
  (59 shorter events, 11.5 us)
Async XLA Ops:
  0.6 43.0 %collective-permute-start.6 = (bf16[512,4096]{1,0:T(8,128)(2,1)}, bf16[512,4096]{1,0:T(8,128)(2,1)}, u32[]{:S(2)}, u32[]{:S(2)}) collective-permute-start(bf16[512,4096]{1,0:T(8,128)(2,1)} %bitcast.43), channel_id=1, source_target_pairs={{0,4},{4,0},{1,5},{5,1},{2,6},{6,2},{3,7},{7,3},{8,12},{12,8},{9,1... | collective-permute-start | bytes 12582920 | tf_op jit(solution)/shard_map/ppermute | solution.py:418
  2.9 6.1 %collective-permute-start.7 = (bf16[512,256]{1,0:T(8,128)(2,1)}, bf16[512,256]{1,0:T(8,128)(2,1)S(1)}, u32[]{:S(2)}, u32[]{:S(2)}) collective-permute-start(bf16[512,256]{1,0:T(8,128)(2,1)} %get-tuple-element.26), channel_id=1, source_target_pairs={{0,4},{4,0},{1,5},{5,1},{2,6},{6,2},{3,7},{7,3},{8,12},{12,8},{9,1... | collective-permute-start | bytes 786440 | tf_op jit(solution)/shard_map/ppermute | solution.py:418
  3.0 5.6 %collective-permute-start.3 = (f32[1,4,512]{2,1,0:T(4,128)}, f32[1,4,512]{2,1,0:T(4,128)S(1)}, u32[]{:S(2)}, u32[]{:S(2)}) collective-permute-start(f32[1,4,512]{2,1,0:T(4,128)} %refs_7_.1), channel_id=1, source_target_pairs={{0,4},{4,0},{1,5},{5,1},{2,6},{6,2},{3,7},{7,3},{8,12},{12,8},{9,1... | collective-permute-start | bytes 24584 | tf_op jit(solution)/shard_map/ppermute | solution.py:418
  3.4 5.5 %collective-permute-start.4 = (f32[1,4,512]{2,1,0:T(4,128)}, f32[1,4,512]{2,1,0:T(4,128)S(1)}, u32[]{:S(2)}, u32[]{:S(2)}) collective-permute-start(f32[1,4,512]{2,1,0:T(4,128)} %refs_8_.1), channel_id=1, source_target_pairs={{0,4},{4,0},{1,5},{5,1},{2,6},{6,2},{3,7},{7,3},{8,12},{12,8},{9,1... | collective-permute-start | bytes 24584 | tf_op jit(solution)/shard_map/ppermute | solution.py:418
  3.5 9.4 %collective-permute-start.8 = (bf16[512,256]{1,0:T(8,128)(2,1)S(1)}, bf16[512,256]{1,0:T(8,128)(2,1)S(1)}, u32[]{:S(2)}, u32[]{:S(2)}) collective-permute-start(bf16[512,256]{1,0:T(8,128)(2,1)S(1)} %get-tuple-element.27.refs_0_), channel_id=1, source_target_pairs={{0,8},{4,12},{8,0},{12,4},{16,24},{20,28},{24,16},{28,20},{1,9},{5... | collective-permute-start | bytes 786440 | tf_op jit(solution)/shard_map/ppermute | solution.py:426
  8.5 14.6 %collective-permute-start = (bf16[1,512,512]{2,1,0:T(8,128)(2,1)}, bf16[1,512,512]{2,1,0:T(8,128)(2,1)S(1)}, u32[]{:S(2)}, u32[]{:S(2)}) collective-permute-start(bf16[1,512,512]{2,1,0:T(8,128)(2,1)} %refs_1_.1), channel_id=1, source_target_pairs={{0,4},{4,0},{1,5},{5,1},{2,6},{6,2},{3,7},{7,3},{8,12},{12,8},{9,1... | collective-permute-start | bytes 1572872 | tf_op jit(solution)/shard_map/ppermute | solution.py:418
  8.9 14.6 %collective-permute-start.1 = (bf16[1,512,512]{2,1,0:T(8,128)(2,1)}, bf16[1,512,512]{2,1,0:T(8,128)(2,1)S(1)}, u32[]{:S(2)}, u32[]{:S(2)}) collective-permute-start(bf16[1,512,512]{2,1,0:T(8,128)(2,1)} %refs_2_.1), channel_id=1, source_target_pairs={{0,4},{4,0},{1,5},{5,1},{2,6},{6,2},{3,7},{7,3},{8,12},{12,8},{9,1... | collective-permute-start | bytes 1572872 | tf_op jit(solution)/shard_map/ppermute | solution.py:418
  9.0 16.1 %collective-permute-start.2 = (bf16[1,512,512]{2,1,0:T(8,128)(2,1)}, bf16[1,512,512]{2,1,0:T(8,128)(2,1)S(1)}, u32[]{:S(2)}, u32[]{:S(2)}) collective-permute-start(bf16[1,512,512]{2,1,0:T(8,128)(2,1)} %refs_3_.1), channel_id=1, source_target_pairs={{0,4},{4,0},{1,5},{5,1},{2,6},{6,2},{3,7},{7,3},{8,12},{12,8},{9,1... | collective-permute-start | bytes 1572872 | tf_op jit(solution)/shard_map/ppermute | solution.py:418
  12.9 8.5 %collective-permute-start.9 = (bf16[512,256]{1,0:T(8,128)(2,1)}, bf16[512,256]{1,0:T(8,128)(2,1)S(1)}, u32[]{:S(2)}, u32[]{:S(2)}) collective-permute-start(bf16[512,256]{1,0:T(8,128)(2,1)} %get-tuple-element.26), channel_id=1, source_target_pairs={{0,20},{4,16},{8,28},{12,24},{16,4},{20,0},{24,12},{28,8},{1,21},{... | collective-permute-start | bytes 786440 | tf_op jit(solution)/shard_map/ppermute | solution.py:426
  21.4 22.2 %collective-permute-start.10 = (bf16[512,256]{1,0:T(8,128)(2,1)}, bf16[512,256]{1,0:T(8,128)(2,1)}, u32[]{:S(2)}, u32[]{:S(2)}) collective-permute-start(bf16[512,256]{1,0:T(8,128)(2,1)} %get-tuple-element.26), channel_id=1, source_target_pairs={{0,12},{4,8},{8,4},{12,0},{16,28},{20,24},{24,20},{28,16},{1,13},{... | collective-permute-start | bytes 786440 | tf_op jit(solution)/shard_map/ppermute | solution.py:426
  23.1 20.5 %collective-permute-start.11 = (bf16[512,256]{1,0:T(8,128)(2,1)S(1)}, bf16[512,256]{1,0:T(8,128)(2,1)}, u32[]{:S(2)}, u32[]{:S(2)}) collective-permute-start(bf16[512,256]{1,0:T(8,128)(2,1)S(1)} %get-tuple-element.27.refs_0_), channel_id=1, source_target_pairs={{0,16},{4,20},{8,24},{12,28},{16,0},{20,4},{24,8},{28,12},{1,17},{... | collective-permute-start | bytes 786440 | tf_op jit(solution)/shard_map/ppermute | solution.py:426
  23.5 27.9 %collective-permute-start.12 = (bf16[512,256]{1,0:T(8,128)(2,1)S(1)}, bf16[512,256]{1,0:T(8,128)(2,1)S(1)}, u32[]{:S(2)}, u32[]{:S(2)}) collective-permute-start(bf16[512,256]{1,0:T(8,128)(2,1)S(1)} %collective-permute-done.8.refs_2_), channel_id=1, source_target_pairs={{0,16},{4,20},{8,24},{12,28},{16,0},{20,4},{24,8},{28,12},{1,17},{... | collective-permute-start | bytes 786440 | tf_op jit(solution)/shard_map/ppermute | solution.py:426
  25.2 26.3 %collective-permute-start.13 = (bf16[512,256]{1,0:T(8,128)(2,1)S(1)}, bf16[512,256]{1,0:T(8,128)(2,1)}, u32[]{:S(2)}, u32[]{:S(2)}) collective-permute-start(bf16[512,256]{1,0:T(8,128)(2,1)S(1)} %collective-permute-done.9.refs_3_), channel_id=1, source_target_pairs={{0,8},{4,12},{8,0},{12,4},{16,24},{20,28},{24,16},{28,20},{1,9},{5... | collective-permute-start | bytes 786440 | tf_op jit(solution)/shard_map/ppermute | solution.py:426
  51.5 9.7 %copy-start = (bf16[1,512,4096]{2,1,0:T(8,128)(2,1)S(1)}, bf16[1,512,4096]{2,1,0:T(8,128)(2,1)}, u32[]{:S(2)}) copy-start(bf16[1,512,4096]{2,1,0:T(8,128)(2,1)} %param.12) | copy-start | bytes 12582916
  64.6 15.3 %collective-permute-start.14 = (bf16[2,256,256]{2,1,0:T(8,128)(2,1)S(1)}, bf16[2,256,256]{2,1,0:T(8,128)(2,1)S(1)}, u32[]{:S(2)}, u32[]{:S(2)}) collective-permute-start(bf16[2,256,256]{2,1,0:T(8,128)(2,1)S(1)} %get-tuple-element.19), channel_id=1, source_target_pairs={{0,8},{4,12},{8,0},{12,4},{16,24},{20,28},{24,16},{28,20},{1,9},{5... | collective-permute-start | bytes 786440 | tf_op jit(solution)/shard_map/ppermute | solution.py:426
  66.5 13.4 %collective-permute-start.15 = (bf16[2,256,256]{2,1,0:T(8,128)(2,1)S(1)}, bf16[2,256,256]{2,1,0:T(8,128)(2,1)S(1)}, u32[]{:S(2)}, u32[]{:S(2)}) collective-permute-start(bf16[2,256,256]{2,1,0:T(8,128)(2,1)S(1)} %get-tuple-element.21), channel_id=1, source_target_pairs={{0,16},{4,20},{8,24},{12,28},{16,0},{20,4},{24,8},{28,12},{1,17},{... | collective-permute-start | bytes 786440 | tf_op jit(solution)/shard_map/ppermute | solution.py:426
  66.9 18.5 %collective-permute-start.5 = (bf16[512,256]{1,0:T(8,128)(2,1)S(1)}, bf16[512,256]{1,0:T(8,128)(2,1)S(1)}, u32[]{:S(2)}, u32[]{:S(2)}) collective-permute-start(bf16[512,256]{1,0:T(8,128)(2,1)S(1)} %get-tuple-element.29), channel_id=1, source_target_pairs={{0,4},{4,0},{1,5},{5,1},{2,6},{6,2},{3,7},{7,3},{8,12},{12,8},{9,1... | collective-permute-start | bytes 786440 | tf_op jit(solution)/shard_map/ppermute | solution.py:418
  72.6 8.8 %collective-permute-start.18 = (bf16[2,256,256]{2,1,0:T(8,128)(2,1)S(1)}, bf16[2,256,256]{2,1,0:T(8,128)(2,1)S(1)}, u32[]{:S(2)}, u32[]{:S(2)}) collective-permute-start(bf16[2,256,256]{2,1,0:T(8,128)(2,1)S(1)} %get-tuple-element.25), channel_id=1, source_target_pairs={{0,16},{4,20},{8,24},{12,28},{16,0},{20,4},{24,8},{28,12},{1,17},{... | collective-permute-start | bytes 786440 | tf_op jit(solution)/shard_map/ppermute | solution.py:426
  74.3 8.4 %collective-permute-start.16 = (bf16[2,256,256]{2,1,0:T(8,128)(2,1)S(1)}, bf16[2,256,256]{2,1,0:T(8,128)(2,1)S(1)}, u32[]{:S(2)}, u32[]{:S(2)}) collective-permute-start(bf16[2,256,256]{2,1,0:T(8,128)(2,1)S(1)} %get-tuple-element.23), channel_id=1, source_target_pairs={{0,8},{4,12},{8,0},{12,4},{16,24},{20,28},{24,16},{28,20},{1,9},{5... | collective-permute-start | bytes 786440 | tf_op jit(solution)/shard_map/ppermute | solution.py:426
  80.1 11.6 %collective-permute-start.20 = (f32[512,256]{1,0:T(8,128)S(1)}, f32[512,256]{1,0:T(8,128)S(1)}, u32[]{:S(2)}, u32[]{:S(2)}) collective-permute-start(f32[512,256]{1,0:T(8,128)S(1)} %fusion.1), channel_id=1, source_target_pairs={{0,4},{4,0},{1,5},{5,1},{2,6},{6,2},{3,7},{7,3},{8,12},{12,8},{9,1... | collective-permute-start | bytes 1572872 | tf_op jit(solution)/shard_map/ppermute | solution.py:418
  83.5 5.4 %collective-permute-start.19 = (bf16[256,256]{1,0:T(8,128)(2,1)}, bf16[256,256]{1,0:T(8,128)(2,1)S(1)}, u32[]{:S(2)}, u32[]{:S(2)}) collective-permute-start(bf16[256,256]{1,0:T(8,128)(2,1)} %get-tuple-element.32), channel_id=1, source_target_pairs={{0,8},{4,12},{8,0},{12,4},{16,24},{20,28},{24,16},{28,20},{1,9},{5... | collective-permute-start | bytes 393224 | tf_op jit(solution)/shard_map/ppermute | solution.py:426
  84.5 5.1 %collective-permute-start.17 = (bf16[256,256]{1,0:T(8,128)(2,1)S(1)}, bf16[256,256]{1,0:T(8,128)(2,1)}, u32[]{:S(2)}, u32[]{:S(2)}) collective-permute-start(bf16[256,256]{1,0:T(8,128)(2,1)S(1)} %get-tuple-element.30), channel_id=1, source_target_pairs={{0,16},{4,20},{8,24},{12,28},{16,0},{20,4},{24,8},{28,12},{1,17},{... | collective-permute-start | bytes 393224 | tf_op jit(solution)/shard_map/ppermute | solution.py:426
  85.5 5.8 %collective-permute-start.22 = (bf16[256,256]{1,0:T(8,128)(2,1)S(1)}, bf16[256,256]{1,0:T(8,128)(2,1)S(1)}, u32[]{:S(2)}, u32[]{:S(2)}) collective-permute-start(bf16[256,256]{1,0:T(8,128)(2,1)S(1)} %get-tuple-element.33), channel_id=1, source_target_pairs={{0,12},{4,8},{8,4},{12,0},{16,28},{20,24},{24,20},{28,16},{1,13},{... | collective-permute-start | bytes 393224 | tf_op jit(solution)/shard_map/ppermute | solution.py:426
  85.5 6.2 %collective-permute-start.21 = (bf16[256,256]{1,0:T(8,128)(2,1)}, bf16[256,256]{1,0:T(8,128)(2,1)S(1)}, u32[]{:S(2)}, u32[]{:S(2)}) collective-permute-start(bf16[256,256]{1,0:T(8,128)(2,1)} %get-tuple-element.31), channel_id=1, source_target_pairs={{0,20},{4,16},{8,28},{12,24},{16,4},{20,0},{24,12},{28,8},{1,21},{... | collective-permute-start | bytes 393224 | tf_op jit(solution)/shard_map/ppermute | solution.py:426
  (6 other events, 6.7 us)

commit v2 on v0

v2 whole, which is shorter than its diff:
```python
import functools
import math

import jax
import jax.numpy as jnp
from jax import lax
from jax.experimental import pallas as pl
from jax.experimental.pallas import tpu as pltpu
from jax.sharding import PartitionSpec as P

D = 4096
DK = 128
SPAN = 128
EPSILON = 1e-06
GROUP = ("dp", "ctx")
BF16 = jnp.bfloat16
F32 = jnp.float32
VMEM_BYTES = 24 * 1024 * 1024


def cost(us):
    return pl.CostEstimate(flops=int(us * 1.1e9), bytes_accessed=int(us * 3.0e6), transcendentals=0)


def in_hbm(block):
    return pltpu.with_memory_space_constraint(block, pltpu.HBM)


def in_vmem(block):
    return pltpu.with_memory_space_constraint(block, pltpu.VMEM)


def kernel_call(kernel, name, place, operands, outs, scratch=(), aliases=None, far=()):
    vmem_spec = pl.BlockSpec(memory_space=pltpu.VMEM)
    return pl.pallas_call(
        kernel,
        grid_spec=pltpu.PrefetchScalarGridSpec(
            num_scalar_prefetch=1,
            grid=(),
            in_specs=[pl.BlockSpec(memory_space=pltpu.HBM)] * len(far) + [vmem_spec] * len(operands),
            out_specs=[vmem_spec] * len(outs),
            scratch_shapes=list(scratch),
        ),
        out_shape=[jax.ShapeDtypeStruct(shape, kind) for shape, kind in outs],
        input_output_aliases=aliases or {},
        compiler_params=pltpu.CompilerParams(vmem_limit_bytes=VMEM_BYTES),
        cost_estimate=cost(0.01),
        name=name,
    )(place, *(in_hbm(block) for block in far), *(in_vmem(block) for block in operands))


def dot(left, right):
    return jnp.dot(left, right, preferred_element_type=F32)


def dot_nt(left, right):
    return lax.dot_general(left, right, (((1,), (1,)), ((), ())), preferred_element_type=F32)


def dot_tn(left, right):
    return lax.dot_general(left, right, (((0,), (0,)), ((), ())), preferred_element_type=F32)


def halves(block):
    high = block.astype(BF16)
    return high, (block - high.astype(F32)).astype(BF16)


def fine_dot(left, right):
    left_high, left_low = halves(left)
    right_high, right_low = halves(right)
    wide = jnp.concatenate([right_high, right_low], 1)
    both = dot(jnp.concatenate([left_high, left_low], 1), jnp.concatenate([wide, wide], 0))
    width = right.shape[1]
    return both[:, :width] + both[:, width:]


def unit(block):
    block = block.astype(F32)
    return (block * lax.rsqrt(jnp.sum(block * block, -1, keepdims=True) + EPSILON)).astype(BF16)


def pack_kernel(place, queries, keys, values, decay, beta, probe, kept, given, own, stack, gates, sems):
    core = place[0]
    width = kept.shape[1]
    same = pl.ds(pl.multiple_of(core * width, width), width)
    cross = pl.ds(pl.multiple_of((1 - core) * width, width), width)
    moves = [(probe.at[:, same], kept), (probe.at[:, cross], given)]
    moves += [(block.at[0, :, cross], stack.at[i]) for i, block in enumerate((queries, keys, values))]
    moves += [(block.at[0, :, same], own.at[i]) for i, block in enumerate((queries, keys, values))]
    if stack.shape[0] > 3:
        moves.append((probe.at[:, cross], stack.at[3]))
    moves += [(decay.at[0], gates.at[0]), (beta.at[0], gates.at[1])]
    copies = [
        pltpu.make_async_copy(source, target, sems.at[i]) for i, (source, target) in enumerate(moves)
    ]
    for copy in copies:
        copy.start()
    for copy in copies:
        copy.wait()


def pack(place, with_probe, queries, keys, values, decay, beta, probe):
    tokens = queries.shape[1]
    width = queries.shape[2] // 2
    hbm_spec = pl.BlockSpec(memory_space=pltpu.HBM)
    vmem_spec = pl.BlockSpec(memory_space=pltpu.VMEM)
    half = jax.ShapeDtypeStruct((probe.shape[0], width), BF16)
    return pl.pallas_call(
        pack_kernel,
        grid_spec=pltpu.PrefetchScalarGridSpec(
            num_scalar_prefetch=1,
            grid=(),
            in_specs=[hbm_spec] * 6,
            out_specs=[vmem_spec] * 5,
            scratch_shapes=[pltpu.SemaphoreType.DMA((11,))],
        ),
        out_shape=[
            half,
            half,
            jax.ShapeDtypeStruct((3, tokens, width), BF16),
            jax.ShapeDtypeStruct((4 if with_probe else 3, tokens, width), BF16),
            jax.ShapeDtypeStruct((2,) + decay.shape[1:], F32),
        ],
        compiler_params=pltpu.CompilerParams(vmem_limit_bytes=VMEM_BYTES),
        cost_estimate=cost(0.01),
        name="pack",
    )(place, *(in_hbm(block) for block in (queries, keys, values, decay, beta, probe)))


def prepare_kernel(side, place, stack, gates, *refs):
    forth, forth_low, back = refs[-3:]
    core = place[0]
    owner = core if side == 0 else 1 - core
    queries, keys = stack[0], stack[1]
    tokens, width = queries.shape
    spans, heads = tokens // SPAN, width // DK
    rows = lax.broadcasted_iota(jnp.int32, (SPAN, SPAN), 0)
    cols = lax.broadcasted_iota(jnp.int32, (SPAN, SPAN), 1)
    inclusive = rows >= cols
    strict = rows > cols
    diagonal = rows == cols
    items = [(span, head) for span in range(spans) for head in range(heads)]

    def gate(index):
        return jnp.where(core == 0, gates[index, :heads], gates[index, heads:])

    def cut(block, item):
        span, head = item
        return block[span * SPAN : (span + 1) * SPAN, head * DK : (head + 1) * DK]

    def cut_row(block, item):
        span, head = item
        return block[head : head + 1, span * SPAN : (span + 1) * SPAN]

    def column_of(row):
        return jnp.sum(jnp.where(diagonal, row, 0.0), 1, keepdims=True)

    def row_of(column):
        return jnp.sum(jnp.where(diagonal, column, 0.0), 0, keepdims=True)

    def lower_left(size):
        return (
            (rows // (2 * size) == cols // (2 * size))
            & ((rows // size) % 2 == 1)
            & ((cols // size) % 2 == 0)
        )

    decay_log = jnp.log(gate(0))
    strengths = gate(1)
    identity = jnp.where(diagonal, 1.0, 0.0)

    def build(items):
        q = [unit(cut(queries, item)) for item in items]
        k = [unit(cut(keys, item)) for item in items]
        growth_log = [
            jnp.sum(jnp.where(inclusive, cut_row(decay_log, item), 0.0), 1, keepdims=True)
            for item in items
        ]
        strength_row = [cut_row(strengths, item) for item in items]
        inner = [dot_nt(jnp.concatenate([kk, qq], 0), kk) for kk, qq in zip(k, q)]
        ratios = [
            jnp.where(inclusive, jnp.exp(jnp.where(inclusive, log - row_of(log), 0.0)), 0.0)
            for log in growth_log
        ]
        coupling = [
            jnp.where(strict, column_of(row) * ratio * both[:SPAN], 0.0)
            for row, ratio, both in zip(strength_row, ratios, inner)
        ]
        mixing = [ratio * both[SPAN:] for ratio, both in zip(ratios, inner)]
        corner = lower_left(1)
        inverse = [identity - jnp.where(corner, block, 0.0) for block in coupling]
        size = 2
        while size < SPAN:
            corner = lower_left(size)
            narrow = [block.astype(BF16) for block in inverse]
            part = [
                dot(x, jnp.where(corner, a, 0.0).astype(BF16)) for x, a in zip(narrow, coupling)
            ]
            step_back = [dot(y.astype(BF16), x) for y, x in zip(part, narrow)]
            inverse = [x - z for x, z in zip(inverse, step_back)]
            size *= 2
        residual = [identity - x - fine_dot(a, x) for a, x in zip(coupling, inverse)]
        inverse = [x + dot(x.astype(BF16), e.astype(BF16)) for x, e in zip(inverse, residual)]
        scaled = [x * row for x, row in zip(inverse, strength_row)]
        growth = [jnp.exp(log) for log in growth_log]
        grown_keys = [g * kk.astype(F32) for g, kk in zip(growth, k)]
        grown_queries = [g * qq.astype(F32) for g, qq in zip(growth, q)]
        tails = [
            (jnp.exp(log[SPAN - 1 :] - log) * kk.astype(F32)).T for log, kk in zip(growth_log, k)
        ]
        upper = [
            fine_dot(jnp.concatenate([tail, mix], 0), b)
            for tail, mix, b in zip(tails, mixing, scaled)
        ]
        removed = [fine_dot(up, gk) for up, gk in zip(upper, grown_keys)]
        for item, g, up, rem, gq in zip(items, growth, upper, removed, grown_queries):
            span, head = item
            kept = jnp.where(diagonal, g[SPAN - 1 :], 0.0)
            whole = jnp.concatenate([jnp.concatenate([kept, gq], 0) - rem, up], 1)
            high, low = halves(whole)
            forth[owner, span, head] = high
            forth_low[owner, span, head] = low
            back[owner, span, head] = whole.T.astype(BF16)

    for start in range(0, len(items), BATCH):
        build(items[start : start + BATCH])


BATCH = 8


def prepare(place, side, stack, gates, maps):
    tokens = stack.shape[1]
    heads = gates.shape[1] // 2
    shape = (2, tokens // SPAN, heads, 2 * DK, 2 * DK)
    return kernel_call(
        functools.partial(prepare_kernel, side),
        "prepare",
        place,
        (stack, gates) + tuple(maps),
        [(shape, BF16)] * 3,
        aliases={3 + index: index for index in range(len(maps))},
    )


def owned(place, blocks):
    mine, theirs = blocks
    first = place[0] == 0
    return jnp.where(first, mine, theirs), jnp.where(first, theirs, mine)


def row_block(place, block):
    if isinstance(block, int):
        return block
    chips, core = block
    if core == "same":
        core = place[0]
    elif core == "other":
        core = 1 - place[0]
    return 2 * lax.bitwise_xor(place[1], chips) + core


def columns_of(place, block, width):
    return pl.ds(pl.multiple_of(row_block(place, block) * width, width), width)


def positions_of(owner, tokens):
    return pl.ds(pl.multiple_of(owner * tokens, tokens), tokens)


def load_piece(ref):
    return ref[...] if len(ref.shape) == 2 else ref[3]


def read_kernel(with_state, blocks, place, mine, theirs, own, stack, forth, low, *refs):
    count = len(blocks)
    pieces, refs = refs[:count], refs[count:]
    if with_state:
        (first, *refs) = refs
    (total, kept, given, last, read) = refs
    tokens, width = own.shape[1:]
    spans, heads = forth.shape[1:3]
    core = place[0]
    values = owned(place, (own[2], stack[2]))
    zero = jnp.zeros((DK, DK), F32)
    states = [first[head] if with_state else zero for head in range(heads)]
    for half in range(2):
        for span in range(spans):
            for head in range(heads):
                positions = slice(span * SPAN, (span + 1) * SPAN)
                columns = slice(head * DK, (head + 1) * DK)
                block = values[half][positions, columns]
                x_high, x_low = halves(states[head])
                wide = jnp.concatenate(
                    [
                        jnp.concatenate([x_high, x_low], 1),
                        jnp.concatenate([block, jnp.zeros_like(block)], 1),
                    ],
                    0,
                )
                both = dot(forth[half, span, head], wide)
                result = both[:, :DK] + both[:, DK:] + dot(low[half, span, head], wide[:, :DK])
                states[head] = result[:DK]
                read[half, positions, columns] = result[DK:].astype(BF16)
    for head in range(heads):
        last[head] = states[head]
    kept[...] = read[core]
    given[...] = read[1 - core]
    add_products(place, blocks, mine, theirs, pieces, total, None)


def paired(blocks):
    return not isinstance(blocks[0], int) and blocks[0][0] == blocks[1][0]


def add_products(place, blocks, mine, theirs, pieces, result, total):
    tokens = mine.shape[0]
    rows = mine.shape[1] // 8
    core = place[0]
    probe = [load_piece(piece) for piece in pieces]
    for source, owner in ((mine, core), (theirs, 1 - core)):
        positions = positions_of(owner, tokens)
        begin = 0
        part = None if total is None else total[positions, :]
        if paired(blocks):
            chip = lax.bitwise_xor(place[1], blocks[0][0])
            columns = pl.ds(pl.multiple_of(chip * 2 * rows, 2 * rows), 2 * rows)
            product = dot(source[:, columns], jnp.concatenate(owned(place, probe[:2]), 0))
            part = product if part is None else part + product
            begin = 2
        for block, piece in zip(blocks[begin:], probe[begin:]):
            product = dot(source[:, columns_of(place, block, rows)], piece)
            part = product if part is None else part + product
        result[positions, :] = part.astype(result.dtype)


def read_values(place, mine, theirs, own, stack, maps, blocks, pieces, entry):
    tokens, width = own.shape[1:]
    heads = width // DK
    extra = () if entry is None else (entry,)
    return kernel_call(
        functools.partial(read_kernel, entry is not None, tuple(blocks)),
        "read_values",
        place,
        (mine, theirs, own, stack, maps[0], maps[1], *pieces, *extra),
        [
            ((2 * tokens, width), F32),
            ((tokens, width), BF16),
            ((tokens, width), BF16),
            ((heads, DK, DK), F32),
        ],
        scratch=[pltpu.VMEM((2, tokens, width), BF16)],
    )


def recur_kernel(weighting, with_state, blocks, chips, lists, place, mine, theirs, total, forth, back, *refs):
    count = len(blocks)
    pieces, refs = refs[:count], refs[count:]
    if with_state:
        (first, final, *refs) = refs
    (grads, last, start, *refs) = refs
    shares, (sums, up) = refs[: len(lists)], refs[len(lists) :]
    tokens = mine.shape[0]
    spans, heads = forth.shape[1:3]
    add_products(place, blocks, mine, theirs, pieces, sums, total)
    zero = jnp.zeros((DK, DK), F32)
    states = [first[head] if with_state else zero for head in range(heads)]
    steps = [(half, span) for half in range(2) for span in range(spans)]
    for half, span in steps:
        begin = half * tokens + span * SPAN
        for head in range(heads):
            block = sums[begin : begin + SPAN, head * DK : (head + 1) * DK]
            fresh = dot(forth[half, span, head, :, DK:], block)
            result = dot(forth[half, span, head, :, :DK], states[head].astype(BF16)) + fresh
            states[head] = result[:DK]
            grad = (weighting * result[DK:]).astype(BF16)
            up[half, span, head] = dot(back[half, span, head, :, DK:], grad)
    for head in range(heads):
        last[head] = states[head]
    states = [final[head] if with_state else zero for head in range(heads)]
    for half, span in reversed(steps):
        begin = half * tokens + span * SPAN
        for head in range(heads):
            result = dot(back[half, span, head, :, :DK], states[head].astype(BF16))
            result = result + up[half, span, head]
            states[head] = result[:DK]
            grads[begin : begin + SPAN, head * DK : (head + 1) * DK] = result[DK:].astype(BF16)
    for head in range(heads):
        start[head] = states[head]
    if lists:
        put_products(place, chips, lists, mine, theirs, grads, shares)


def put_products(place, chips, lists, mine, theirs, grads, outs):
    tokens, width = mine.shape
    if chips is None:
        columns = pl.ds(0, width)
    else:
        columns = pl.ds(pl.multiple_of(lax.bitwise_xor(place[1], chips) * 4 * ROWS, 4 * ROWS), 4 * ROWS)
    core = place[0]
    part = dot_tn(mine[:, columns], grads[positions_of(core, tokens), :])
    part += dot_tn(theirs[:, columns], grads[positions_of(1 - core, tokens), :])
    for out, indices in zip(outs, lists):
        for slot, index in enumerate(indices):
            out[slot] = part[index * ROWS : (index + 1) * ROWS].astype(out.dtype)


def recur(weighting, place, mine, theirs, total, maps, blocks, pieces, chips, lists, states):
    tokens = mine.shape[0]
    width = total.shape[1]
    spans, heads = maps[0].shape[1:3]
    extra = () if states is None else states
    return kernel_call(
        functools.partial(
            recur_kernel, weighting, states is not None, tuple(blocks), chips, lists
        ),
        "recur",
        place,
        (mine, theirs, total, maps[0], maps[2], *pieces, *extra),
        [((2 * tokens, width), BF16), ((heads, DK, DK), F32), ((heads, DK, DK), F32)]
        + [((len(part), ROWS, width), BF16) for part in lists],
        scratch=[
            pltpu.VMEM((2 * tokens, width), BF16),
            pltpu.VMEM((2, spans, heads, 2 * DK, DK), F32),
        ],
    )


ROWS = 256


def curvature_kernel(jobs, place, mine, theirs, grads, *outs):
    begin = 0
    for chips, lists in jobs:
        put_products(place, chips, lists, mine, theirs, grads, outs[begin : begin + len(lists)])
        begin += len(lists)


def curvature(place, mine, theirs, grads, jobs, types):
    width = grads.shape[1]
    lengths = [len(part) for chips, lists in jobs for part in lists]
    return kernel_call(
        functools.partial(curvature_kernel, jobs),
        "curvature",
        place,
        (mine, theirs, grads),
        [((length, ROWS, width), kind) for length, kind in zip(lengths, types)],
    )


def join_kernel(place, *refs):
    core = place[0]
    count = len(refs) // 3
    for index in range(count):
        same, cross, whole = refs[2 * index], refs[2 * index + 1], refs[2 * count + index]
        width = same.shape[1]
        whole[:, positions_of(core, width)] = same[...]
        whole[:, positions_of(1 - core, width)] = cross[...]


def join(place, *pairs):
    return kernel_call(
        join_kernel,
        "join",
        place,
        [block for pair in pairs for block in pair],
        [((same.shape[0], 2 * same.shape[1]), same.dtype) for same, cross in pairs],
    )


def local(square, dp_size, ctx_size, queries, keys, values, decay, beta, inputs, probe):
    tokens = queries.shape[1]
    width = queries.shape[2] // 2
    weighting = math.sqrt(D) / (dp_size * ctx_size * tokens)
    ctx = lax.axis_index("ctx")
    chip = lax.axis_index("dp")
    core = lax.rem(ctx, 2)
    groups = ctx_size // 2
    partner = [(index, index ^ 1) for index in range(ctx_size)]
    mine = inputs[0]
    place = jnp.stack([core, chip])

    def swap(block):
        return lax.ppermute(block, "ctx", partner)

    def send(block, chips, cores):
        pairs = [
            (2 * index + which, 2 * (index ^ chips) + (which ^ cores))
            for index in range(dp_size)
            for which in range(2)
        ]
        return lax.ppermute(block, GROUP, pairs)

    def part(block, index):
        return lax.dynamic_slice_in_dim(block, index * width, width, 1)

    kept, given, own, stack, gates = pack(place, square, queries, keys, values, decay, beta, probe)
    gates, mine = lax.optimization_barrier((gates, mine))
    gates_t = swap(gates)
    if square:
        x_one = send(kept, 1, 0)
        y_one = send(given, 2, 1)
        stack = swap(stack)
        theirs = swap(mine)
        stack, kept, given = lax.optimization_barrier((stack, kept, given))
        x_two = send(given, 1, 1)
        y_two = send(kept, 2, 0)
        maps = prepare(place, 0, own, gates, ())
        x_one, y_one, *maps = lax.optimization_barrier((x_one, y_one, *maps))
        far_one = send(x_one, 2, 0)
        far_two = send(y_one, 1, 0)
        maps = prepare(place, 1, stack, gates_t, maps)
        pieces = [kept, stack, x_one, y_one, far_one, far_two, x_two, y_two]
        places = [
            (0, "same"),
            (0, "other"),
            (1, "same"),
            (2, "other"),
            (3, "same"),
            (3, "other"),
            (1, "other"),
            (2, "same"),
        ]
    else:
        stack = swap(stack)
        theirs = swap(mine)
        maps = prepare(place, 0, own, gates, ())
        maps = prepare(place, 1, stack, gates_t, maps)
        gathered = part(lax.all_gather(probe, GROUP, axis=0, tiled=True), core)
        places = list(range(8))
        rows = D // len(places)
        pieces = [gathered[index * rows : (index + 1) * rows] for index in places]
    def shift(block, by):
        pairs = [
            (index, index + 2 * by)
            for index in range(ctx_size)
            if 0 <= index + 2 * by < ctx_size
        ]
        return lax.ppermute(block, "ctx", pairs)

    entry = None
    if groups > 1:
        entry = jnp.zeros((width // DK, DK, DK), F32)
    read = functools.partial(
        read_values,
        place,
        mine,
        theirs,
        own,
        stack,
        maps,
        places[:4],
        pieces[:4],
    )
    for _ in range(groups - 1):
        entry = shift(read(entry)[3], 1)
    total, read_kept, read_given, unused = read(entry)
    read_swapped = swap(read_given)
    lists = ((0, 2), (1, 3)) if square else ()
    run = functools.partial(
        recur,
        weighting,
        place,
        mine,
        theirs,
        total,
        maps,
        places[4:],
        pieces[4:],
        3,
        lists,
    )
    states = None
    if groups > 1:
        states = (jnp.zeros((width // DK, DK, DK), F32),) * 2
        for _ in range(groups - 1):
            states = (shift(run(states)[1], 1), states[1])
        for _ in range(groups - 1):
            states = (states[0], shift(run(states)[2], -1))
    grads, unused, unused, *shares = run(states)
    build = functools.partial(curvature, place, mine, theirs, grads)
    if not square:
        everything = build(((None, (tuple(range(D // ROWS)),)),), [F32])[0]
        flat = everything.reshape(D, width)
        zero = jnp.zeros_like(flat)
        both = jnp.where(
            core == 0, jnp.concatenate([flat, zero], 1), jnp.concatenate([zero, flat], 1)
        )
        mixed = join(place, (read_kept, read_swapped))[0]
        return mixed[None], lax.psum_scatter(both, GROUP, scatter_dimension=0, tiled=True)

    far_x = send(shares[0], 1, 0)
    far_y = send(shares[1], 2, 0)
    upper, lower = (0, 2), (1, 3)
    near_x, keep_x, keep_y, near_y, own_top, own_low = build(
        ((1, (upper, lower)), (2, (upper, lower)), (0, (upper, lower))),
        [BF16, F32, F32, BF16, F32, F32],
    )
    near_x = send(near_x, 1, 0)
    near_y = send(near_y, 2, 0)
    far_x, far_y = lax.optimization_barrier((far_x, far_y))
    relay_y = send((keep_y + far_x.astype(F32)).astype(BF16), 2, 0)
    relay_x = send((keep_x + far_y.astype(F32)).astype(BF16), 1, 0)
    near_x, near_y, relay_x, relay_y = lax.optimization_barrier((near_x, near_y, relay_x, relay_y))
    top = own_top + near_x.astype(F32) + relay_y.astype(F32)
    low = own_low + near_y.astype(F32) + relay_x.astype(F32)
    sums = jnp.concatenate([top, low], 1)

    def at(block, index):
        return lax.dynamic_index_in_dim(block, index, 0, keepdims=False)

    near = at(sums, core)
    distant = swap(at(sums, 1 - core))
    mixed, result = join(place, (read_kept, read_swapped), (near, distant))
    return mixed[None], result


def solution(mesh):
    dp_size, ctx_size = mesh.shape["dp"], mesh.shape["ctx"]
    square = dp_size == 4 and ctx_size == 2
    return jax.shard_map(
        functools.partial(local, square, dp_size, ctx_size),
        mesh=mesh,
        in_specs=(
            P("dp", "ctx", "head"),
            P("dp", "ctx", "head"),
            P("dp", "ctx", "head"),
            P("dp", "head", "ctx"),
            P("dp", "head", "ctx"),
            P("dp", "ctx", None),
            P(("dp", "ctx"), "head"),
        ),
        out_specs=(P("dp", "ctx", "head"), P(("dp", "ctx"), "head")),
        check_vma=False,
    )
```

time: 356 us -> 62.3 us (0.17); the launches traced: 351 us -> 62.1 us
  matrix products: 175 us -> 0 us
  waiting for transfers between devices: 95.8 us -> 18.2 us
  local copies, waits for them, and re-layouts: 42.6 us -> 0.01 us
  Pallas kernels: 0 us -> 26.4 us
  starting transfers between devices: 0.08 us -> 15.7 us
  between operations: 14.9 us -> 0.72 us
  other arithmetic: 14.5 us -> 1.15 us
  blocking collectives: 6.5 us -> 0 us
    dot_general x104 -> x0, matrix products: 175 us -> none  [the longest x100 158 us: contract(): return jnp.einsum(form, left, right, precision=EXACT)]
    reduce_scatter x1 -> x0, waiting for transfers between devices: 68.7 us -> none  [local(): lax.psum_scatter(lax.dot_general(columns, grad_values, (((0,), (0,)), (()...]
    pallas_call x0 -> x7, Pallas kernels: none -> 26.4 us  [the longest x6 24.2 us: kernel_call(): pl.pallas_call(kernel, grid_spec=pltpu.PrefetchScalarGridSpec(num_scalar_...]
    all_gather x1 -> x0, waiting for transfers between devices: 26.4 us -> none  [local(): lax.all_gather(probe, ('dp', 'ctx'), axis=0, tiled=True)]
    ppermute x0 -> x17, waiting for transfers between devices: none -> 18.2 us  [the longest x12 16.4 us: send(): return lax.ppermute(block, GROUP, pairs)]
    ppermute x0 -> x17, starting transfers between devices: none -> 15.7 us  [the longest x12 13.8 us: send(): return lax.ppermute(block, GROUP, pairs)]
    unnamed x48 -> x2, local copies, waits for them, and re-layouts: 11.3 us -> 0.01 us
    dynamic_slice x32 -> x0, local copies, waits for them, and re-layouts: 10.9 us -> none  [the longest x24 6.08 us: local(): unused, produced_all = lax.scan(forward_step, entry_state, forward_items)]
  transfers between devices with their start and end apart: 2 -> 17, of which waited for: 2 -> 10; matrix products, arithmetic and copies ran while one was open for 5% -> 1% of each run, Pallas kernels for 0% -> 23%
where the time goes in v2:
time: 62.3 us; the launch traced here: 62.1 us
  Pallas kernels  26.4 us (42%)
  waiting for transfers between devices  18.2 us (29%)
  starting transfers between devices  15.7 us (25%)
  other arithmetic  1.15 us (2%)
  between operations  0.72 us (1%)
    pallas_call x6, Pallas kernels, kernel_call(): pl.pallas_call(kernel, grid_spec=pltpu.PrefetchScalarGridSpec(num_scalar_...  24.2 us
    ppermute x12, waiting for transfers between devices, send(): return lax.ppermute(block, GROUP, pairs)  16.4 us
    ppermute x12, starting transfers between devices, send(): return lax.ppermute(block, GROUP, pairs)  13.8 us
    pallas_call x1, Pallas kernels, pack(): pl.pallas_call(pack_kernel, grid_spec=pltpu.PrefetchScalarGridSpec(num_sc...  2.22 us
    ppermute x5, starting transfers between devices, swap(): return lax.ppermute(block, 'ctx', partner)  1.88 us
    ppermute x5, waiting for transfers between devices, swap(): return lax.ppermute(block, 'ctx', partner)  1.79 us
  transfers between devices with their start and end apart: 17, of which 10 were waited for; matrix products, arithmetic and copies ran while one was open for 1% of the time, Pallas kernels for 23%

profile of v2, /device:TPU:0, one launch (start us, length us, event | category | flops | bytes accessed | tf_op | source)
XLA Modules:
  0.0 62.1 jit_solution(3439732672294689039)
XLA Ops:
  0.7 2.2 %pack.1 = (bf16[512,256]{1,0:T(8,128)(2,1)S(1)}, bf16[512,256]{1,0:T(8,128)(2,1)S(1)}, bf16[3,512,256]{2,1,0:T(8,128)(2,1)S(1)}, bf16[4,512,256]{2,1,0:T(8,128)(2,1)S(1)}, f32[2,4,512]{2,1,0:T(4,128)S(1)}) custom-call(s32[2]{0:T(128)S(1)} %pad_add_fusion.place, bf16[1,512,512]{2,1,0:T(8,128)(2,1)} %queries.1, bf16[1,512,512]{2,1,0:T(8,128)(2,1)} %keys.1, ...), custom_call_target="tpu_custom_call" | custom-call | flops 11000000 | bytes 30000 | tf_op jit(solution)/shard_map/pack/pallas_call | solution.py:109
  3.5 2.9 %collective-permute-start.3 = (bf16[512,256]{1,0:T(8,128)(2,1)S(1)}, bf16[512,256]{1,0:T(8,128)(2,1)S(1)}, u32[]{:S(2)}, u32[]{:S(2)}) collective-permute-start(bf16[512,256]{1,0:T(8,128)(2,1)S(1)} %get-tuple-element.59.refs_0_), channel_id=1, source_target_pairs={{0,8},{4,12},{8,0},{12,4},{16,24},{20,28},{24,16},{28,20},{1,9},{5... | collective-permute-start | bytes 786440 | tf_op jit(solution)/shard_map/ppermute | solution.py:493
  6.5 0.9 %collective-permute-start.4 = (bf16[512,256]{1,0:T(8,128)(2,1)S(1)}, bf16[512,256]{1,0:T(8,128)(2,1)S(1)}, u32[]{:S(2)}, u32[]{:S(2)}) collective-permute-start(bf16[512,256]{1,0:T(8,128)(2,1)S(1)} %get-tuple-element.66), channel_id=1, source_target_pairs={{0,20},{4,16},{8,28},{12,24},{16,4},{20,0},{24,12},{28,8},{1,21},{... | collective-permute-start | bytes 786440 | tf_op jit(solution)/shard_map/ppermute | solution.py:493
  8.1 4.1 %prepare.2 = (bf16[2,4,2,256,256]{4,3,2,1,0:T(8,128)(2,1)S(1)}, bf16[2,4,2,256,256]{4,3,2,1,0:T(8,128)(2,1)S(1)}, bf16[2,4,2,256,256]{4,3,2,1,0:T(8,128)(2,1)S(1)}) custom-call(s32[2]{0:T(128)S(1)} %pad_add_fusion.place, bf16[3,512,256]{2,1,0:T(8,128)(2,1)S(1)} %get-tuple-element.45.stack.own, f32[2,4,512]{2,1,0:T(4,128)S(1)} %get-tuple-element.50.gates), custom_call_target="tpu_custom_call" | custom-call | flops 11000000 | bytes 30000 | tf_op jit(solution)/shard_map/prepare/pallas_call | solution.py:35
  12.2 0.8 %collective-permute-done.3.refs_2_ = bf16[512,256]{1,0:T(8,128)(2,1)S(1)} collective-permute-done((bf16[512,256]{1,0:T(8,128)(2,1)S(1)}, bf16[512,256]{1,0:T(8,128)(2,1)S(1)}, u32[]{:S(2)}, u32[]{:S(2)}) %collective-permute-start.3) | collective-permute-done | bytes 262176 | tf_op jit(solution)/shard_map/ppermute | solution.py:493
  13.0 2.0 %collective-permute-done.4.refs_3_ = bf16[512,256]{1,0:T(8,128)(2,1)S(1)} collective-permute-done((bf16[512,256]{1,0:T(8,128)(2,1)S(1)}, bf16[512,256]{1,0:T(8,128)(2,1)S(1)}, u32[]{:S(2)}, u32[]{:S(2)}) %collective-permute-start.4) | collective-permute-done | bytes 262176 | tf_op jit(solution)/shard_map/ppermute | solution.py:493
  15.0 1.6 %collective-permute-start.6 = (bf16[512,256]{1,0:T(8,128)(2,1)S(1)}, bf16[512,256]{1,0:T(8,128)(2,1)S(1)}, u32[]{:S(2)}, u32[]{:S(2)}) collective-permute-start(bf16[512,256]{1,0:T(8,128)(2,1)S(1)} %collective-permute-done.3.refs_2_), channel_id=1, source_target_pairs={{0,16},{4,20},{8,24},{12,28},{16,0},{20,4},{24,8},{28,12},{1,17},{... | collective-permute-start | bytes 786440 | tf_op jit(solution)/shard_map/ppermute | solution.py:493
  17.1 0.8 %collective-permute-start.8 = (bf16[512,256]{1,0:T(8,128)(2,1)S(1)}, bf16[512,256]{1,0:T(8,128)(2,1)S(1)}, u32[]{:S(2)}, u32[]{:S(2)}) collective-permute-start(bf16[512,256]{1,0:T(8,128)(2,1)S(1)} %get-tuple-element.66), channel_id=1, source_target_pairs={{0,12},{4,8},{8,4},{12,0},{16,28},{20,24},{24,20},{28,16},{1,13},{... | collective-permute-start | bytes 786440 | tf_op jit(solution)/shard_map/ppermute | solution.py:493
  17.9 4.1 %prepare.3 = (bf16[2,4,2,256,256]{4,3,2,1,0:T(8,128)(2,1)S(1)}, bf16[2,4,2,256,256]{4,3,2,1,0:T(8,128)(2,1)S(1)}, bf16[2,4,2,256,256]{4,3,2,1,0:T(8,128)(2,1)S(1)}) custom-call(s32[2]{0:T(128)S(1)} %pad_add_fusion.place, bf16[4,512,256]{2,1,0:T(8,128)(2,1)S(1)} %collective-permute-done.1.stack.refs_1_, ...), custom_call_target="tpu_custom_call", output_to_operand_aliasing={{0}: (3, {}), {1}: (4, {}), {2}: (5, {})} | custom-call | flops 11000000 | bytes 30000 | tf_op jit(solution)/shard_map/prepare/pallas_call | solution.py:35
  22.1 3.7 %read_values.1 = (f32[1024,256]{1,0:T(8,128)S(1)}, bf16[512,256]{1,0:T(8,128)(2,1)S(1)}, bf16[512,256]{1,0:T(8,128)(2,1)S(1)}, f32[2,128,128]{2,1,0:T(8,128)}) custom-call(s32[2]{0:T(128)S(1)} %pad_add_fusion.place, bf16[512,4096]{1,0:T(8,128)(2,1)S(1)} %bitcast.9, bf16[512,4096]{1,0:T(8,128)(2,1)S(1)} %collective-permute-done.theirs, ...), custom_call_target="tpu_custom_call" | custom-call | flops 11000000 | bytes 30000 | tf_op jit(solution)/shard_map/read_values/pallas_call | solution.py:35
  25.8 3.2 %collective-permute-done.9.refs_3_ = bf16[512,256]{1,0:T(8,128)(2,1)S(1)} collective-permute-done((bf16[512,256]{1,0:T(8,128)(2,1)S(1)}, bf16[512,256]{1,0:T(8,128)(2,1)S(1)}, u32[]{:S(2)}, u32[]{:S(2)}) %collective-permute-start.9) | collective-permute-done | bytes 262176 | tf_op jit(solution)/shard_map/ppermute | solution.py:493
  29.0 8.0 %recur.1 = (bf16[1024,256]{1,0:T(8,128)(2,1)S(1)}, f32[2,128,128]{2,1,0:T(8,128)}, f32[2,128,128]{2,1,0:T(8,128)}, bf16[2,256,256]{2,1,0:T(8,128)(2,1)S(1)}, bf16[2,256,256]{2,1,0:T(8,128)(2,1)S(1)}) custom-call(s32[2]{0:T(128)S(1)} %pad_add_fusion.place, bf16[512,4096]{1,0:T(8,128)(2,1)S(1)} %bitcast.10, bf16[512,4096]{1,0:T(8,128)(2,1)S(1)} %collective-permute-done.theirs, ...), custom_call_target="tpu_custom_call" | custom-call | flops 11000000 | bytes 30000 | tf_op jit(solution)/shard_map/recur/pallas_call | solution.py:35
  37.0 0.7 %collective-permute-start.12 = (bf16[2,256,256]{2,1,0:T(8,128)(2,1)S(1)}, bf16[2,256,256]{2,1,0:T(8,128)(2,1)S(1)}, u32[]{:S(2)}, u32[]{:S(2)}) collective-permute-start(bf16[2,256,256]{2,1,0:T(8,128)(2,1)S(1)} %get-tuple-element.72), channel_id=1, source_target_pairs={{0,8},{4,12},{8,0},{12,4},{16,24},{20,28},{24,16},{28,20},{1,9},{5... | collective-permute-start | bytes 786440 | tf_op jit(solution)/shard_map/ppermute | solution.py:493
  37.7 1.3 %collective-permute-start.13 = (bf16[2,256,256]{2,1,0:T(8,128)(2,1)S(1)}, bf16[2,256,256]{2,1,0:T(8,128)(2,1)S(1)}, u32[]{:S(2)}, u32[]{:S(2)}) collective-permute-start(bf16[2,256,256]{2,1,0:T(8,128)(2,1)S(1)} %get-tuple-element.73), channel_id=1, source_target_pairs={{0,16},{4,20},{8,24},{12,28},{16,0},{20,4},{24,8},{28,12},{1,17},{... | collective-permute-start | bytes 786440 | tf_op jit(solution)/shard_map/ppermute | solution.py:493
  39.0 2.5 %curvature.1 = (bf16[2,256,256]{2,1,0:T(8,128)(2,1)S(1)}, f32[2,256,256]{2,1,0:T(8,128)S(1)}, f32[2,256,256]{2,1,0:T(8,128)S(1)}, bf16[2,256,256]{2,1,0:T(8,128)...) custom-call(s32[2]{0:T(128)S(1)} %pad_add_fusion.place, bf16[512,4096]{1,0:T(8,128)(2,1)S(1)} %bitcast.11, ...), custom_call_target="tpu_custom_call" | custom-call | flops 11000000 | bytes 30000 | tf_op jit(solution)/shard_map/curvature/pallas_call | solution.py:35
  41.5 1.5 %collective-permute-start.10 = (bf16[2,256,256]{2,1,0:T(8,128)(2,1)S(1)}, bf16[2,256,256]{2,1,0:T(8,128)(2,1)S(1)}, u32[]{:S(2)}, u32[]{:S(2)}) collective-permute-start(bf16[2,256,256]{2,1,0:T(8,128)(2,1)S(1)} %get-tuple-element.69), channel_id=1, source_target_pairs={{0,8},{4,12},{8,0},{12,4},{16,24},{20,28},{24,16},{28,20},{1,9},{5... | collective-permute-start | bytes 786440 | tf_op jit(solution)/shard_map/ppermute | solution.py:493
  43.6 2.5 %collective-permute-done.12 = bf16[2,256,256]{2,1,0:T(8,128)(2,1)S(1)} collective-permute-done((bf16[2,256,256]{2,1,0:T(8,128)(2,1)S(1)}, bf16[2,256,256]{2,1,0:T(8,128)(2,1)S(1)}, u32[]{:S(2)}, u32[]{:S(2)}) %collective-permute-start.12) | collective-permute-done | bytes 262176 | tf_op jit(solution)/shard_map/ppermute | solution.py:493
  46.9 0.9 %collective-permute-start.15 = (bf16[2,256,256]{2,1,0:T(8,128)(2,1)S(1)}, bf16[2,256,256]{2,1,0:T(8,128)(2,1)S(1)}, u32[]{:S(2)}, u32[]{:S(2)}) collective-permute-start(bf16[2,256,256]{2,1,0:T(8,128)(2,1)S(1)} %add_convert_fusion), channel_id=1, source_target_pairs={{0,16},{4,20},{8,24},{12,28},{16,0},{20,4},{24,8},{28,12},{1,17},{... | collective-permute-start | bytes 786440 | tf_op jit(solution)/shard_map/ppermute | solution.py:493
  47.8 0.8 %add_convert_fusion.1 = bf16[2,256,256]{2,1,0:T(8,128)(2,1)} fusion(f32[2,256,256]{2,1,0:T(8,128)S(1)} %get-tuple-element.71, bf16[2,256,256]{2,1,0:T(8,128)(2,1)S(1)} %collective-permute-done.13), kind=kLoop, calls=%fused_computation.11 | loop fusion | flops 393216 | bytes 1048576 | tf_op jit(solution)/shard_map/convert_element_type | solution.py:604
  48.6 2.0 %collective-permute-start.14 = (bf16[2,256,256]{2,1,0:T(8,128)(2,1)}, bf16[2,256,256]{2,1,0:T(8,128)(2,1)S(1)}, u32[]{:S(2)}, u32[]{:S(2)}) collective-permute-start(bf16[2,256,256]{2,1,0:T(8,128)(2,1)} %add_convert_fusion.1), channel_id=1, source_target_pairs={{0,8},{4,12},{8,0},{12,4},{16,24},{20,28},{24,16},{28,20},{1,9},{5... | collective-permute-start | bytes 786440 | tf_op jit(solution)/shard_map/ppermute | solution.py:493
  50.6 1.2 %collective-permute-done.10 = bf16[2,256,256]{2,1,0:T(8,128)(2,1)S(1)} collective-permute-done((bf16[2,256,256]{2,1,0:T(8,128)(2,1)S(1)}, bf16[2,256,256]{2,1,0:T(8,128)(2,1)S(1)}, u32[]{:S(2)}, u32[]{:S(2)}) %collective-permute-start.10) | collective-permute-done | bytes 262176 | tf_op jit(solution)/shard_map/ppermute | solution.py:493
  52.5 5.3 %collective-permute-done.15 = bf16[2,256,256]{2,1,0:T(8,128)(2,1)S(1)} collective-permute-done((bf16[2,256,256]{2,1,0:T(8,128)(2,1)S(1)}, bf16[2,256,256]{2,1,0:T(8,128)(2,1)S(1)}, u32[]{:S(2)}, u32[]{:S(2)}) %collective-permute-start.15) | collective-permute-done | bytes 262176 | tf_op jit(solution)/shard_map/ppermute | solution.py:493
  58.6 1.8 %collective-permute-done.5.refs_1_ = bf16[512,256]{1,0:T(8,128)(2,1)S(1)} collective-permute-done((bf16[512,256]{1,0:T(8,128)(2,1)S(1)}, bf16[512,256]{1,0:T(8,128)(2,1)S(1)}, u32[]{:S(2)}, u32[]{:S(2)}) %collective-permute-start.5) | collective-permute-done | bytes 262176 | tf_op jit(solution)/shard_map/ppermute | solution.py:485
  60.3 1.8 %join.1 = (bf16[512,512]{1,0:T(8,128)(2,1)}, f32[512,512]{1,0:T(8,128)}) custom-call(s32[2]{0:T(128)S(1)} %pad_add_fusion.place, bf16[512,256]{1,0:T(8,128)(2,1)S(1)} %get-tuple-element.62.refs_0_, bf16[512,256]{1,0:T(8,128)(2,1)S(1)} %collective-permute-done.5.refs_1_, f32[512,256]{1,0:T(8,128)S(1)} %get-tuple-element.85.refs_2_, ...), custom_call_target="tpu_custom_call" | custom-call | flops 11000000 | bytes 30000 | tf_op jit(solution)/shard_map/join/pallas_call | solution.py:35
  (24 shorter events, 4.8 us)
Async XLA Ops:
  2.9 19.1 %collective-permute-start = (bf16[512,4096]{1,0:T(8,128)(2,1)}, bf16[512,4096]{1,0:T(8,128)(2,1)S(1)}, u32[]{:S(2)}, u32[]{:S(2)}) collective-permute-start(bf16[512,4096]{1,0:T(8,128)(2,1)} %bitcast.8), channel_id=1, source_target_pairs={{0,4},{4,0},{1,5},{5,1},{2,6},{6,2},{3,7},{7,3},{8,12},{12,8},{9,1... | collective-permute-start | bytes 12582920 | tf_op jit(solution)/shard_map/ppermute | solution.py:485
  3.5 13.6 %collective-permute-start.1 = (bf16[4,512,256]{2,1,0:T(8,128)(2,1)S(1)}, bf16[4,512,256]{2,1,0:T(8,128)(2,1)S(1)}, u32[]{:S(2)}, u32[]{:S(2)}) collective-permute-start(bf16[4,512,256]{2,1,0:T(8,128)(2,1)S(1)} %get-tuple-element.46), channel_id=1, source_target_pairs={{0,4},{4,0},{1,5},{5,1},{2,6},{6,2},{3,7},{7,3},{8,12},{12,8},{9,1... | collective-permute-start | bytes 3145736 | tf_op jit(solution)/shard_map/ppermute | solution.py:485
  3.5 9.5 %collective-permute-start.3 = (bf16[512,256]{1,0:T(8,128)(2,1)S(1)}, bf16[512,256]{1,0:T(8,128)(2,1)S(1)}, u32[]{:S(2)}, u32[]{:S(2)}) collective-permute-start(bf16[512,256]{1,0:T(8,128)(2,1)S(1)} %get-tuple-element.59.refs_0_), channel_id=1, source_target_pairs={{0,8},{4,12},{8,0},{12,4},{16,24},{20,28},{24,16},{28,20},{1,9},{5... | collective-permute-start | bytes 786440 | tf_op jit(solution)/shard_map/ppermute | solution.py:493
  6.5 8.5 %collective-permute-start.4 = (bf16[512,256]{1,0:T(8,128)(2,1)S(1)}, bf16[512,256]{1,0:T(8,128)(2,1)S(1)}, u32[]{:S(2)}, u32[]{:S(2)}) collective-permute-start(bf16[512,256]{1,0:T(8,128)(2,1)S(1)} %get-tuple-element.66), channel_id=1, source_target_pairs={{0,20},{4,16},{8,28},{12,24},{16,4},{20,0},{24,12},{28,8},{1,21},{... | collective-permute-start | bytes 786440 | tf_op jit(solution)/shard_map/ppermute | solution.py:493
  7.4 9.7 %collective-permute-start.2 = (f32[2,4,512]{2,1,0:T(4,128)S(1)}, f32[2,4,512]{2,1,0:T(4,128)S(1)}, u32[]{:S(2)}, u32[]{:S(2)}) collective-permute-start(f32[2,4,512]{2,1,0:T(4,128)S(1)} %get-tuple-element.50.gates), channel_id=1, source_target_pairs={{0,4},{4,0},{1,5},{5,1},{2,6},{6,2},{3,7},{7,3},{8,12},{12,8},{9,1... | collective-permute-start | bytes 49160 | tf_op jit(solution)/shard_map/ppermute | solution.py:485
  15.0 7.1 %copy-start = (bf16[1,512,4096]{2,1,0:T(8,128)(2,1)S(1)}, bf16[1,512,4096]{2,1,0:T(8,128)(2,1)}, u32[]{:S(2)}) copy-start(bf16[1,512,4096]{2,1,0:T(8,128)(2,1)} %param.12) | copy-start | bytes 12582916
  15.0 10.8 %collective-permute-start.6 = (bf16[512,256]{1,0:T(8,128)(2,1)S(1)}, bf16[512,256]{1,0:T(8,128)(2,1)S(1)}, u32[]{:S(2)}, u32[]{:S(2)}) collective-permute-start(bf16[512,256]{1,0:T(8,128)(2,1)S(1)} %collective-permute-done.3.refs_2_), channel_id=1, source_target_pairs={{0,16},{4,20},{8,24},{12,28},{16,0},{20,4},{24,8},{28,12},{1,17},{... | collective-permute-start | bytes 786440 | tf_op jit(solution)/shard_map/ppermute | solution.py:493
  16.6 9.2 %collective-permute-start.7 = (bf16[512,256]{1,0:T(8,128)(2,1)S(1)}, bf16[512,256]{1,0:T(8,128)(2,1)S(1)}, u32[]{:S(2)}, u32[]{:S(2)}) collective-permute-start(bf16[512,256]{1,0:T(8,128)(2,1)S(1)} %collective-permute-done.4.refs_3_), channel_id=1, source_target_pairs={{0,8},{4,12},{8,0},{12,4},{16,24},{20,28},{24,16},{28,20},{1,9},{5... | collective-permute-start | bytes 786440 | tf_op jit(solution)/shard_map/ppermute | solution.py:493
  17.1 11.8 %collective-permute-start.9 = (bf16[512,256]{1,0:T(8,128)(2,1)S(1)}, bf16[512,256]{1,0:T(8,128)(2,1)S(1)}, u32[]{:S(2)}, u32[]{:S(2)}) collective-permute-start(bf16[512,256]{1,0:T(8,128)(2,1)S(1)} %get-tuple-element.59.refs_0_), channel_id=1, source_target_pairs={{0,16},{4,20},{8,24},{12,28},{16,0},{20,4},{24,8},{28,12},{1,17},{... | collective-permute-start | bytes 786440 | tf_op jit(solution)/shard_map/ppermute | solution.py:493
  17.1 11.9 %collective-permute-start.8 = (bf16[512,256]{1,0:T(8,128)(2,1)S(1)}, bf16[512,256]{1,0:T(8,128)(2,1)S(1)}, u32[]{:S(2)}, u32[]{:S(2)}) collective-permute-start(bf16[512,256]{1,0:T(8,128)(2,1)S(1)} %get-tuple-element.66), channel_id=1, source_target_pairs={{0,12},{4,8},{8,4},{12,0},{16,28},{20,24},{24,20},{28,16},{1,13},{... | collective-permute-start | bytes 786440 | tf_op jit(solution)/shard_map/ppermute | solution.py:493
  37.0 9.1 %collective-permute-start.12 = (bf16[2,256,256]{2,1,0:T(8,128)(2,1)S(1)}, bf16[2,256,256]{2,1,0:T(8,128)(2,1)S(1)}, u32[]{:S(2)}, u32[]{:S(2)}) collective-permute-start(bf16[2,256,256]{2,1,0:T(8,128)(2,1)S(1)} %get-tuple-element.72), channel_id=1, source_target_pairs={{0,8},{4,12},{8,0},{12,4},{16,24},{20,28},{24,16},{28,20},{1,9},{5... | collective-permute-start | bytes 786440 | tf_op jit(solution)/shard_map/ppermute | solution.py:493
  37.7 9.1 %collective-permute-start.13 = (bf16[2,256,256]{2,1,0:T(8,128)(2,1)S(1)}, bf16[2,256,256]{2,1,0:T(8,128)(2,1)S(1)}, u32[]{:S(2)}, u32[]{:S(2)}) collective-permute-start(bf16[2,256,256]{2,1,0:T(8,128)(2,1)S(1)} %get-tuple-element.73), channel_id=1, source_target_pairs={{0,16},{4,20},{8,24},{12,28},{16,0},{20,4},{24,8},{28,12},{1,17},{... | collective-permute-start | bytes 786440 | tf_op jit(solution)/shard_map/ppermute | solution.py:493
  41.5 10.3 %collective-permute-start.10 = (bf16[2,256,256]{2,1,0:T(8,128)(2,1)S(1)}, bf16[2,256,256]{2,1,0:T(8,128)(2,1)S(1)}, u32[]{:S(2)}, u32[]{:S(2)}) collective-permute-start(bf16[2,256,256]{2,1,0:T(8,128)(2,1)S(1)} %get-tuple-element.69), channel_id=1, source_target_pairs={{0,8},{4,12},{8,0},{12,4},{16,24},{20,28},{24,16},{28,20},{1,9},{5... | collective-permute-start | bytes 786440 | tf_op jit(solution)/shard_map/ppermute | solution.py:493
  43.0 9.4 %collective-permute-start.11 = (bf16[2,256,256]{2,1,0:T(8,128)(2,1)S(1)}, bf16[2,256,256]{2,1,0:T(8,128)(2,1)S(1)}, u32[]{:S(2)}, u32[]{:S(2)}) collective-permute-start(bf16[2,256,256]{2,1,0:T(8,128)(2,1)S(1)} %get-tuple-element.70), channel_id=1, source_target_pairs={{0,16},{4,20},{8,24},{12,28},{16,0},{20,4},{24,8},{28,12},{1,17},{... | collective-permute-start | bytes 786440 | tf_op jit(solution)/shard_map/ppermute | solution.py:493
  46.9 10.8 %collective-permute-start.15 = (bf16[2,256,256]{2,1,0:T(8,128)(2,1)S(1)}, bf16[2,256,256]{2,1,0:T(8,128)(2,1)S(1)}, u32[]{:S(2)}, u32[]{:S(2)}) collective-permute-start(bf16[2,256,256]{2,1,0:T(8,128)(2,1)S(1)} %add_convert_fusion), channel_id=1, source_target_pairs={{0,16},{4,20},{8,24},{12,28},{16,0},{20,4},{24,8},{28,12},{1,17},{... | collective-permute-start | bytes 786440 | tf_op jit(solution)/shard_map/ppermute | solution.py:493
  48.6 9.2 %collective-permute-start.14 = (bf16[2,256,256]{2,1,0:T(8,128)(2,1)}, bf16[2,256,256]{2,1,0:T(8,128)(2,1)S(1)}, u32[]{:S(2)}, u32[]{:S(2)}) collective-permute-start(bf16[2,256,256]{2,1,0:T(8,128)(2,1)} %add_convert_fusion.1), channel_id=1, source_target_pairs={{0,8},{4,12},{8,0},{12,4},{16,24},{20,28},{24,16},{28,20},{1,9},{5... | collective-permute-start | bytes 786440 | tf_op jit(solution)/shard_map/ppermute | solution.py:493
  58.0 2.4 %collective-permute-start.16 = (f32[512,256]{1,0:T(8,128)S(1)}, f32[512,256]{1,0:T(8,128)S(1)}, u32[]{:S(2)}, u32[]{:S(2)}) collective-permute-start(f32[512,256]{1,0:T(8,128)S(1)} %get-tuple-element.84), channel_id=1, source_target_pairs={{0,4},{4,0},{1,5},{5,1},{2,6},{6,2},{3,7},{7,3},{8,12},{12,8},{9,1... | collective-permute-start | bytes 1572872 | tf_op jit(solution)/shard_map/ppermute | solution.py:485
  58.1 2.3 %collective-permute-start.5 = (bf16[512,256]{1,0:T(8,128)(2,1)S(1)}, bf16[512,256]{1,0:T(8,128)(2,1)S(1)}, u32[]{:S(2)}, u32[]{:S(2)}) collective-permute-start(bf16[512,256]{1,0:T(8,128)(2,1)S(1)} %get-tuple-element.63), channel_id=1, source_target_pairs={{0,4},{4,0},{1,5},{5,1},{2,6},{6,2},{3,7},{7,3},{8,12},{12,8},{9,1... | collective-permute-start | bytes 786440 | tf_op jit(solution)/shard_map/ppermute | solution.py:485

commit v3 on v2

--- a/solution.py
+++ b/solution.py
@@ -57,10 +57,6 @@
     return lax.dot_general(left, right, (((1,), (1,)), ((), ())), preferred_element_type=F32)
 
 
-def dot_tn(left, right):
-    return lax.dot_general(left, right, (((0,), (0,)), ((), ())), preferred_element_type=F32)
-
-
 def halves(block):
     high = block.astype(BF16)
     return high, (block - high.astype(F32)).astype(BF16)
@@ -80,24 +76,68 @@
     return (block * lax.rsqrt(jnp.sum(block * block, -1, keepdims=True) + EPSILON)).astype(BF16)
 
 
+GATE_ROWS = 32
+
+
+def terms_of(block):
+    terms = []
+    for _ in range(3):
+        term = block.astype(BF16)
+        terms.append(term.astype(F32))
+        block = block - terms[-1]
+    return terms
+
+
 def pack_kernel(place, queries, keys, values, decay, beta, probe, kept, given, own, stack, gates, sems):
     core = place[0]
-    width = kept.shape[1]
+    tokens, width = own.shape[1:]
     same = pl.ds(pl.multiple_of(core * width, width), width)
     cross = pl.ds(pl.multiple_of((1 - core) * width, width), width)
-    moves = [(probe.at[:, same], kept), (probe.at[:, cross], given)]
-    moves += [(block.at[0, :, cross], stack.at[i]) for i, block in enumerate((queries, keys, values))]
+    slots = [pl.ds(i * tokens, tokens) for i in range(4)]
+    moves = [(decay.at[0], gates.at[0]), (beta.at[0], gates.at[1])]
+    moves += [(probe.at[:, same], kept), (probe.at[:, cross], given)]
+    moves += [
+        (block.at[0, :, cross], stack.at[slots[i], :]) for i, block in enumerate((queries, keys, values))
+    ]
+    if stack.shape[0] > 4 * tokens:
+        moves.append((probe.at[:, cross], stack.at[slots[3], :]))
     moves += [(block.at[0, :, same], own.at[i]) for i, block in enumerate((queries, keys, values))]
-    if stack.shape[0] > 3:
-        moves.append((probe.at[:, cross], stack.at[3]))
-    moves += [(decay.at[0], gates.at[0]), (beta.at[0], gates.at[1])]
     copies = [
         pltpu.make_async_copy(source, target, sems.at[i]) for i, (source, target) in enumerate(moves)
     ]
     for copy in copies:
         copy.start()
-    for copy in copies:
+    copies[0].wait()
+    copies[1].wait()
+    heads = gates.shape[1] // 2
+    rows = []
+    for kind in range(2):
+        block = jnp.where(core == 0, gates[kind, heads:], gates[kind, :heads])
+        for term in terms_of(block):
+            rows += [term[:, begin : begin + width] for begin in range(0, tokens, width)]
+    used = sum(row.shape[0] for row in rows)
+    rows.append(jnp.zeros((GATE_ROWS - used, width), F32))
+    stack[stack.shape[0] - GATE_ROWS :, :] = jnp.concatenate(rows, 0).astype(BF16)
+    for copy in copies[2:]:
         copy.wait()
+
+
+def received_gates(stack, tokens, heads):
+    width = stack.shape[1]
+    block = stack[stack.shape[0] - GATE_ROWS :, :].astype(F32)
+    cuts = tokens // width
+    out = []
+    for kind in range(2):
+        terms = []
+        for term in range(3):
+            begin = (kind * 3 + term) * cuts * heads
+            terms.append(
+                jnp.concatenate(
+                    [block[begin + cut * heads : begin + (cut + 1) * heads] for cut in range(cuts)], 1
+                )
+            )
+        out.append(terms[0] + terms[1] + terms[2])
+    return out
 
 
 def pack(place, with_probe, queries, keys, values, decay, beta, probe):
@@ -119,7 +159,7 @@
             half,
             half,
             jax.ShapeDtypeStruct((3, tokens, width), BF16),
-            jax.ShapeDtypeStruct((4 if with_probe else 3, tokens, width), BF16),
+            jax.ShapeDtypeStruct(((4 if with_probe else 3) * tokens + GATE_ROWS, width), BF16),
             jax.ShapeDtypeStruct((2,) + decay.shape[1:], F32),
         ],
         compiler_params=pltpu.CompilerParams(vmem_limit_bytes=VMEM_BYTES),
@@ -128,12 +168,15 @@
     )(place, *(in_hbm(block) for block in (queries, keys, values, decay, beta, probe)))
 
 
-def prepare_kernel(side, place, stack, gates, *refs):
-    forth, forth_low, back = refs[-3:]
+def prepare_kernel(side, tokens, place, stack, *refs):
+    forth, back, back_low = refs[-3:]
     core = place[0]
     owner = core if side == 0 else 1 - core
-    queries, keys = stack[0], stack[1]
-    tokens, width = queries.shape
+    if side == 0:
+        queries, keys = stack[0], stack[1]
+    else:
+        queries, keys = stack[:tokens], stack[tokens : 2 * tokens]
+    width = queries.shape[1]
     spans, heads = tokens // SPAN, width // DK
     rows = lax.broadcasted_iota(jnp.int32, (SPAN, SPAN), 0)
     cols = lax.broadcasted_iota(jnp.int32, (SPAN, SPAN), 1)
@@ -142,8 +185,6 @@
     diagonal = rows == cols
     items = [(span, head) for span in range(spans) for head in range(heads)]
 
-    def gate(index):
-        return jnp.where(core == 0, gates[index, :heads], gates[index, heads:])
 
     def cut(block, item):
         span, head = item
@@ -166,8 +207,14 @@
             & ((cols // size) % 2 == 0)
         )
 
-    decay_log = jnp.log(gate(0))
-    strengths = gate(1)
+    if side == 0:
+        gates = refs[0]
+        decays, strengths = [
+            jnp.where(core == 0, gates[kind, :heads], gates[kind, heads:]) for kind in range(2)
+        ]
+    else:
+        decays, strengths = received_gates(stack, tokens, heads)
+    decay_log = jnp.log(decays)
     identity = jnp.where(diagonal, 1.0, 0.0)
 
     def build(items):
@@ -218,10 +265,10 @@
             span, head = item
             kept = jnp.where(diagonal, g[SPAN - 1 :], 0.0)
             whole = jnp.concatenate([jnp.concatenate([kept, gq], 0) - rem, up], 1)
-            high, low = halves(whole)
-            forth[owner, span, head] = high
-            forth_low[owner, span, head] = low
-            back[owner, span, head] = whole.T.astype(BF16)
+            high, low = halves(whole.T)
+            forth[owner, span, head] = whole.astype(BF16)
+            back[owner, span, head] = high
+            back_low[owner, span, head] = low
 
     for start in range(0, len(items), BATCH):
         build(items[start : start + BATCH])
@@ -230,17 +277,16 @@
 BATCH = 8
 
 
-def prepare(place, side, stack, gates, maps):
-    tokens = stack.shape[1]
-    heads = gates.shape[1] // 2
+def prepare(place, side, tokens, width, stack, others):
+    heads = width // DK
     shape = (2, tokens // SPAN, heads, 2 * DK, 2 * DK)
     return kernel_call(
-        functools.partial(prepare_kernel, side),
+        functools.partial(prepare_kernel, side, tokens),
         "prepare",
         place,
-        (stack, gates) + tuple(maps),
+        (stack,) + tuple(others),
         [(shape, BF16)] * 3,
-        aliases={3 + index: index for index in range(len(maps))},
+        aliases={2 + index: index for index in range(3)} if side else {},
     )
 
 
@@ -269,20 +315,20 @@
     return pl.ds(pl.multiple_of(owner * tokens, tokens), tokens)
 
 
-def load_piece(ref):
-    return ref[...] if len(ref.shape) == 2 else ref[3]
-
-
-def read_kernel(with_state, blocks, place, mine, theirs, own, stack, forth, low, *refs):
+def load_piece(ref, rows):
+    return ref[:rows] if ref.shape[0] < 3 * rows else ref[3 * rows : 4 * rows]
+
+
+def read_kernel(with_state, blocks, place, mine, theirs, own, stack, back, low, *refs):
     count = len(blocks)
     pieces, refs = refs[:count], refs[count:]
     if with_state:
         (first, *refs) = refs
     (total, kept, given, last, read) = refs
     tokens, width = own.shape[1:]
-    spans, heads = forth.shape[1:3]
-    core = place[0]
-    values = owned(place, (own[2], stack[2]))
+    spans, heads = back.shape[1:3]
+    core = place[0]
+    values = owned(place, (own[2], stack[2 * tokens : 3 * tokens]))
     zero = jnp.zeros((DK, DK), F32)
     states = [first[head] if with_state else zero for head in range(heads)]
     for half in range(2):
@@ -290,19 +336,14 @@
             for head in range(heads):
                 positions = slice(span * SPAN, (span + 1) * SPAN)
                 columns = slice(head * DK, (head + 1) * DK)
-                block = values[half][positions, columns]
+                block = values[half][positions, columns].T
                 x_high, x_low = halves(states[head])
-                wide = jnp.concatenate(
-                    [
-                        jnp.concatenate([x_high, x_low], 1),
-                        jnp.concatenate([block, jnp.zeros_like(block)], 1),
-                    ],
-                    0,
-                )
-                both = dot(forth[half, span, head], wide)
-                result = both[:, :DK] + both[:, DK:] + dot(low[half, span, head], wide[:, :DK])
-                states[head] = result[:DK]
-                read[half, positions, columns] = result[DK:].astype(BF16)
+                left = jnp.concatenate([x_high, block], 1)
+                rest = jnp.concatenate([x_low, jnp.zeros_like(block)], 1)
+                both = dot(jnp.concatenate([left, rest], 0), back[half, span, head])
+                result = both[:DK] + both[DK:] + dot(left, low[half, span, head])
+                states[head] = result[:, :DK]
+                read[half, positions, columns] = result[:, DK:].T.astype(BF16)
     for head in range(heads):
         last[head] = states[head]
     kept[...] = read[core]
@@ -318,7 +359,7 @@
     tokens = mine.shape[0]
     rows = mine.shape[1] // 8
     core = place[0]
-    probe = [load_piece(piece) for piece in pieces]
+    probe = [load_piece(piece, rows) for piece in pieces]
     for source, owner in ((mine, core), (theirs, 1 - core)):
         positions = positions_of(owner, tokens)
         begin = 0
@@ -343,7 +384,7 @@
         functools.partial(read_kernel, entry is not None, tuple(blocks)),
         "read_values",
         place,
-        (mine, theirs, own, stack, maps[0], maps[1], *pieces, *extra),
+        (mine, theirs, own, stack, maps[1], maps[2], *pieces, *extra),
         [
             ((2 * tokens, width), F32),
             ((tokens, width), BF16),
@@ -354,12 +395,13 @@
     )
 
 
-def recur_kernel(weighting, with_state, blocks, chips, lists, place, mine, theirs, total, forth, back, *refs):
+def recur_kernel(weighting, with_state, blocks, chips, lists, place, mine, theirs, total, forth, back, read, *refs):
     count = len(blocks)
     pieces, refs = refs[:count], refs[count:]
     if with_state:
         (first, final, *refs) = refs
     (grads, last, start, *refs) = refs
+    width = total.shape[1]
     shares, (sums, up) = refs[: len(lists)], refs[len(lists) :]
     tokens = mine.shape[0]
     spans, heads = forth.shape[1:3]
@@ -370,26 +412,33 @@
     for half, span in steps:
         begin = half * tokens + span * SPAN
         for head in range(heads):
-            block = sums[begin : begin + SPAN, head * DK : (head + 1) * DK]
-            fresh = dot(forth[half, span, head, :, DK:], block)
-            result = dot(forth[half, span, head, :, :DK], states[head].astype(BF16)) + fresh
-            states[head] = result[:DK]
-            grad = (weighting * result[DK:]).astype(BF16)
-            up[half, span, head] = dot(back[half, span, head, :, DK:], grad)
+            block = sums[begin : begin + SPAN, head * DK : (head + 1) * DK].T.astype(BF16)
+            left = jnp.concatenate([states[head].astype(BF16), block], 1)
+            result = dot(left, back[half, span, head])
+            states[head] = result[:, :DK]
+            up[half, span, head] = (weighting * result[:, DK:]).astype(BF16)
     for head in range(heads):
         last[head] = states[head]
     states = [final[head] if with_state else zero for head in range(heads)]
     for half, span in reversed(steps):
         begin = half * tokens + span * SPAN
         for head in range(heads):
-            result = dot(back[half, span, head, :, :DK], states[head].astype(BF16))
-            result = result + up[half, span, head]
-            states[head] = result[:DK]
-            grads[begin : begin + SPAN, head * DK : (head + 1) * DK] = result[DK:].astype(BF16)
+            left = jnp.concatenate([states[head].astype(BF16), up[half, span, head]], 1)
+            result = dot(left, forth[half, span, head])
+            states[head] = result[:, :DK]
+            row = begin // width * width + head * DK
+            grads[row : row + DK, begin % width : begin % width + SPAN] = result[:, DK:].astype(BF16)
+    grads[2 * tokens :, :] = read[...]
     for head in range(heads):
         start[head] = states[head]
     if lists:
         put_products(place, chips, lists, mine, theirs, grads, shares)
+
+
+def grads_of(grads, owner, tokens):
+    width = grads.shape[1]
+    block = grads[positions_of(owner, tokens), :]
+    return jnp.concatenate([block[i : i + width] for i in range(0, tokens, width)], 1)
 
 
 def put_products(place, chips, lists, mine, theirs, grads, outs):
@@ -399,14 +448,15 @@
     else:
         columns = pl.ds(pl.multiple_of(lax.bitwise_xor(place[1], chips) * 4 * ROWS, 4 * ROWS), 4 * ROWS)
     core = place[0]
-    part = dot_tn(mine[:, columns], grads[positions_of(core, tokens), :])
-    part += dot_tn(theirs[:, columns], grads[positions_of(1 - core, tokens), :])
+    part = dot(grads_of(grads, core, tokens), mine[:, columns])
+    part += dot(grads_of(grads, 1 - core, tokens), theirs[:, columns])
+    part = part.T
     for out, indices in zip(outs, lists):
         for slot, index in enumerate(indices):
             out[slot] = part[index * ROWS : (index + 1) * ROWS].astype(out.dtype)
 
 
-def recur(weighting, place, mine, theirs, total, maps, blocks, pieces, chips, lists, states):
+def recur(weighting, place, mine, theirs, total, maps, read, blocks, pieces, chips, lists, states):
     tokens = mine.shape[0]
     width = total.shape[1]
     spans, heads = maps[0].shape[1:3]
@@ -417,12 +467,12 @@
         ),
         "recur",
         place,
-        (mine, theirs, total, maps[0], maps[2], *pieces, *extra),
-        [((2 * tokens, width), BF16), ((heads, DK, DK), F32), ((heads, DK, DK), F32)]
+        (mine, theirs, total, maps[0], maps[1], read, *pieces, *extra),
+        [((3 * tokens, width), BF16), ((heads, DK, DK), F32), ((heads, DK, DK), F32)]
         + [((len(part), ROWS, width), BF16) for part in lists],
         scratch=[
-            pltpu.VMEM((2 * tokens, width), BF16),
-            pltpu.VMEM((2, spans, heads, 2 * DK, DK), F32),
+            pltpu.VMEM((2 * tokens, width), F32),
+            pltpu.VMEM((2, spans, heads, DK, SPAN), BF16),
         ],
     )
 
@@ -449,24 +499,97 @@
     )
 
 
-def join_kernel(place, *refs):
-    core = place[0]
-    count = len(refs) // 3
-    for index in range(count):
-        same, cross, whole = refs[2 * index], refs[2 * index + 1], refs[2 * count + index]
-        width = same.shape[1]
-        whole[:, positions_of(core, width)] = same[...]
-        whole[:, positions_of(1 - core, width)] = cross[...]
-
-
-def join(place, *pairs):
+def keep_kernel(place, mine, theirs, grads, keep_x, keep_y):
+    for chips, half, out in ((1, 1, keep_x), (2, 0, keep_y)):
+        for block in range(2):
+            columns = half_block(place, chips, block, half)
+            out[block] = products(place, mine, theirs, grads, columns)
+
+
+def half_block(place, chips, block, half):
+    index = 2 * (2 * lax.bitwise_xor(place[1], chips) + block) + half
+    return pl.ds(pl.multiple_of(index * ROWS, ROWS), ROWS)
+
+
+def products(place, mine, theirs, grads, columns):
+    tokens = mine.shape[0]
+    core = place[0]
+    part = dot(grads_of(grads, core, tokens), mine[:, columns])
+    part += dot(grads_of(grads, 1 - core, tokens), theirs[:, columns])
+    return part.T
+
+
+def keep(place, mine, theirs, grads):
+    shape = (2, ROWS, grads.shape[1])
+    return kernel_call(keep_kernel, "keep", place, (mine, theirs, grads), [(shape, F32)] * 2)
+
+
+def near_kernel(place, mine, theirs, grads, grads_other, read, near_x, near_y, own, mixed):
+    core = place[0]
+    tokens, width = read.shape
+    join(place, read[...], grads_other[2 * tokens :, :], mixed)
+    jobs = (
+        (half_block(place, 1, core, 0), near_x),
+        (half_block(place, 2, core, 1), near_y),
+        (pl.ds(pl.multiple_of((2 * place[1] + core) * 2 * ROWS, 2 * ROWS), 2 * ROWS), own),
+    )
+    for columns, out in jobs:
+        for source, owner in ((grads, core), (grads_other, 1 - core)):
+            part = products(place, mine, theirs, source, columns)
+            out[:, positions_of(owner, width)] = part.astype(out.dtype)
+
+
+def near(place, mine, theirs, grads, grads_other, read):
+    rows, width = read.shape
     return kernel_call(
-        join_kernel,
-        "join",
+        near_kernel,
+        "near",
         place,
-        [block for pair in pairs for block in pair],
-        [((same.shape[0], 2 * same.shape[1]), same.dtype) for same, cross in pairs],
-    )
+        (mine, theirs, grads, grads_other, read),
+        [
+            ((ROWS, 2 * width), BF16),
+            ((ROWS, 2 * width), BF16),
+            ((2 * ROWS, 2 * width), F32),
+            ((rows, 2 * width), BF16),
+        ],
+    )
+
+
+def join(place, same, cross, whole):
+    width = same.shape[1]
+    whole[:, positions_of(place[0], width)] = same
+    whole[:, positions_of(1 - place[0], width)] = cross
+
+
+def relay_kernel(place, far_x, far_y, keep_x, keep_y, after, *outs):
+    core = place[0]
+    for index, (far, keep) in enumerate(((far_x, keep_y), (far_y, keep_x))):
+        for which, owner in enumerate((core, 1 - core)):
+            outs[2 * index + which][...] = (keep[owner] + far[owner].astype(F32)).astype(BF16)
+
+
+def relay(place, far_x, far_y, keep_x, keep_y, after):
+    shape = keep_x.shape[1:]
+    operands = (far_x, far_y, keep_x, keep_y, after)
+    return kernel_call(relay_kernel, "relay", place, operands, [(shape, BF16)] * 4)
+
+
+def finish_kernel(place, own, near_x, near_y, top_same, low_same, top_cross, low_cross, whole):
+    core = place[0]
+    width = top_same.shape[1]
+    for owner, top, low in ((core, top_same, low_same), (1 - core, top_cross, low_cross)):
+        columns = positions_of(owner, width)
+        for rows, first, second in ((slice(0, ROWS), near_x, top), (slice(ROWS, 2 * ROWS), near_y, low)):
+            part = first[:, columns].astype(F32) + second[...].astype(F32)
+            whole[rows, columns] = own[rows, columns] + part
+
+
+def finish(place, *parts):
+    return kernel_call(finish_kernel, "finish", place, parts, [(parts[0].shape, F32)])[0]
+
+
+def join_kernel(place, same, cross, whole):
+    join(place, same[...], cross[...], whole)
 
 
 def local(square, dp_size, ctx_size, queries, keys, values, decay, beta, inputs, probe):
@@ -496,37 +619,36 @@
         return lax.dynamic_slice_in_dim(block, index * width, width, 1)
 
     kept, given, own, stack, gates = pack(place, square, queries, keys, values, decay, beta, probe)
-    gates, mine = lax.optimization_barrier((gates, mine))
-    gates_t = swap(gates)
     if square:
+        stack, mine = lax.optimization_barrier((stack, mine))
+        stack = swap(stack)
+        theirs = swap(mine)
         x_one = send(kept, 1, 0)
         y_one = send(given, 2, 1)
-        stack = swap(stack)
-        theirs = swap(mine)
-        stack, kept, given = lax.optimization_barrier((stack, kept, given))
         x_two = send(given, 1, 1)
-        y_two = send(kept, 2, 0)
-        maps = prepare(place, 0, own, gates, ())
+        maps = prepare(place, 0, tokens, width, own, (gates,))
+        late, *maps = lax.optimization_barrier((kept, *maps))
+        y_two = send(late, 2, 0)
         x_one, y_one, *maps = lax.optimization_barrier((x_one, y_one, *maps))
         far_one = send(x_one, 2, 0)
         far_two = send(y_one, 1, 0)
-        maps = prepare(place, 1, stack, gates_t, maps)
-        pieces = [kept, stack, x_one, y_one, far_one, far_two, x_two, y_two]
+        maps = prepare(place, 1, tokens, width, stack, maps)
+        pieces = [kept, stack, x_one, y_one, x_two, y_two, far_one, far_two]
         places = [
             (0, "same"),
             (0, "other"),
             (1, "same"),
             (2, "other"),
+            (1, "other"),
+            (2, "same"),
             (3, "same"),
             (3, "other"),
-            (1, "other"),
-            (2, "same"),
         ]
     else:
         stack = swap(stack)
         theirs = swap(mine)
-        maps = prepare(place, 0, own, gates, ())
-        maps = prepare(place, 1, stack, gates_t, maps)
+        maps = prepare(place, 0, tokens, width, own, (gates,))
+        maps = prepare(place, 1, tokens, width, stack, maps)
         gathered = part(lax.all_gather(probe, GROUP, axis=0, tiled=True), core)
         places = list(range(8))
         rows = D // len(places)
@@ -550,13 +672,12 @@
         own,
         stack,
         maps,
-        places[:4],
-        pieces[:4],
+        places[:6],
+        pieces[:6],
     )
     for _ in range(groups - 1):
         entry = shift(read(entry)[3], 1)
     total, read_kept, read_given, unused = read(entry)
-    read_swapped = swap(read_given)
     lists = ((0, 2), (1, 3)) if square else ()
     run = functools.partial(
         recur,
@@ -566,8 +687,9 @@
         theirs,
         total,
         maps,
-        places[4:],
-        pieces[4:],
+        read_given,
+        places[6:],
+        pieces[6:],
         3,
         lists,
     )
@@ -587,32 +709,29 @@
         both = jnp.where(
             core == 0, jnp.concatenate([flat, zero], 1), jnp.concatenate([zero, flat], 1)
         )
-        mixed = join(place, (read_kept, read_swapped))[0]
+        read_swapped = swap(read_given)
+        mixed = kernel_call(
+            join_kernel, "join", place, (read_kept, read_swapped), [((tokens, 2 * width), BF16)]
+        )[0]
         return mixed[None], lax.psum_scatter(both, GROUP, scatter_dimension=0, tiled=True)
 
     far_x = send(shares[0], 1, 0)
     far_y = send(shares[1], 2, 0)
-    upper, lower = (0, 2), (1, 3)
-    near_x, keep_x, keep_y, near_y, own_top, own_low = build(
-        ((1, (upper, lower)), (2, (upper, lower)), (0, (upper, lower))),
-        [BF16, F32, F32, BF16, F32, F32],
-    )
+    grads_other = swap(grads)
+    keep_x, keep_y = keep(place, mine, theirs, grads)
+    near_x, near_y, rest, mixed = near(place, mine, theirs, grads, grads_other, read_kept)
+    after = near_x
     near_x = send(near_x, 1, 0)
     near_y = send(near_y, 2, 0)
-    far_x, far_y = lax.optimization_barrier((far_x, far_y))
-    relay_y = send((keep_y + far_x.astype(F32)).astype(BF16), 2, 0)
-    relay_x = send((keep_x + far_y.astype(F32)).astype(BF16), 1, 0)
-    near_x, near_y, relay_x, relay_y = lax.optimization_barrier((near_x, near_y, relay_x, relay_y))
-    top = own_top + near_x.astype(F32) + relay_y.astype(F32)
-    low = own_low + near_y.astype(F32) + relay_x.astype(F32)
-    sums = jnp.concatenate([top, low], 1)
-
-    def at(block, index):
-        return lax.dynamic_index_in_dim(block, index, 0, keepdims=False)
-
-    near = at(sums, core)
-    distant = swap(at(sums, 1 - core))
-    mixed, result = join(place, (read_kept, read_swapped), (near, distant))
+    top_same, top_cross, low_same, low_cross = relay(place, far_x, far_y, keep_x, keep_y, after)
+    top_same = send(top_same, 2, 0)
+    low_same = send(low_same, 1, 0)
+    near_x, near_y, top_cross, low_cross = lax.optimization_barrier(
+        (near_x, near_y, top_cross, low_cross)
+    )
+    top_cross = send(top_cross, 2, 1)
+    low_cross = send(low_cross, 1, 1)
+    result = finish(place, rest, near_x, near_y, top_same, low_same, top_cross, low_cross)
     return mixed[None], result
 
 

time: 62.3 us -> 55.4 us (0.89)
  waiting for transfers between devices: 18.2 us -> 10.4 us
  starting transfers between devices: 15.7 us -> 17.6 us
  other arithmetic: 1.15 us -> 0.08 us
    ppermute x12 -> x14, waiting for transfers between devices: 16.4 us -> 10.4 us  [send(): return lax.ppermute(block, GROUP, pairs)]
    ppermute x12 -> x14, starting transfers between devices: 13.8 us -> 17 us  [send(): return lax.ppermute(block, GROUP, pairs)]
    ppermute x5 -> x3, waiting for transfers between devices: 1.79 us -> 0.01 us  [swap(): return lax.ppermute(block, 'ctx', partner)]
    ppermute x5 -> x3, starting transfers between devices: 1.88 us -> 0.6 us  [swap(): return lax.ppermute(block, 'ctx', partner)]
    convert_element_type x2 -> x0, other arithmetic: 0.82 us -> none  [the longest x1 0.76 us: local(): relay_x = send((keep_x + far_y.astype(F32)).astype(BF16), 1, 0)]
    pallas_call x6 -> x8, Pallas kernels: 24.2 us -> 23.9 us  [kernel_call(): pl.pallas_call(kernel, grid_spec=pltpu.PrefetchScalarGridSpec(num_scalar_...]
  transfers between devices with their start and end apart: 17 -> 17, of which waited for: 10 -> 9; matrix products, arithmetic and copies ran while one was open for 1% -> 0% of each run, Pallas kernels for 23% -> 32%
where the time goes in v3:
time: 55.4 us; the launch traced here: 55 us
  Pallas kernels  26.2 us (47%)
  starting transfers between devices  17.6 us (32%)
  waiting for transfers between devices  10.4 us (19%)
  between operations  0.73 us (1%)
    pallas_call x8, Pallas kernels, kernel_call(): pl.pallas_call(kernel, grid_spec=pltpu.PrefetchScalarGridSpec(num_scalar_...  23.9 us
    ppermute x14, starting transfers between devices, send(): return lax.ppermute(block, GROUP, pairs)  17 us
    ppermute x14, waiting for transfers between devices, send(): return lax.ppermute(block, GROUP, pairs)  10.4 us
    pallas_call x1, Pallas kernels, pack(): pl.pallas_call(pack_kernel, grid_spec=pltpu.PrefetchScalarGridSpec(num_sc...  2.25 us
  transfers between devices with their start and end apart: 17, of which 9 were waited for; matrix products, arithmetic and copies ran while one was open for 0% of the time, Pallas kernels for 32%

profile of v3, /device:TPU:0, one launch (start us, length us, event | category | flops | bytes accessed | tf_op | source)
XLA Modules:
  0.0 55.0 jit_solution(2129519751823056614)
XLA Ops:
  0.7 2.2 %pack.1 = (bf16[512,256]{1,0:T(8,128)(2,1)S(1)}, bf16[512,256]{1,0:T(8,128)(2,1)S(1)}, bf16[3,512,256]{2,1,0:T(8,128)(2,1)S(1)}, bf16[2080,256]{1,0:T(8,128)(2,1)S(1)}, f32[2,4,512]{2,1,0:T(4,128)S(1)}) custom-call(s32[2]{0:T(128)S(1)} %pad_add_fusion.place, bf16[1,512,512]{2,1,0:T(8,128)(2,1)} %queries.1, bf16[1,512,512]{2,1,0:T(8,128)(2,1)} %keys.1, ...), custom_call_target="tpu_custom_call" | custom-call | flops 11000000 | bytes 30000 | tf_op jit(solution)/shard_map/pack/pallas_call | solution.py:149
  3.6 2.9 %collective-permute-start.2 = (bf16[512,256]{1,0:T(8,128)(2,1)S(1)}, bf16[512,256]{1,0:T(8,128)(2,1)S(1)}, u32[]{:S(2)}, u32[]{:S(2)}) collective-permute-start(bf16[512,256]{1,0:T(8,128)(2,1)S(1)} %get-tuple-element.64.refs_0_), channel_id=1, source_target_pairs={{0,8},{4,12},{8,0},{12,4},{16,24},{20,28},{24,16},{28,20},{1,9},{5... | collective-permute-start | bytes 786440 | tf_op jit(solution)/shard_map/ppermute | solution.py:616
  6.5 0.9 %collective-permute-start.3 = (bf16[512,256]{1,0:T(8,128)(2,1)S(1)}, bf16[512,256]{1,0:T(8,128)(2,1)S(1)}, u32[]{:S(2)}, u32[]{:S(2)}) collective-permute-start(bf16[512,256]{1,0:T(8,128)(2,1)S(1)} %get-tuple-element.49), channel_id=1, source_target_pairs={{0,20},{4,16},{8,28},{12,24},{16,4},{20,0},{24,12},{28,8},{1,21},{... | collective-permute-start | bytes 786440 | tf_op jit(solution)/shard_map/ppermute | solution.py:616
  7.4 4.3 %prepare.2 = (bf16[2,4,2,256,256]{4,3,2,1,0:T(8,128)(2,1)S(1)}, bf16[2,4,2,256,256]{4,3,2,1,0:T(8,128)(2,1)S(1)}, bf16[2,4,2,256,256]{4,3,2,1,0:T(8,128)(2,1)S(1)}) custom-call(s32[2]{0:T(128)S(1)} %pad_add_fusion.place, bf16[3,512,256]{2,1,0:T(8,128)(2,1)S(1)} %get-tuple-element.46.stack.own, f32[2,4,512]{2,1,0:T(4,128)S(1)} %get-tuple-element.50.refs_0_), custom_call_target="tpu_custom_call" | custom-call | flops 11000000 | bytes 30000 | tf_op jit(solution)/shard_map/prepare/pallas_call | solution.py:35
  11.7 0.7 %collective-permute-start.5 = (bf16[512,256]{1,0:T(8,128)(2,1)S(1)}, bf16[512,256]{1,0:T(8,128)(2,1)S(1)}, u32[]{:S(2)}, u32[]{:S(2)}) collective-permute-start(bf16[512,256]{1,0:T(8,128)(2,1)S(1)} %get-tuple-element.64.refs_0_), channel_id=1, source_target_pairs={{0,16},{4,20},{8,24},{12,28},{16,0},{20,4},{24,8},{28,12},{1,17},{... | collective-permute-start | bytes 786440 | tf_op jit(solution)/shard_map/ppermute | solution.py:616
  12.4 0.7 %collective-permute-done.2.refs_2_ = bf16[512,256]{1,0:T(8,128)(2,1)S(1)} collective-permute-done((bf16[512,256]{1,0:T(8,128)(2,1)S(1)}, bf16[512,256]{1,0:T(8,128)(2,1)S(1)}, u32[]{:S(2)}, u32[]{:S(2)}) %collective-permute-start.2) | collective-permute-done | bytes 262176 | tf_op jit(solution)/shard_map/ppermute | solution.py:616
  13.6 1.4 %collective-permute-done.3.refs_3_ = bf16[512,256]{1,0:T(8,128)(2,1)S(1)} collective-permute-done((bf16[512,256]{1,0:T(8,128)(2,1)S(1)}, bf16[512,256]{1,0:T(8,128)(2,1)S(1)}, u32[]{:S(2)}, u32[]{:S(2)}) %collective-permute-start.3) | collective-permute-done | bytes 262176 | tf_op jit(solution)/shard_map/ppermute | solution.py:616
  15.0 1.6 %collective-permute-start.6 = (bf16[512,256]{1,0:T(8,128)(2,1)S(1)}, bf16[512,256]{1,0:T(8,128)(2,1)S(1)}, u32[]{:S(2)}, u32[]{:S(2)}) collective-permute-start(bf16[512,256]{1,0:T(8,128)(2,1)S(1)} %collective-permute-done.2.refs_2_), channel_id=1, source_target_pairs={{0,16},{4,20},{8,24},{12,28},{16,0},{20,4},{24,8},{28,12},{1,17},{... | collective-permute-start | bytes 786440 | tf_op jit(solution)/shard_map/ppermute | solution.py:616
  17.1 4.3 %prepare.3 = (bf16[2,4,2,256,256]{4,3,2,1,0:T(8,128)(2,1)S(1)}, bf16[2,4,2,256,256]{4,3,2,1,0:T(8,128)(2,1)S(1)}, bf16[2,4,2,256,256]{4,3,2,1,0:T(8,128)(2,1)S(1)}) custom-call(s32[2]{0:T(128)S(1)} %pad_add_fusion.place, bf16[2080,256]{1,0:T(8,128)(2,1)S(1)} %collective-permute-done.1.stack.refs_1_, ...), custom_call_target="tpu_custom_call", output_to_operand_aliasing={{0}: (2, {}), {1}: (3, {}), {2}: (4, {})} | custom-call | flops 11000000 | bytes 30000 | tf_op jit(solution)/shard_map/prepare/pallas_call | solution.py:35
  21.5 4.5 %read_values.1 = (f32[1024,256]{1,0:T(8,128)S(1)}, bf16[512,256]{1,0:T(8,128)(2,1)S(1)}, bf16[512,256]{1,0:T(8,128)(2,1)S(1)}, f32[2,128,128]{2,1,0:T(8,128)}) custom-call(s32[2]{0:T(128)S(1)} %pad_add_fusion.place, bf16[512,4096]{1,0:T(8,128)(2,1)S(1)} %bitcast.5, bf16[512,4096]{1,0:T(8,128)(2,1)S(1)} %collective-permute-done.theirs, ...), custom_call_target="tpu_custom_call" | custom-call | flops 11000000 | bytes 30000 | tf_op jit(solution)/shard_map/read_values/pallas_call | solution.py:35
  26.3 0.9 %collective-permute-done.7.refs_1_ = bf16[512,256]{1,0:T(8,128)(2,1)S(1)} collective-permute-done((bf16[512,256]{1,0:T(8,128)(2,1)S(1)}, bf16[512,256]{1,0:T(8,128)(2,1)S(1)}, u32[]{:S(2)}, u32[]{:S(2)}) %collective-permute-start.7) | collective-permute-done | bytes 262176 | tf_op jit(solution)/shard_map/ppermute | solution.py:616
  27.3 4.5 %recur.1 = (bf16[1536,256]{1,0:T(8,128)(2,1)S(1)}, f32[2,128,128]{2,1,0:T(8,128)}, f32[2,128,128]{2,1,0:T(8,128)}, bf16[2,256,256]{2,1,0:T(8,128)(2,1)S(1)}, bf16[2,256,256]{2,1,0:T(8,128)(2,1)S(1)}) custom-call(s32[2]{0:T(128)S(1)} %pad_add_fusion.place, bf16[512,4096]{1,0:T(8,128)(2,1)S(1)} %bitcast.6, bf16[512,4096]{1,0:T(8,128)(2,1)S(1)} %collective-permute-done.theirs, ...), custom_call_target="tpu_custom_call" | custom-call | flops 11000000 | bytes 30000 | tf_op jit(solution)/shard_map/recur/pallas_call | solution.py:35
  31.8 1.0 %collective-permute-start.11 = (bf16[2,256,256]{2,1,0:T(8,128)(2,1)S(1)}, bf16[2,256,256]{2,1,0:T(8,128)(2,1)S(1)}, u32[]{:S(2)}, u32[]{:S(2)}) collective-permute-start(bf16[2,256,256]{2,1,0:T(8,128)(2,1)S(1)} %get-tuple-element.74), channel_id=1, source_target_pairs={{0,8},{4,12},{8,0},{12,4},{16,24},{20,28},{24,16},{28,20},{1,9},{5... | collective-permute-start | bytes 786440 | tf_op jit(solution)/shard_map/ppermute | solution.py:616
  32.7 1.5 %collective-permute-start.12 = (bf16[2,256,256]{2,1,0:T(8,128)(2,1)S(1)}, bf16[2,256,256]{2,1,0:T(8,128)(2,1)S(1)}, u32[]{:S(2)}, u32[]{:S(2)}) collective-permute-start(bf16[2,256,256]{2,1,0:T(8,128)(2,1)S(1)} %get-tuple-element.75), channel_id=1, source_target_pairs={{0,16},{4,20},{8,24},{12,28},{16,0},{20,4},{24,8},{28,12},{1,17},{... | collective-permute-start | bytes 786440 | tf_op jit(solution)/shard_map/ppermute | solution.py:616
  34.3 2.7 %near.1 = (bf16[256,512]{1,0:T(8,128)(2,1)S(1)}, bf16[256,512]{1,0:T(8,128)(2,1)S(1)}, f32[512,512]{1,0:T(8,128)S(1)}, bf16[512,512]{1,0:T(8,128)(2,1)}) custom-call(s32[2]{0:T(128)S(1)} %pad_add_fusion.place, bf16[512,4096]{1,0:T(8,128)(2,1)S(1)} %bitcast.7, bf16[512,4096]{1,0:T(8,128)(2,1)S(1)} %collective-permute-done.theirs, ...), custom_call_target="tpu_custom_call" | custom-call | flops 11000000 | bytes 30000 | tf_op jit(solution)/shard_map/near/pallas_call | solution.py:35
  36.9 1.6 %collective-permute-start.10 = (bf16[256,512]{1,0:T(8,128)(2,1)S(1)}, bf16[256,512]{1,0:T(8,128)(2,1)S(1)}, u32[]{:S(2)}, u32[]{:S(2)}) collective-permute-start(bf16[256,512]{1,0:T(8,128)(2,1)S(1)} %get-tuple-element.73), channel_id=1, source_target_pairs={{0,16},{4,20},{8,24},{12,28},{16,0},{20,4},{24,8},{28,12},{1,17},{... | collective-permute-start | bytes 786440 | tf_op jit(solution)/shard_map/ppermute | solution.py:616
  38.9 1.4 %keep.1 = (f32[2,256,256]{2,1,0:T(8,128)S(1)}, f32[2,256,256]{2,1,0:T(8,128)S(1)}) custom-call(s32[2]{0:T(128)S(1)} %pad_add_fusion.place, bf16[512,4096]{1,0:T(8,128)(2,1)S(1)} %bitcast.8, bf16[512,4096]{1,0:T(8,128)(2,1)S(1)} %collective-permute-done.theirs, bf16[1536,256]{1,0:T(8,128)(2,1)S(1)} %get-tuple-element.68.grads), custom_call_target="tpu_custom_call" | custom-call | flops 11000000 | bytes 30000 | tf_op jit(solution)/shard_map/keep/pallas_call | solution.py:35
  40.5 1.4 %collective-permute-done.12.far_y = bf16[2,256,256]{2,1,0:T(8,128)(2,1)S(1)} collective-permute-done((bf16[2,256,256]{2,1,0:T(8,128)(2,1)S(1)}, bf16[2,256,256]{2,1,0:T(8,128)(2,1)S(1)}, u32[]{:S(2)}, u32[]{:S(2)}) %collective-permute-start.12) | collective-permute-done | bytes 262176 | tf_op jit(solution)/shard_map/ppermute | solution.py:616
  42.6 1.5 %collective-permute-start.13 = (bf16[256,256]{1,0:T(8,128)(2,1)S(1)}, bf16[256,256]{1,0:T(8,128)(2,1)S(1)}, u32[]{:S(2)}, u32[]{:S(2)}) collective-permute-start(bf16[256,256]{1,0:T(8,128)(2,1)S(1)} %get-tuple-element.82), channel_id=1, source_target_pairs={{0,16},{4,20},{8,24},{12,28},{16,0},{20,4},{24,8},{28,12},{1,17},{... | collective-permute-start | bytes 393224 | tf_op jit(solution)/shard_map/ppermute | solution.py:616
  44.1 1.4 %collective-permute-start.14 = (bf16[256,256]{1,0:T(8,128)(2,1)S(1)}, bf16[256,256]{1,0:T(8,128)(2,1)S(1)}, u32[]{:S(2)}, u32[]{:S(2)}) collective-permute-start(bf16[256,256]{1,0:T(8,128)(2,1)S(1)} %get-tuple-element.83), channel_id=1, source_target_pairs={{0,8},{4,12},{8,0},{12,4},{16,24},{20,28},{24,16},{28,20},{1,9},{5... | collective-permute-start | bytes 393224 | tf_op jit(solution)/shard_map/ppermute | solution.py:616
  45.5 2.1 %collective-permute-done.10.near_y = bf16[256,512]{1,0:T(8,128)(2,1)S(1)} collective-permute-done((bf16[256,512]{1,0:T(8,128)(2,1)S(1)}, bf16[256,512]{1,0:T(8,128)(2,1)S(1)}, u32[]{:S(2)}, u32[]{:S(2)}) %collective-permute-start.10) | collective-permute-done | bytes 262176 | tf_op jit(solution)/shard_map/ppermute | solution.py:616
  47.7 2.4 %collective-permute-start.16 = (bf16[256,256]{1,0:T(8,128)(2,1)S(1)}, bf16[256,256]{1,0:T(8,128)(2,1)S(1)}, u32[]{:S(2)}, u32[]{:S(2)}) collective-permute-start(bf16[256,256]{1,0:T(8,128)(2,1)S(1)} %get-tuple-element.85), channel_id=1, source_target_pairs={{0,12},{4,8},{8,4},{12,0},{16,28},{20,24},{24,20},{28,16},{1,13},{... | collective-permute-start | bytes 393224 | tf_op jit(solution)/shard_map/ppermute | solution.py:616
  50.1 3.2 %collective-permute-done.15.top_cross = bf16[256,256]{1,0:T(8,128)(2,1)S(1)} collective-permute-done((bf16[256,256]{1,0:T(8,128)(2,1)S(1)}, bf16[256,256]{1,0:T(8,128)(2,1)S(1)}, u32[]{:S(2)}, u32[]{:S(2)}) %collective-permute-start.15) | collective-permute-done | bytes 131104 | tf_op jit(solution)/shard_map/ppermute | solution.py:616
  53.3 1.7 %finish.1 = f32[512,512]{1,0:T(8,128)} custom-call(s32[2]{0:T(128)S(1)} %pad_add_fusion.place, f32[512,512]{1,0:T(8,128)S(1)} %get-tuple-element.71.own, bf16[256,512]{1,0:T(8,128)(2,1)S(1)} %collective-permute-done.9.near_x, bf16[256,512]{1,0:T(8,128)(2,1)S(1)} %collective-permute-done.10.near_y, bf16[256,256]{1,0:T(8,128)(2,1)S(1)} %collective-permute-done.13.top_same, ...), custom_call_target="tpu_custom_call" | custom-call | flops 11000000 | bytes 30000 | tf_op jit(solution)/shard_map/finish/pallas_call | solution.py:35
  (22 shorter events, 3.5 us)
Async XLA Ops:
  3.0 18.5 %collective-permute-start = (bf16[512,4096]{1,0:T(8,128)(2,1)}, bf16[512,4096]{1,0:T(8,128)(2,1)S(1)}, u32[]{:S(2)}, u32[]{:S(2)}) collective-permute-start(bf16[512,4096]{1,0:T(8,128)(2,1)} %bitcast.4), channel_id=1, source_target_pairs={{0,4},{4,0},{1,5},{5,1},{2,6},{6,2},{3,7},{7,3},{8,12},{12,8},{9,1... | collective-permute-start | bytes 12582920 | tf_op jit(solution)/shard_map/ppermute | solution.py:608
  3.5 13.1 %collective-permute-start.1 = (bf16[2080,256]{1,0:T(8,128)(2,1)S(1)}, bf16[2080,256]{1,0:T(8,128)(2,1)S(1)}, u32[]{:S(2)}, u32[]{:S(2)}) collective-permute-start(bf16[2080,256]{1,0:T(8,128)(2,1)S(1)} %get-tuple-element.47), channel_id=1, source_target_pairs={{0,4},{4,0},{1,5},{5,1},{2,6},{6,2},{3,7},{7,3},{8,12},{12,8},{9,1... | collective-permute-start | bytes 3194888 | tf_op jit(solution)/shard_map/ppermute | solution.py:608
  3.6 9.5 %collective-permute-start.2 = (bf16[512,256]{1,0:T(8,128)(2,1)S(1)}, bf16[512,256]{1,0:T(8,128)(2,1)S(1)}, u32[]{:S(2)}, u32[]{:S(2)}) collective-permute-start(bf16[512,256]{1,0:T(8,128)(2,1)S(1)} %get-tuple-element.64.refs_0_), channel_id=1, source_target_pairs={{0,8},{4,12},{8,0},{12,4},{16,24},{20,28},{24,16},{28,20},{1,9},{5... | collective-permute-start | bytes 786440 | tf_op jit(solution)/shard_map/ppermute | solution.py:616
  6.5 8.5 %collective-permute-start.3 = (bf16[512,256]{1,0:T(8,128)(2,1)S(1)}, bf16[512,256]{1,0:T(8,128)(2,1)S(1)}, u32[]{:S(2)}, u32[]{:S(2)}) collective-permute-start(bf16[512,256]{1,0:T(8,128)(2,1)S(1)} %get-tuple-element.49), channel_id=1, source_target_pairs={{0,20},{4,16},{8,28},{12,24},{16,4},{20,0},{24,12},{28,8},{1,21},{... | collective-permute-start | bytes 786440 | tf_op jit(solution)/shard_map/ppermute | solution.py:616
  11.7 9.8 %copy-start = (bf16[1,512,4096]{2,1,0:T(8,128)(2,1)S(1)}, bf16[1,512,4096]{2,1,0:T(8,128)(2,1)}, u32[]{:S(2)}) copy-start(bf16[1,512,4096]{2,1,0:T(8,128)(2,1)} %param.12) | copy-start | bytes 12582916
  11.7 9.7 %collective-permute-start.5 = (bf16[512,256]{1,0:T(8,128)(2,1)S(1)}, bf16[512,256]{1,0:T(8,128)(2,1)S(1)}, u32[]{:S(2)}, u32[]{:S(2)}) collective-permute-start(bf16[512,256]{1,0:T(8,128)(2,1)S(1)} %get-tuple-element.64.refs_0_), channel_id=1, source_target_pairs={{0,16},{4,20},{8,24},{12,28},{16,0},{20,4},{24,8},{28,12},{1,17},{... | collective-permute-start | bytes 786440 | tf_op jit(solution)/shard_map/ppermute | solution.py:616
  13.0 8.4 %collective-permute-start.4 = (bf16[512,256]{1,0:T(8,128)(2,1)S(1)}, bf16[512,256]{1,0:T(8,128)(2,1)S(1)}, u32[]{:S(2)}, u32[]{:S(2)}) collective-permute-start(bf16[512,256]{1,0:T(8,128)(2,1)S(1)} %get-tuple-element.49), channel_id=1, source_target_pairs={{0,12},{4,8},{8,4},{12,0},{16,28},{20,24},{24,20},{28,16},{1,13},{... | collective-permute-start | bytes 786440 | tf_op jit(solution)/shard_map/ppermute | solution.py:616
  15.0 11.3 %collective-permute-start.6 = (bf16[512,256]{1,0:T(8,128)(2,1)S(1)}, bf16[512,256]{1,0:T(8,128)(2,1)S(1)}, u32[]{:S(2)}, u32[]{:S(2)}) collective-permute-start(bf16[512,256]{1,0:T(8,128)(2,1)S(1)} %collective-permute-done.2.refs_2_), channel_id=1, source_target_pairs={{0,16},{4,20},{8,24},{12,28},{16,0},{20,4},{24,8},{28,12},{1,17},{... | collective-permute-start | bytes 786440 | tf_op jit(solution)/shard_map/ppermute | solution.py:616
  16.6 10.6 %collective-permute-start.7 = (bf16[512,256]{1,0:T(8,128)(2,1)S(1)}, bf16[512,256]{1,0:T(8,128)(2,1)S(1)}, u32[]{:S(2)}, u32[]{:S(2)}) collective-permute-start(bf16[512,256]{1,0:T(8,128)(2,1)S(1)} %collective-permute-done.3.refs_3_), channel_id=1, source_target_pairs={{0,8},{4,12},{8,0},{12,4},{16,24},{20,28},{24,16},{28,20},{1,9},{5... | collective-permute-start | bytes 786440 | tf_op jit(solution)/shard_map/ppermute | solution.py:616
  31.8 2.5 %collective-permute-start.8 = (bf16[1536,256]{1,0:T(8,128)(2,1)S(1)}, bf16[1536,256]{1,0:T(8,128)(2,1)S(1)}, u32[]{:S(2)}, u32[]{:S(2)}) collective-permute-start(bf16[1536,256]{1,0:T(8,128)(2,1)S(1)} %get-tuple-element.68.grads), channel_id=1, source_target_pairs={{0,4},{4,0},{1,5},{5,1},{2,6},{6,2},{3,7},{7,3},{8,12},{12,8},{9,1... | collective-permute-start | bytes 2359304 | tf_op jit(solution)/shard_map/ppermute | solution.py:608
  31.8 8.7 %collective-permute-start.11 = (bf16[2,256,256]{2,1,0:T(8,128)(2,1)S(1)}, bf16[2,256,256]{2,1,0:T(8,128)(2,1)S(1)}, u32[]{:S(2)}, u32[]{:S(2)}) collective-permute-start(bf16[2,256,256]{2,1,0:T(8,128)(2,1)S(1)} %get-tuple-element.74), channel_id=1, source_target_pairs={{0,8},{4,12},{8,0},{12,4},{16,24},{20,28},{24,16},{28,20},{1,9},{5... | collective-permute-start | bytes 786440 | tf_op jit(solution)/shard_map/ppermute | solution.py:616
  32.7 9.2 %collective-permute-start.12 = (bf16[2,256,256]{2,1,0:T(8,128)(2,1)S(1)}, bf16[2,256,256]{2,1,0:T(8,128)(2,1)S(1)}, u32[]{:S(2)}, u32[]{:S(2)}) collective-permute-start(bf16[2,256,256]{2,1,0:T(8,128)(2,1)S(1)} %get-tuple-element.75), channel_id=1, source_target_pairs={{0,16},{4,20},{8,24},{12,28},{16,0},{20,4},{24,8},{28,12},{1,17},{... | collective-permute-start | bytes 786440 | tf_op jit(solution)/shard_map/ppermute | solution.py:616
  36.9 10.6 %collective-permute-start.10 = (bf16[256,512]{1,0:T(8,128)(2,1)S(1)}, bf16[256,512]{1,0:T(8,128)(2,1)S(1)}, u32[]{:S(2)}, u32[]{:S(2)}) collective-permute-start(bf16[256,512]{1,0:T(8,128)(2,1)S(1)} %get-tuple-element.73), channel_id=1, source_target_pairs={{0,16},{4,20},{8,24},{12,28},{16,0},{20,4},{24,8},{28,12},{1,17},{... | collective-permute-start | bytes 786440 | tf_op jit(solution)/shard_map/ppermute | solution.py:616
  38.5 9.2 %collective-permute-start.9 = (bf16[256,512]{1,0:T(8,128)(2,1)S(1)}, bf16[256,512]{1,0:T(8,128)(2,1)S(1)}, u32[]{:S(2)}, u32[]{:S(2)}) collective-permute-start(bf16[256,512]{1,0:T(8,128)(2,1)S(1)} %get-tuple-element.72.after), channel_id=1, source_target_pairs={{0,8},{4,12},{8,0},{12,4},{16,24},{20,28},{24,16},{28,20},{1,9},{5... | collective-permute-start | bytes 786440 | tf_op jit(solution)/shard_map/ppermute | solution.py:616
  42.6 7.6 %collective-permute-start.13 = (bf16[256,256]{1,0:T(8,128)(2,1)S(1)}, bf16[256,256]{1,0:T(8,128)(2,1)S(1)}, u32[]{:S(2)}, u32[]{:S(2)}) collective-permute-start(bf16[256,256]{1,0:T(8,128)(2,1)S(1)} %get-tuple-element.82), channel_id=1, source_target_pairs={{0,16},{4,20},{8,24},{12,28},{16,0},{20,4},{24,8},{28,12},{1,17},{... | collective-permute-start | bytes 393224 | tf_op jit(solution)/shard_map/ppermute | solution.py:616
  44.1 6.0 %collective-permute-start.14 = (bf16[256,256]{1,0:T(8,128)(2,1)S(1)}, bf16[256,256]{1,0:T(8,128)(2,1)S(1)}, u32[]{:S(2)}, u32[]{:S(2)}) collective-permute-start(bf16[256,256]{1,0:T(8,128)(2,1)S(1)} %get-tuple-element.83), channel_id=1, source_target_pairs={{0,8},{4,12},{8,0},{12,4},{16,24},{20,28},{24,16},{28,20},{1,9},{5... | collective-permute-start | bytes 393224 | tf_op jit(solution)/shard_map/ppermute | solution.py:616
  47.7 5.7 %collective-permute-start.15 = (bf16[256,256]{1,0:T(8,128)(2,1)S(1)}, bf16[256,256]{1,0:T(8,128)(2,1)S(1)}, u32[]{:S(2)}, u32[]{:S(2)}) collective-permute-start(bf16[256,256]{1,0:T(8,128)(2,1)S(1)} %get-tuple-element.84), channel_id=1, source_target_pairs={{0,20},{4,16},{8,28},{12,24},{16,4},{20,0},{24,12},{28,8},{1,21},{... | collective-permute-start | bytes 393224 | tf_op jit(solution)/shard_map/ppermute | solution.py:616
  47.7 5.7 %collective-permute-start.16 = (bf16[256,256]{1,0:T(8,128)(2,1)S(1)}, bf16[256,256]{1,0:T(8,128)(2,1)S(1)}, u32[]{:S(2)}, u32[]{:S(2)}) collective-permute-start(bf16[256,256]{1,0:T(8,128)(2,1)S(1)} %get-tuple-element.85), channel_id=1, source_target_pairs={{0,12},{4,8},{8,4},{12,0},{16,28},{20,24},{24,20},{28,16},{1,13},{... | collective-permute-start | bytes 393224 | tf_op jit(solution)/shard_map/ppermute | solution.py:616

commit v4 on v3

--- a/solution.py
+++ b/solution.py
@@ -574,18 +574,43 @@
     return kernel_call(relay_kernel, "relay", place, operands, [(shape, BF16)] * 4)
 
 
-def finish_kernel(place, own, near_x, near_y, top_same, low_same, top_cross, low_cross, whole):
+def finish_kernel(place, own, near_x, near_y, top_same, low_same, top_cross, low_cross, whole, sums, sems):
     core = place[0]
     width = top_same.shape[1]
+    copies = []
     for owner, top, low in ((core, top_same, low_same), (1 - core, top_cross, low_cross)):
         columns = positions_of(owner, width)
         for rows, first, second in ((slice(0, ROWS), near_x, top), (slice(ROWS, 2 * ROWS), near_y, low)):
             part = first[:, columns].astype(F32) + second[...].astype(F32)
-            whole[rows, columns] = own[rows, columns] + part
+            sums[rows, columns] = own[rows, columns] + part
+            place_rows = pl.ds(rows.start, ROWS)
+            copies.append(
+                pltpu.make_async_copy(
+                    sums.at[place_rows, columns], whole.at[place_rows, columns], sems.at[len(copies)]
+                )
+            )
+            copies[-1].start()
+    for copy in copies:
+        copy.wait()
 
 
 def finish(place, *parts):
-    return kernel_call(finish_kernel, "finish", place, parts, [(parts[0].shape, F32)])[0]
+    shape = parts[0].shape
+    vmem_spec = pl.BlockSpec(memory_space=pltpu.VMEM)
+    return pl.pallas_call(
+        finish_kernel,
+        grid_spec=pltpu.PrefetchScalarGridSpec(
+            num_scalar_prefetch=1,
+            grid=(),
+            in_specs=[vmem_spec] * len(parts),
+            out_specs=pl.BlockSpec(memory_space=pltpu.HBM),
+            scratch_shapes=[pltpu.VMEM(shape, F32), pltpu.SemaphoreType.DMA((4,))],
+        ),
+        out_shape=jax.ShapeDtypeStruct(shape, F32),
+        compiler_params=pltpu.CompilerParams(vmem_limit_bytes=VMEM_BYTES),
+        cost_estimate=cost(0.01),
+        name="finish",
+    )(place, *(in_vmem(part) for part in parts))
 
 
 def join_kernel(place, same, cross, whole):
@@ -726,9 +751,7 @@
     top_same, top_cross, low_same, low_cross = relay(place, far_x, far_y, keep_x, keep_y, after)
     top_same = send(top_same, 2, 0)
     low_same = send(low_same, 1, 0)
-    near_x, near_y, top_cross, low_cross = lax.optimization_barrier(
-        (near_x, near_y, top_cross, low_cross)
-    )
+    near_x, low_cross = lax.optimization_barrier((near_x, low_cross))
     top_cross = send(top_cross, 2, 1)
     low_cross = send(low_cross, 1, 1)
     result = finish(place, rest, near_x, near_y, top_same, low_same, top_cross, low_cross)

time: 55.4 us -> 53.6 us (0.968)
  starting transfers between devices: 17.6 us -> 16.1 us
    pallas_call x8 -> x7, Pallas kernels: 23.9 us -> 22.2 us  [kernel_call(): pl.pallas_call(kernel, grid_spec=pltpu.PrefetchScalarGridSpec(num_scalar_...]
    pallas_call x0 -> x1, Pallas kernels: none -> 1.57 us  [finish(): pl.pallas_call(finish_kernel, grid_spec=pltpu.PrefetchScalarGridSpec(num_...]
    ppermute x14, starting transfers between devices: 17 us -> 15.5 us  [send(): return lax.ppermute(block, GROUP, pairs)]
  transfers between devices with their start and end apart: 17 -> 17, of which waited for: 9 -> 10; matrix products, arithmetic and copies ran while one was open for 0% -> 0% of each run, Pallas kernels for 32% -> 33%
where the time goes in v4:
time: 53.6 us; the launch traced here: 53.4 us
  Pallas kernels  26.1 us (49%)
  starting transfers between devices  16.1 us (30%)
  waiting for transfers between devices  10.4 us (19%)
  between operations  0.73 us (1%)
    pallas_call x7, Pallas kernels, kernel_call(): pl.pallas_call(kernel, grid_spec=pltpu.PrefetchScalarGridSpec(num_scalar_...  22.2 us
    ppermute x14, starting transfers between devices, send(): return lax.ppermute(block, GROUP, pairs)  15.5 us
    ppermute x14, waiting for transfers between devices, send(): return lax.ppermute(block, GROUP, pairs)  10.4 us
    pallas_call x1, Pallas kernels, pack(): pl.pallas_call(pack_kernel, grid_spec=pltpu.PrefetchScalarGridSpec(num_sc...  2.25 us
    pallas_call x1, Pallas kernels, finish(): pl.pallas_call(finish_kernel, grid_spec=pltpu.PrefetchScalarGridSpec(num_...  1.57 us
  transfers between devices with their start and end apart: 17, of which 10 were waited for; matrix products, arithmetic and copies ran while one was open for 0% of the time, Pallas kernels for 33%

profile of v4, /device:TPU:0, one launch (start us, length us, event | category | flops | bytes accessed | tf_op | source)
XLA Modules:
  0.0 53.4 jit_solution(1788621151221865822)
XLA Ops:
  0.7 2.2 %pack.1 = (bf16[512,256]{1,0:T(8,128)(2,1)S(1)}, bf16[512,256]{1,0:T(8,128)(2,1)S(1)}, bf16[3,512,256]{2,1,0:T(8,128)(2,1)S(1)}, bf16[2080,256]{1,0:T(8,128)(2,1)S(1)}, f32[2,4,512]{2,1,0:T(4,128)S(1)}) custom-call(s32[2]{0:T(128)S(1)} %pad_add_fusion.place, bf16[1,512,512]{2,1,0:T(8,128)(2,1)} %queries.1, bf16[1,512,512]{2,1,0:T(8,128)(2,1)} %keys.1, ...), custom_call_target="tpu_custom_call" | custom-call | flops 11000000 | bytes 30000 | tf_op jit(solution)/shard_map/pack/pallas_call | solution.py:149
  3.6 2.9 %collective-permute-start.2 = (bf16[512,256]{1,0:T(8,128)(2,1)S(1)}, bf16[512,256]{1,0:T(8,128)(2,1)S(1)}, u32[]{:S(2)}, u32[]{:S(2)}) collective-permute-start(bf16[512,256]{1,0:T(8,128)(2,1)S(1)} %get-tuple-element.62.refs_0_), channel_id=1, source_target_pairs={{0,8},{4,12},{8,0},{12,4},{16,24},{20,28},{24,16},{28,20},{1,9},{5... | collective-permute-start | bytes 786440 | tf_op jit(solution)/shard_map/ppermute | solution.py:641
  6.5 0.9 %collective-permute-start.3 = (bf16[512,256]{1,0:T(8,128)(2,1)S(1)}, bf16[512,256]{1,0:T(8,128)(2,1)S(1)}, u32[]{:S(2)}, u32[]{:S(2)}) collective-permute-start(bf16[512,256]{1,0:T(8,128)(2,1)S(1)} %get-tuple-element.47), channel_id=1, source_target_pairs={{0,20},{4,16},{8,28},{12,24},{16,4},{20,0},{24,12},{28,8},{1,21},{... | collective-permute-start | bytes 786440 | tf_op jit(solution)/shard_map/ppermute | solution.py:641
  7.4 4.3 %prepare.2 = (bf16[2,4,2,256,256]{4,3,2,1,0:T(8,128)(2,1)S(1)}, bf16[2,4,2,256,256]{4,3,2,1,0:T(8,128)(2,1)S(1)}, bf16[2,4,2,256,256]{4,3,2,1,0:T(8,128)(2,1)S(1)}) custom-call(s32[2]{0:T(128)S(1)} %pad_add_fusion.place, bf16[3,512,256]{2,1,0:T(8,128)(2,1)S(1)} %get-tuple-element.44.stack.own, f32[2,4,512]{2,1,0:T(4,128)S(1)} %get-tuple-element.48.refs_0_), custom_call_target="tpu_custom_call" | custom-call | flops 11000000 | bytes 30000 | tf_op jit(solution)/shard_map/prepare/pallas_call | solution.py:35
  11.7 0.7 %collective-permute-start.5 = (bf16[512,256]{1,0:T(8,128)(2,1)S(1)}, bf16[512,256]{1,0:T(8,128)(2,1)S(1)}, u32[]{:S(2)}, u32[]{:S(2)}) collective-permute-start(bf16[512,256]{1,0:T(8,128)(2,1)S(1)} %get-tuple-element.62.refs_0_), channel_id=1, source_target_pairs={{0,16},{4,20},{8,24},{12,28},{16,0},{20,4},{24,8},{28,12},{1,17},{... | collective-permute-start | bytes 786440 | tf_op jit(solution)/shard_map/ppermute | solution.py:641
  12.4 0.7 %collective-permute-done.2.refs_2_ = bf16[512,256]{1,0:T(8,128)(2,1)S(1)} collective-permute-done((bf16[512,256]{1,0:T(8,128)(2,1)S(1)}, bf16[512,256]{1,0:T(8,128)(2,1)S(1)}, u32[]{:S(2)}, u32[]{:S(2)}) %collective-permute-start.2) | collective-permute-done | bytes 262176 | tf_op jit(solution)/shard_map/ppermute | solution.py:641
  13.6 1.4 %collective-permute-done.3.refs_3_ = bf16[512,256]{1,0:T(8,128)(2,1)S(1)} collective-permute-done((bf16[512,256]{1,0:T(8,128)(2,1)S(1)}, bf16[512,256]{1,0:T(8,128)(2,1)S(1)}, u32[]{:S(2)}, u32[]{:S(2)}) %collective-permute-start.3) | collective-permute-done | bytes 262176 | tf_op jit(solution)/shard_map/ppermute | solution.py:641
  15.0 1.6 %collective-permute-start.6 = (bf16[512,256]{1,0:T(8,128)(2,1)S(1)}, bf16[512,256]{1,0:T(8,128)(2,1)S(1)}, u32[]{:S(2)}, u32[]{:S(2)}) collective-permute-start(bf16[512,256]{1,0:T(8,128)(2,1)S(1)} %collective-permute-done.2.refs_2_), channel_id=1, source_target_pairs={{0,16},{4,20},{8,24},{12,28},{16,0},{20,4},{24,8},{28,12},{1,17},{... | collective-permute-start | bytes 786440 | tf_op jit(solution)/shard_map/ppermute | solution.py:641
  17.1 4.3 %prepare.3 = (bf16[2,4,2,256,256]{4,3,2,1,0:T(8,128)(2,1)S(1)}, bf16[2,4,2,256,256]{4,3,2,1,0:T(8,128)(2,1)S(1)}, bf16[2,4,2,256,256]{4,3,2,1,0:T(8,128)(2,1)S(1)}) custom-call(s32[2]{0:T(128)S(1)} %pad_add_fusion.place, bf16[2080,256]{1,0:T(8,128)(2,1)S(1)} %collective-permute-done.1.stack.refs_1_, ...), custom_call_target="tpu_custom_call", output_to_operand_aliasing={{0}: (2, {}), {1}: (3, {}), {2}: (4, {})} | custom-call | flops 11000000 | bytes 30000 | tf_op jit(solution)/shard_map/prepare/pallas_call | solution.py:35
  21.5 4.5 %read_values.1 = (f32[1024,256]{1,0:T(8,128)S(1)}, bf16[512,256]{1,0:T(8,128)(2,1)S(1)}, bf16[512,256]{1,0:T(8,128)(2,1)S(1)}, f32[2,128,128]{2,1,0:T(8,128)}) custom-call(s32[2]{0:T(128)S(1)} %pad_add_fusion.place, bf16[512,4096]{1,0:T(8,128)(2,1)S(1)} %bitcast.5, bf16[512,4096]{1,0:T(8,128)(2,1)S(1)} %collective-permute-done.theirs, ...), custom_call_target="tpu_custom_call" | custom-call | flops 11000000 | bytes 30000 | tf_op jit(solution)/shard_map/read_values/pallas_call | solution.py:35
  26.3 0.9 %collective-permute-done.7.refs_1_ = bf16[512,256]{1,0:T(8,128)(2,1)S(1)} collective-permute-done((bf16[512,256]{1,0:T(8,128)(2,1)S(1)}, bf16[512,256]{1,0:T(8,128)(2,1)S(1)}, u32[]{:S(2)}, u32[]{:S(2)}) %collective-permute-start.7) | collective-permute-done | bytes 262176 | tf_op jit(solution)/shard_map/ppermute | solution.py:641
  27.3 4.5 %recur.1 = (bf16[1536,256]{1,0:T(8,128)(2,1)S(1)}, f32[2,128,128]{2,1,0:T(8,128)}, f32[2,128,128]{2,1,0:T(8,128)}, bf16[2,256,256]{2,1,0:T(8,128)(2,1)S(1)}, bf16[2,256,256]{2,1,0:T(8,128)(2,1)S(1)}) custom-call(s32[2]{0:T(128)S(1)} %pad_add_fusion.place, bf16[512,4096]{1,0:T(8,128)(2,1)S(1)} %bitcast.6, bf16[512,4096]{1,0:T(8,128)(2,1)S(1)} %collective-permute-done.theirs, ...), custom_call_target="tpu_custom_call" | custom-call | flops 11000000 | bytes 30000 | tf_op jit(solution)/shard_map/recur/pallas_call | solution.py:35
  31.8 1.0 %collective-permute-start.10 = (bf16[2,256,256]{2,1,0:T(8,128)(2,1)S(1)}, bf16[2,256,256]{2,1,0:T(8,128)(2,1)S(1)}, u32[]{:S(2)}, u32[]{:S(2)}) collective-permute-start(bf16[2,256,256]{2,1,0:T(8,128)(2,1)S(1)} %get-tuple-element.71), channel_id=1, source_target_pairs={{0,8},{4,12},{8,0},{12,4},{16,24},{20,28},{24,16},{28,20},{1,9},{5... | collective-permute-start | bytes 786440 | tf_op jit(solution)/shard_map/ppermute | solution.py:641
  32.7 1.5 %collective-permute-start.11 = (bf16[2,256,256]{2,1,0:T(8,128)(2,1)S(1)}, bf16[2,256,256]{2,1,0:T(8,128)(2,1)S(1)}, u32[]{:S(2)}, u32[]{:S(2)}) collective-permute-start(bf16[2,256,256]{2,1,0:T(8,128)(2,1)S(1)} %get-tuple-element.72), channel_id=1, source_target_pairs={{0,16},{4,20},{8,24},{12,28},{16,0},{20,4},{24,8},{28,12},{1,17},{... | collective-permute-start | bytes 786440 | tf_op jit(solution)/shard_map/ppermute | solution.py:641
  34.3 2.7 %near.1 = (bf16[256,512]{1,0:T(8,128)(2,1)S(1)}, bf16[256,512]{1,0:T(8,128)(2,1)S(1)}, f32[512,512]{1,0:T(8,128)S(1)}, bf16[512,512]{1,0:T(8,128)(2,1)}) custom-call(s32[2]{0:T(128)S(1)} %pad_add_fusion.place, bf16[512,4096]{1,0:T(8,128)(2,1)S(1)} %bitcast.7, bf16[512,4096]{1,0:T(8,128)(2,1)S(1)} %collective-permute-done.theirs, ...), custom_call_target="tpu_custom_call" | custom-call | flops 11000000 | bytes 30000 | tf_op jit(solution)/shard_map/near/pallas_call | solution.py:35
  36.9 1.4 %collective-permute-start.9 = (bf16[256,512]{1,0:T(8,128)(2,1)S(1)}, bf16[256,512]{1,0:T(8,128)(2,1)S(1)}, u32[]{:S(2)}, u32[]{:S(2)}) collective-permute-start(bf16[256,512]{1,0:T(8,128)(2,1)S(1)} %get-tuple-element.70.after), channel_id=1, source_target_pairs={{0,8},{4,12},{8,0},{12,4},{16,24},{20,28},{24,16},{28,20},{1,9},{5... | collective-permute-start | bytes 786440 | tf_op jit(solution)/shard_map/ppermute | solution.py:641
  38.9 1.4 %keep.1 = (f32[2,256,256]{2,1,0:T(8,128)S(1)}, f32[2,256,256]{2,1,0:T(8,128)S(1)}) custom-call(s32[2]{0:T(128)S(1)} %pad_add_fusion.place, bf16[512,4096]{1,0:T(8,128)(2,1)S(1)} %bitcast.8, bf16[512,4096]{1,0:T(8,128)(2,1)S(1)} %collective-permute-done.theirs, bf16[1536,256]{1,0:T(8,128)(2,1)S(1)} %get-tuple-element.66.grads), custom_call_target="tpu_custom_call" | custom-call | flops 11000000 | bytes 30000 | tf_op jit(solution)/shard_map/keep/pallas_call | solution.py:35
  41.0 0.6 %relay.1 = (bf16[256,256]{1,0:T(8,128)(2,1)S(1)}, bf16[256,256]{1,0:T(8,128)(2,1)S(1)}, bf16[256,256]{1,0:T(8,128)(2,1)S(1)}, bf16[256,256]{1,0:T(8,128)(2,1)S(1)}) custom-call(s32[2]{0:T(128)S(1)} %pad_add_fusion.place, bf16[2,256,256]{2,1,0:T(8,128)(2,1)S(1)} %collective-permute-done.10.far_x, bf16[2,256,256]{2,1,0:T(8,128)(2,1)S(1)} %collective-permute-done.11.far_y, ...), custom_call_target="tpu_custom_call" | custom-call | flops 11000000 | bytes 30000 | tf_op jit(solution)/shard_map/relay/pallas_call | solution.py:35
  41.7 2.1 %collective-permute-start.13 = (bf16[256,256]{1,0:T(8,128)(2,1)S(1)}, bf16[256,256]{1,0:T(8,128)(2,1)S(1)}, u32[]{:S(2)}, u32[]{:S(2)}) collective-permute-start(bf16[256,256]{1,0:T(8,128)(2,1)S(1)} %get-tuple-element.78), channel_id=1, source_target_pairs={{0,16},{4,20},{8,24},{12,28},{16,0},{20,4},{24,8},{28,12},{1,17},{... | collective-permute-start | bytes 393224 | tf_op jit(solution)/shard_map/ppermute | solution.py:641
  43.8 1.7 %collective-permute-start.14 = (bf16[256,256]{1,0:T(8,128)(2,1)S(1)}, bf16[256,256]{1,0:T(8,128)(2,1)S(1)}, u32[]{:S(2)}, u32[]{:S(2)}) collective-permute-start(bf16[256,256]{1,0:T(8,128)(2,1)S(1)} %get-tuple-element.79), channel_id=1, source_target_pairs={{0,8},{4,12},{8,0},{12,4},{16,24},{20,28},{24,16},{28,20},{1,9},{5... | collective-permute-start | bytes 393224 | tf_op jit(solution)/shard_map/ppermute | solution.py:641
  45.5 1.0 %collective-permute-done.9.near_x = bf16[256,512]{1,0:T(8,128)(2,1)S(1)} collective-permute-done((bf16[256,512]{1,0:T(8,128)(2,1)S(1)}, bf16[256,512]{1,0:T(8,128)(2,1)S(1)}, u32[]{:S(2)}, u32[]{:S(2)}) %collective-permute-start.9) | collective-permute-done | bytes 262176 | tf_op jit(solution)/shard_map/ppermute | solution.py:641
  46.5 3.5 %collective-permute-done.13.top_same = bf16[256,256]{1,0:T(8,128)(2,1)S(1)} collective-permute-done((bf16[256,256]{1,0:T(8,128)(2,1)S(1)}, bf16[256,256]{1,0:T(8,128)(2,1)S(1)}, u32[]{:S(2)}, u32[]{:S(2)}) %collective-permute-start.13) | collective-permute-done | bytes 131104 | tf_op jit(solution)/shard_map/ppermute | solution.py:641
  50.0 1.4 %collective-permute-done.15.top_cross = bf16[256,256]{1,0:T(8,128)(2,1)S(1)} collective-permute-done((bf16[256,256]{1,0:T(8,128)(2,1)S(1)}, bf16[256,256]{1,0:T(8,128)(2,1)S(1)}, u32[]{:S(2)}, u32[]{:S(2)}) %collective-permute-start.15) | collective-permute-done | bytes 131104 | tf_op jit(solution)/shard_map/ppermute | solution.py:641
  51.8 1.6 %finish.1 = f32[512,512]{1,0:T(8,128)} custom-call(s32[2]{0:T(128)S(1)} %pad_add_fusion.place, f32[512,512]{1,0:T(8,128)S(1)} %get-tuple-element.69.own, bf16[256,512]{1,0:T(8,128)(2,1)S(1)} %collective-permute-done.9.near_x, bf16[256,512]{1,0:T(8,128)(2,1)S(1)} %collective-permute-done.12.near_y, bf16[256,256]{1,0:T(8,128)(2,1)S(1)} %collective-permute-done.13.top_same, ...), custom_call_target="tpu_custom_call" | custom-call | flops 11000000 | bytes 30000 | tf_op jit(solution)/shard_map/finish/pallas_call | solution.py:600
  (22 shorter events, 4.0 us)
Async XLA Ops:
  3.0 18.5 %collective-permute-start = (bf16[512,4096]{1,0:T(8,128)(2,1)}, bf16[512,4096]{1,0:T(8,128)(2,1)S(1)}, u32[]{:S(2)}, u32[]{:S(2)}) collective-permute-start(bf16[512,4096]{1,0:T(8,128)(2,1)} %bitcast.4), channel_id=1, source_target_pairs={{0,4},{4,0},{1,5},{5,1},{2,6},{6,2},{3,7},{7,3},{8,12},{12,8},{9,1... | collective-permute-start | bytes 12582920 | tf_op jit(solution)/shard_map/ppermute | solution.py:633
  3.5 13.1 %collective-permute-start.1 = (bf16[2080,256]{1,0:T(8,128)(2,1)S(1)}, bf16[2080,256]{1,0:T(8,128)(2,1)S(1)}, u32[]{:S(2)}, u32[]{:S(2)}) collective-permute-start(bf16[2080,256]{1,0:T(8,128)(2,1)S(1)} %get-tuple-element.45), channel_id=1, source_target_pairs={{0,4},{4,0},{1,5},{5,1},{2,6},{6,2},{3,7},{7,3},{8,12},{12,8},{9,1... | collective-permute-start | bytes 3194888 | tf_op jit(solution)/shard_map/ppermute | solution.py:633
  3.6 9.5 %collective-permute-start.2 = (bf16[512,256]{1,0:T(8,128)(2,1)S(1)}, bf16[512,256]{1,0:T(8,128)(2,1)S(1)}, u32[]{:S(2)}, u32[]{:S(2)}) collective-permute-start(bf16[512,256]{1,0:T(8,128)(2,1)S(1)} %get-tuple-element.62.refs_0_), channel_id=1, source_target_pairs={{0,8},{4,12},{8,0},{12,4},{16,24},{20,28},{24,16},{28,20},{1,9},{5... | collective-permute-start | bytes 786440 | tf_op jit(solution)/shard_map/ppermute | solution.py:641
  6.5 8.5 %collective-permute-start.3 = (bf16[512,256]{1,0:T(8,128)(2,1)S(1)}, bf16[512,256]{1,0:T(8,128)(2,1)S(1)}, u32[]{:S(2)}, u32[]{:S(2)}) collective-permute-start(bf16[512,256]{1,0:T(8,128)(2,1)S(1)} %get-tuple-element.47), channel_id=1, source_target_pairs={{0,20},{4,16},{8,28},{12,24},{16,4},{20,0},{24,12},{28,8},{1,21},{... | collective-permute-start | bytes 786440 | tf_op jit(solution)/shard_map/ppermute | solution.py:641
  11.7 9.8 %copy-start = (bf16[1,512,4096]{2,1,0:T(8,128)(2,1)S(1)}, bf16[1,512,4096]{2,1,0:T(8,128)(2,1)}, u32[]{:S(2)}) copy-start(bf16[1,512,4096]{2,1,0:T(8,128)(2,1)} %param.12) | copy-start | bytes 12582916
  11.7 9.7 %collective-permute-start.5 = (bf16[512,256]{1,0:T(8,128)(2,1)S(1)}, bf16[512,256]{1,0:T(8,128)(2,1)S(1)}, u32[]{:S(2)}, u32[]{:S(2)}) collective-permute-start(bf16[512,256]{1,0:T(8,128)(2,1)S(1)} %get-tuple-element.62.refs_0_), channel_id=1, source_target_pairs={{0,16},{4,20},{8,24},{12,28},{16,0},{20,4},{24,8},{28,12},{1,17},{... | collective-permute-start | bytes 786440 | tf_op jit(solution)/shard_map/ppermute | solution.py:641
  13.0 8.4 %collective-permute-start.4 = (bf16[512,256]{1,0:T(8,128)(2,1)S(1)}, bf16[512,256]{1,0:T(8,128)(2,1)S(1)}, u32[]{:S(2)}, u32[]{:S(2)}) collective-permute-start(bf16[512,256]{1,0:T(8,128)(2,1)S(1)} %get-tuple-element.47), channel_id=1, source_target_pairs={{0,12},{4,8},{8,4},{12,0},{16,28},{20,24},{24,20},{28,16},{1,13},{... | collective-permute-start | bytes 786440 | tf_op jit(solution)/shard_map/ppermute | solution.py:641
  15.0 11.3 %collective-permute-start.6 = (bf16[512,256]{1,0:T(8,128)(2,1)S(1)}, bf16[512,256]{1,0:T(8,128)(2,1)S(1)}, u32[]{:S(2)}, u32[]{:S(2)}) collective-permute-start(bf16[512,256]{1,0:T(8,128)(2,1)S(1)} %collective-permute-done.2.refs_2_), channel_id=1, source_target_pairs={{0,16},{4,20},{8,24},{12,28},{16,0},{20,4},{24,8},{28,12},{1,17},{... | collective-permute-start | bytes 786440 | tf_op jit(solution)/shard_map/ppermute | solution.py:641
  16.6 10.6 %collective-permute-start.7 = (bf16[512,256]{1,0:T(8,128)(2,1)S(1)}, bf16[512,256]{1,0:T(8,128)(2,1)S(1)}, u32[]{:S(2)}, u32[]{:S(2)}) collective-permute-start(bf16[512,256]{1,0:T(8,128)(2,1)S(1)} %collective-permute-done.3.refs_3_), channel_id=1, source_target_pairs={{0,8},{4,12},{8,0},{12,4},{16,24},{20,28},{24,16},{28,20},{1,9},{5... | collective-permute-start | bytes 786440 | tf_op jit(solution)/shard_map/ppermute | solution.py:641
  31.8 2.5 %collective-permute-start.8 = (bf16[1536,256]{1,0:T(8,128)(2,1)S(1)}, bf16[1536,256]{1,0:T(8,128)(2,1)S(1)}, u32[]{:S(2)}, u32[]{:S(2)}) collective-permute-start(bf16[1536,256]{1,0:T(8,128)(2,1)S(1)} %get-tuple-element.66.grads), channel_id=1, source_target_pairs={{0,4},{4,0},{1,5},{5,1},{2,6},{6,2},{3,7},{7,3},{8,12},{12,8},{9,1... | collective-permute-start | bytes 2359304 | tf_op jit(solution)/shard_map/ppermute | solution.py:633
  31.8 9.1 %collective-permute-start.10 = (bf16[2,256,256]{2,1,0:T(8,128)(2,1)S(1)}, bf16[2,256,256]{2,1,0:T(8,128)(2,1)S(1)}, u32[]{:S(2)}, u32[]{:S(2)}) collective-permute-start(bf16[2,256,256]{2,1,0:T(8,128)(2,1)S(1)} %get-tuple-element.71), channel_id=1, source_target_pairs={{0,8},{4,12},{8,0},{12,4},{16,24},{20,28},{24,16},{28,20},{1,9},{5... | collective-permute-start | bytes 786440 | tf_op jit(solution)/shard_map/ppermute | solution.py:641
  32.7 8.3 %collective-permute-start.11 = (bf16[2,256,256]{2,1,0:T(8,128)(2,1)S(1)}, bf16[2,256,256]{2,1,0:T(8,128)(2,1)S(1)}, u32[]{:S(2)}, u32[]{:S(2)}) collective-permute-start(bf16[2,256,256]{2,1,0:T(8,128)(2,1)S(1)} %get-tuple-element.72), channel_id=1, source_target_pairs={{0,16},{4,20},{8,24},{12,28},{16,0},{20,4},{24,8},{28,12},{1,17},{... | collective-permute-start | bytes 786440 | tf_op jit(solution)/shard_map/ppermute | solution.py:641
  36.9 9.5 %collective-permute-start.9 = (bf16[256,512]{1,0:T(8,128)(2,1)S(1)}, bf16[256,512]{1,0:T(8,128)(2,1)S(1)}, u32[]{:S(2)}, u32[]{:S(2)}) collective-permute-start(bf16[256,512]{1,0:T(8,128)(2,1)S(1)} %get-tuple-element.70.after), channel_id=1, source_target_pairs={{0,8},{4,12},{8,0},{12,4},{16,24},{20,28},{24,16},{28,20},{1,9},{5... | collective-permute-start | bytes 786440 | tf_op jit(solution)/shard_map/ppermute | solution.py:641
  38.3 13.0 %collective-permute-start.12 = (bf16[256,512]{1,0:T(8,128)(2,1)S(1)}, bf16[256,512]{1,0:T(8,128)(2,1)S(1)}, u32[]{:S(2)}, u32[]{:S(2)}) collective-permute-start(bf16[256,512]{1,0:T(8,128)(2,1)S(1)} %get-tuple-element.77), channel_id=1, source_target_pairs={{0,16},{4,20},{8,24},{12,28},{16,0},{20,4},{24,8},{28,12},{1,17},{... | collective-permute-start | bytes 786440 | tf_op jit(solution)/shard_map/ppermute | solution.py:641
  41.7 8.3 %collective-permute-start.13 = (bf16[256,256]{1,0:T(8,128)(2,1)S(1)}, bf16[256,256]{1,0:T(8,128)(2,1)S(1)}, u32[]{:S(2)}, u32[]{:S(2)}) collective-permute-start(bf16[256,256]{1,0:T(8,128)(2,1)S(1)} %get-tuple-element.78), channel_id=1, source_target_pairs={{0,16},{4,20},{8,24},{12,28},{16,0},{20,4},{24,8},{28,12},{1,17},{... | collective-permute-start | bytes 393224 | tf_op jit(solution)/shard_map/ppermute | solution.py:641
  43.8 6.2 %collective-permute-start.14 = (bf16[256,256]{1,0:T(8,128)(2,1)S(1)}, bf16[256,256]{1,0:T(8,128)(2,1)S(1)}, u32[]{:S(2)}, u32[]{:S(2)}) collective-permute-start(bf16[256,256]{1,0:T(8,128)(2,1)S(1)} %get-tuple-element.79), channel_id=1, source_target_pairs={{0,8},{4,12},{8,0},{12,4},{16,24},{20,28},{24,16},{28,20},{1,9},{5... | collective-permute-start | bytes 393224 | tf_op jit(solution)/shard_map/ppermute | solution.py:641
  45.5 5.9 %collective-permute-start.15 = (bf16[256,256]{1,0:T(8,128)(2,1)S(1)}, bf16[256,256]{1,0:T(8,128)(2,1)S(1)}, u32[]{:S(2)}, u32[]{:S(2)}) collective-permute-start(bf16[256,256]{1,0:T(8,128)(2,1)S(1)} %get-tuple-element.80), channel_id=1, source_target_pairs={{0,20},{4,16},{8,28},{12,24},{16,4},{20,0},{24,12},{28,8},{1,21},{... | collective-permute-start | bytes 393224 | tf_op jit(solution)/shard_map/ppermute | solution.py:641
  46.5 5.3 %collective-permute-start.16 = (bf16[256,256]{1,0:T(8,128)(2,1)S(1)}, bf16[256,256]{1,0:T(8,128)(2,1)S(1)}, u32[]{:S(2)}, u32[]{:S(2)}) collective-permute-start(bf16[256,256]{1,0:T(8,128)(2,1)S(1)} %get-tuple-element.81), channel_id=1, source_target_pairs={{0,12},{4,8},{8,4},{12,0},{16,28},{20,24},{24,20},{28,16},{1,13},{... | collective-permute-start | bytes 393224 | tf_op jit(solution)/shard_map/ppermute | solution.py:641

commit v5 on v4

--- a/solution.py
+++ b/solution.py
@@ -329,6 +329,7 @@
     spans, heads = back.shape[1:3]
     core = place[0]
     values = owned(place, (own[2], stack[2 * tokens : 3 * tokens]))
+    products = product_steps(place, blocks, mine, theirs, pieces, total, None)
     zero = jnp.zeros((DK, DK), F32)
     states = [first[head] if with_state else zero for head in range(heads)]
     for half in range(2):
@@ -344,11 +345,13 @@
                 result = both[:DK] + both[DK:] + dot(left, low[half, span, head])
                 states[head] = result[:, :DK]
                 read[half, positions, columns] = result[:, DK:].T.astype(BF16)
+            next(products, None)
     for head in range(heads):
         last[head] = states[head]
+    for _ in products:
+        pass
     kept[...] = read[core]
     given[...] = read[1 - core]
-    add_products(place, blocks, mine, theirs, pieces, total, None)
 
 
 def paired(blocks):
@@ -356,6 +359,11 @@
 
 
 def add_products(place, blocks, mine, theirs, pieces, result, total):
+    for _ in product_steps(place, blocks, mine, theirs, pieces, result, total):
+        pass
+
+
+def product_steps(place, blocks, mine, theirs, pieces, result, total):
     tokens = mine.shape[0]
     rows = mine.shape[1] // 8
     core = place[0]
@@ -370,9 +378,11 @@
             product = dot(source[:, columns], jnp.concatenate(owned(place, probe[:2]), 0))
             part = product if part is None else part + product
             begin = 2
+            yield
         for block, piece in zip(blocks[begin:], probe[begin:]):
             product = dot(source[:, columns_of(place, block, rows)], piece)
             part = product if part is None else part + product
+            yield
         result[positions, :] = part.astype(result.dtype)
 
 
@@ -650,10 +660,10 @@
         theirs = swap(mine)
         x_one = send(kept, 1, 0)
         y_one = send(given, 2, 1)
-        x_two = send(given, 1, 1)
+        y_two = send(kept, 2, 0)
         maps = prepare(place, 0, tokens, width, own, (gates,))
-        late, *maps = lax.optimization_barrier((kept, *maps))
-        y_two = send(late, 2, 0)
+        late, *maps = lax.optimization_barrier((given, *maps))
+        x_two = send(late, 1, 1)
         x_one, y_one, *maps = lax.optimization_barrier((x_one, y_one, *maps))
         far_one = send(x_one, 2, 0)
         far_two = send(y_one, 1, 0)

time: 53.6 us -> 53.5 us (level)
  starting transfers between devices: 16.1 us -> 18 us
  waiting for transfers between devices: 10.4 us -> 8.92 us
    ppermute x14, starting transfers between devices: 15.5 us -> 17.4 us  [send(): return lax.ppermute(block, GROUP, pairs)]
    ppermute x14, waiting for transfers between devices: 10.4 us -> 8.91 us  [send(): return lax.ppermute(block, GROUP, pairs)]
  transfers between devices with their start and end apart: 17 -> 17, of which waited for: 10 -> 9; matrix products, arithmetic and copies ran while one was open for 0% -> 0% of each run, Pallas kernels for 33% -> 32%
where the time goes in v5:
time: 53.5 us; the launch traced here: 53.3 us
  Pallas kernels  25.6 us (48%)
  starting transfers between devices  18 us (34%)
  waiting for transfers between devices  8.92 us (17%)
  between operations  0.71 us (1%)
    pallas_call x7, Pallas kernels, kernel_call(): pl.pallas_call(kernel, grid_spec=pltpu.PrefetchScalarGridSpec(num_scalar_...  21.8 us
    ppermute x14, starting transfers between devices, send(): return lax.ppermute(block, GROUP, pairs)  17.4 us
    ppermute x14, waiting for transfers between devices, send(): return lax.ppermute(block, GROUP, pairs)  8.91 us
    pallas_call x1, Pallas kernels, pack(): pl.pallas_call(pack_kernel, grid_spec=pltpu.PrefetchScalarGridSpec(num_sc...  2.25 us
    pallas_call x1, Pallas kernels, finish(): pl.pallas_call(finish_kernel, grid_spec=pltpu.PrefetchScalarGridSpec(num_...  1.57 us
  transfers between devices with their start and end apart: 17, of which 9 were waited for; matrix products, arithmetic and copies ran while one was open for 0% of the time, Pallas kernels for 32%

profile of v5, /device:TPU:0, one launch (start us, length us, event | category | flops | bytes accessed | tf_op | source)
XLA Modules:
  0.0 53.3 jit_solution(14105621902952897214)
XLA Ops:
  0.7 2.2 %pack.1 = (bf16[512,256]{1,0:T(8,128)(2,1)S(1)}, bf16[512,256]{1,0:T(8,128)(2,1)S(1)}, bf16[3,512,256]{2,1,0:T(8,128)(2,1)S(1)}, bf16[2080,256]{1,0:T(8,128)(2,1)S(1)}, f32[2,4,512]{2,1,0:T(4,128)S(1)}) custom-call(s32[2]{0:T(128)S(1)} %pad_add_fusion.place, bf16[1,512,512]{2,1,0:T(8,128)(2,1)} %queries.1, bf16[1,512,512]{2,1,0:T(8,128)(2,1)} %keys.1, ...), custom_call_target="tpu_custom_call" | custom-call | flops 11000000 | bytes 30000 | tf_op jit(solution)/shard_map/pack/pallas_call | solution.py:149
  3.6 2.9 %collective-permute-start.2 = (bf16[512,256]{1,0:T(8,128)(2,1)S(1)}, bf16[512,256]{1,0:T(8,128)(2,1)S(1)}, u32[]{:S(2)}, u32[]{:S(2)}) collective-permute-start(bf16[512,256]{1,0:T(8,128)(2,1)S(1)} %get-tuple-element.46.refs_0_), channel_id=1, source_target_pairs={{0,8},{4,12},{8,0},{12,4},{16,24},{20,28},{24,16},{28,20},{1,9},{5... | collective-permute-start | bytes 786440 | tf_op jit(solution)/shard_map/ppermute | solution.py:651
  6.5 0.9 %collective-permute-start.3 = (bf16[512,256]{1,0:T(8,128)(2,1)S(1)}, bf16[512,256]{1,0:T(8,128)(2,1)S(1)}, u32[]{:S(2)}, u32[]{:S(2)}) collective-permute-start(bf16[512,256]{1,0:T(8,128)(2,1)S(1)} %get-tuple-element.62), channel_id=1, source_target_pairs={{0,20},{4,16},{8,28},{12,24},{16,4},{20,0},{24,12},{28,8},{1,21},{... | collective-permute-start | bytes 786440 | tf_op jit(solution)/shard_map/ppermute | solution.py:651
  7.4 4.3 %prepare.2 = (bf16[2,4,2,256,256]{4,3,2,1,0:T(8,128)(2,1)S(1)}, bf16[2,4,2,256,256]{4,3,2,1,0:T(8,128)(2,1)S(1)}, bf16[2,4,2,256,256]{4,3,2,1,0:T(8,128)(2,1)S(1)}) custom-call(s32[2]{0:T(128)S(1)} %pad_add_fusion.place, bf16[3,512,256]{2,1,0:T(8,128)(2,1)S(1)} %get-tuple-element.44.stack.own, f32[2,4,512]{2,1,0:T(4,128)S(1)} %get-tuple-element.48.refs_0_), custom_call_target="tpu_custom_call" | custom-call | flops 11000000 | bytes 30000 | tf_op jit(solution)/shard_map/prepare/pallas_call | solution.py:35
  11.7 0.9 %collective-permute-start.4 = (bf16[512,256]{1,0:T(8,128)(2,1)S(1)}, bf16[512,256]{1,0:T(8,128)(2,1)S(1)}, u32[]{:S(2)}, u32[]{:S(2)}) collective-permute-start(bf16[512,256]{1,0:T(8,128)(2,1)S(1)} %get-tuple-element.62), channel_id=1, source_target_pairs={{0,12},{4,8},{8,4},{12,0},{16,28},{20,24},{24,20},{28,16},{1,13},{... | collective-permute-start | bytes 786440 | tf_op jit(solution)/shard_map/ppermute | solution.py:651
  13.0 1.8 %collective-permute-start.5 = (bf16[512,256]{1,0:T(8,128)(2,1)S(1)}, bf16[512,256]{1,0:T(8,128)(2,1)S(1)}, u32[]{:S(2)}, u32[]{:S(2)}) collective-permute-start(bf16[512,256]{1,0:T(8,128)(2,1)S(1)} %get-tuple-element.46.refs_0_), channel_id=1, source_target_pairs={{0,16},{4,20},{8,24},{12,28},{16,0},{20,4},{24,8},{28,12},{1,17},{... | collective-permute-start | bytes 786440 | tf_op jit(solution)/shard_map/ppermute | solution.py:651
  15.0 1.6 %collective-permute-start.6 = (bf16[512,256]{1,0:T(8,128)(2,1)S(1)}, bf16[512,256]{1,0:T(8,128)(2,1)S(1)}, u32[]{:S(2)}, u32[]{:S(2)}) collective-permute-start(bf16[512,256]{1,0:T(8,128)(2,1)S(1)} %collective-permute-done.2.refs_2_), channel_id=1, source_target_pairs={{0,16},{4,20},{8,24},{12,28},{16,0},{20,4},{24,8},{28,12},{1,17},{... | collective-permute-start | bytes 786440 | tf_op jit(solution)/shard_map/ppermute | solution.py:651
  17.1 4.3 %prepare.3 = (bf16[2,4,2,256,256]{4,3,2,1,0:T(8,128)(2,1)S(1)}, bf16[2,4,2,256,256]{4,3,2,1,0:T(8,128)(2,1)S(1)}, bf16[2,4,2,256,256]{4,3,2,1,0:T(8,128)(2,1)S(1)}) custom-call(s32[2]{0:T(128)S(1)} %pad_add_fusion.place, bf16[2080,256]{1,0:T(8,128)(2,1)S(1)} %collective-permute-done.1.stack.refs_1_, ...), custom_call_target="tpu_custom_call", output_to_operand_aliasing={{0}: (2, {}), {1}: (3, {}), {2}: (4, {})} | custom-call | flops 11000000 | bytes 30000 | tf_op jit(solution)/shard_map/prepare/pallas_call | solution.py:35
  21.4 0.8 %collective-permute-done.5.refs_5_ = bf16[512,256]{1,0:T(8,128)(2,1)S(1)} collective-permute-done((bf16[512,256]{1,0:T(8,128)(2,1)S(1)}, bf16[512,256]{1,0:T(8,128)(2,1)S(1)}, u32[]{:S(2)}, u32[]{:S(2)}) %collective-permute-start.5) | collective-permute-done | bytes 262176 | tf_op jit(solution)/shard_map/ppermute | solution.py:651
  22.3 4.0 %read_values.1 = (f32[1024,256]{1,0:T(8,128)S(1)}, bf16[512,256]{1,0:T(8,128)(2,1)S(1)}, bf16[512,256]{1,0:T(8,128)(2,1)S(1)}, f32[2,128,128]{2,1,0:T(8,128)}) custom-call(s32[2]{0:T(128)S(1)} %pad_add_fusion.place, bf16[512,4096]{1,0:T(8,128)(2,1)S(1)} %bitcast.5, bf16[512,4096]{1,0:T(8,128)(2,1)S(1)} %collective-permute-done.theirs, ...), custom_call_target="tpu_custom_call" | custom-call | flops 11000000 | bytes 30000 | tf_op jit(solution)/shard_map/read_values/pallas_call | solution.py:35
  26.4 4.5 %recur.1 = (bf16[1536,256]{1,0:T(8,128)(2,1)S(1)}, f32[2,128,128]{2,1,0:T(8,128)}, f32[2,128,128]{2,1,0:T(8,128)}, bf16[2,256,256]{2,1,0:T(8,128)(2,1)S(1)}, bf16[2,256,256]{2,1,0:T(8,128)(2,1)S(1)}) custom-call(s32[2]{0:T(128)S(1)} %pad_add_fusion.place, bf16[512,4096]{1,0:T(8,128)(2,1)S(1)} %bitcast.6, bf16[512,4096]{1,0:T(8,128)(2,1)S(1)} %collective-permute-done.theirs, ...), custom_call_target="tpu_custom_call" | custom-call | flops 11000000 | bytes 30000 | tf_op jit(solution)/shard_map/recur/pallas_call | solution.py:35
  30.9 1.6 %collective-permute-start.10 = (bf16[2,256,256]{2,1,0:T(8,128)(2,1)S(1)}, bf16[2,256,256]{2,1,0:T(8,128)(2,1)S(1)}, u32[]{:S(2)}, u32[]{:S(2)}) collective-permute-start(bf16[2,256,256]{2,1,0:T(8,128)(2,1)S(1)} %get-tuple-element.71), channel_id=1, source_target_pairs={{0,8},{4,12},{8,0},{12,4},{16,24},{20,28},{24,16},{28,20},{1,9},{5... | collective-permute-start | bytes 786440 | tf_op jit(solution)/shard_map/ppermute | solution.py:651
  32.5 1.9 %collective-permute-start.11 = (bf16[2,256,256]{2,1,0:T(8,128)(2,1)S(1)}, bf16[2,256,256]{2,1,0:T(8,128)(2,1)S(1)}, u32[]{:S(2)}, u32[]{:S(2)}) collective-permute-start(bf16[2,256,256]{2,1,0:T(8,128)(2,1)S(1)} %get-tuple-element.72), channel_id=1, source_target_pairs={{0,16},{4,20},{8,24},{12,28},{16,0},{20,4},{24,8},{28,12},{1,17},{... | collective-permute-start | bytes 786440 | tf_op jit(solution)/shard_map/ppermute | solution.py:651
  34.4 2.7 %near.1 = (bf16[256,512]{1,0:T(8,128)(2,1)S(1)}, bf16[256,512]{1,0:T(8,128)(2,1)S(1)}, f32[512,512]{1,0:T(8,128)S(1)}, bf16[512,512]{1,0:T(8,128)(2,1)}) custom-call(s32[2]{0:T(128)S(1)} %pad_add_fusion.place, bf16[512,4096]{1,0:T(8,128)(2,1)S(1)} %bitcast.7, bf16[512,4096]{1,0:T(8,128)(2,1)S(1)} %collective-permute-done.theirs, ...), custom_call_target="tpu_custom_call" | custom-call | flops 11000000 | bytes 30000 | tf_op jit(solution)/shard_map/near/pallas_call | solution.py:35
  37.5 1.9 %collective-permute-start.12 = (bf16[256,512]{1,0:T(8,128)(2,1)S(1)}, bf16[256,512]{1,0:T(8,128)(2,1)S(1)}, u32[]{:S(2)}, u32[]{:S(2)}) collective-permute-start(bf16[256,512]{1,0:T(8,128)(2,1)S(1)} %get-tuple-element.77), channel_id=1, source_target_pairs={{0,16},{4,20},{8,24},{12,28},{16,0},{20,4},{24,8},{28,12},{1,17},{... | collective-permute-start | bytes 786440 | tf_op jit(solution)/shard_map/ppermute | solution.py:651
  39.4 1.4 %keep.1 = (f32[2,256,256]{2,1,0:T(8,128)S(1)}, f32[2,256,256]{2,1,0:T(8,128)S(1)}) custom-call(s32[2]{0:T(128)S(1)} %pad_add_fusion.place, bf16[512,4096]{1,0:T(8,128)(2,1)S(1)} %bitcast.8, bf16[512,4096]{1,0:T(8,128)(2,1)S(1)} %collective-permute-done.theirs, bf16[1536,256]{1,0:T(8,128)(2,1)S(1)} %get-tuple-element.66.grads), custom_call_target="tpu_custom_call" | custom-call | flops 11000000 | bytes 30000 | tf_op jit(solution)/shard_map/keep/pallas_call | solution.py:35
  40.8 0.8 %collective-permute-done.11.far_y = bf16[2,256,256]{2,1,0:T(8,128)(2,1)S(1)} collective-permute-done((bf16[2,256,256]{2,1,0:T(8,128)(2,1)S(1)}, bf16[2,256,256]{2,1,0:T(8,128)(2,1)S(1)}, u32[]{:S(2)}, u32[]{:S(2)}) %collective-permute-start.11) | collective-permute-done | bytes 262176 | tf_op jit(solution)/shard_map/ppermute | solution.py:651
  41.7 0.6 %relay.1 = (bf16[256,256]{1,0:T(8,128)(2,1)S(1)}, bf16[256,256]{1,0:T(8,128)(2,1)S(1)}, bf16[256,256]{1,0:T(8,128)(2,1)S(1)}, bf16[256,256]{1,0:T(8,128)(2,1)S(1)}) custom-call(s32[2]{0:T(128)S(1)} %pad_add_fusion.place, bf16[2,256,256]{2,1,0:T(8,128)(2,1)S(1)} %collective-permute-done.10.far_x, bf16[2,256,256]{2,1,0:T(8,128)(2,1)S(1)} %collective-permute-done.11.far_y, ...), custom_call_target="tpu_custom_call" | custom-call | flops 11000000 | bytes 30000 | tf_op jit(solution)/shard_map/relay/pallas_call | solution.py:35
  42.3 2.0 %collective-permute-start.13 = (bf16[256,256]{1,0:T(8,128)(2,1)S(1)}, bf16[256,256]{1,0:T(8,128)(2,1)S(1)}, u32[]{:S(2)}, u32[]{:S(2)}) collective-permute-start(bf16[256,256]{1,0:T(8,128)(2,1)S(1)} %get-tuple-element.78), channel_id=1, source_target_pairs={{0,16},{4,20},{8,24},{12,28},{16,0},{20,4},{24,8},{28,12},{1,17},{... | collective-permute-start | bytes 393224 | tf_op jit(solution)/shard_map/ppermute | solution.py:651
  44.4 0.9 %collective-permute-done.9.near_x = bf16[256,512]{1,0:T(8,128)(2,1)S(1)} collective-permute-done((bf16[256,512]{1,0:T(8,128)(2,1)S(1)}, bf16[256,512]{1,0:T(8,128)(2,1)S(1)}, u32[]{:S(2)}, u32[]{:S(2)}) %collective-permute-start.9) | collective-permute-done | bytes 262176 | tf_op jit(solution)/shard_map/ppermute | solution.py:651
  45.3 0.9 %collective-permute-start.16 = (bf16[256,256]{1,0:T(8,128)(2,1)S(1)}, bf16[256,256]{1,0:T(8,128)(2,1)S(1)}, u32[]{:S(2)}, u32[]{:S(2)}) collective-permute-start(bf16[256,256]{1,0:T(8,128)(2,1)S(1)} %get-tuple-element.81), channel_id=1, source_target_pairs={{0,12},{4,8},{8,4},{12,0},{16,28},{20,24},{24,20},{28,16},{1,13},{... | collective-permute-start | bytes 393224 | tf_op jit(solution)/shard_map/ppermute | solution.py:651
  46.2 3.9 %collective-permute-done.13.top_same = bf16[256,256]{1,0:T(8,128)(2,1)S(1)} collective-permute-done((bf16[256,256]{1,0:T(8,128)(2,1)S(1)}, bf16[256,256]{1,0:T(8,128)(2,1)S(1)}, u32[]{:S(2)}, u32[]{:S(2)}) %collective-permute-start.13) | collective-permute-done | bytes 131104 | tf_op jit(solution)/shard_map/ppermute | solution.py:651
  50.3 1.5 %collective-permute-done.15.top_cross = bf16[256,256]{1,0:T(8,128)(2,1)S(1)} collective-permute-done((bf16[256,256]{1,0:T(8,128)(2,1)S(1)}, bf16[256,256]{1,0:T(8,128)(2,1)S(1)}, u32[]{:S(2)}, u32[]{:S(2)}) %collective-permute-start.15) | collective-permute-done | bytes 131104 | tf_op jit(solution)/shard_map/ppermute | solution.py:651
  51.8 1.6 %finish.1 = f32[512,512]{1,0:T(8,128)} custom-call(s32[2]{0:T(128)S(1)} %pad_add_fusion.place, f32[512,512]{1,0:T(8,128)S(1)} %get-tuple-element.69.own, bf16[256,512]{1,0:T(8,128)(2,1)S(1)} %collective-permute-done.9.near_x, bf16[256,512]{1,0:T(8,128)(2,1)S(1)} %collective-permute-done.12.near_y, bf16[256,256]{1,0:T(8,128)(2,1)S(1)} %collective-permute-done.13.top_same, ...), custom_call_target="tpu_custom_call" | custom-call | flops 11000000 | bytes 30000 | tf_op jit(solution)/shard_map/finish/pallas_call | solution.py:610
  (22 shorter events, 2.8 us)
Async XLA Ops:
  3.0 19.3 %collective-permute-start = (bf16[512,4096]{1,0:T(8,128)(2,1)}, bf16[512,4096]{1,0:T(8,128)(2,1)S(1)}, u32[]{:S(2)}, u32[]{:S(2)}) collective-permute-start(bf16[512,4096]{1,0:T(8,128)(2,1)} %bitcast.4), channel_id=1, source_target_pairs={{0,4},{4,0},{1,5},{5,1},{2,6},{6,2},{3,7},{7,3},{8,12},{12,8},{9,1... | collective-permute-start | bytes 12582920 | tf_op jit(solution)/shard_map/ppermute | solution.py:643
  3.5 13.1 %collective-permute-start.1 = (bf16[2080,256]{1,0:T(8,128)(2,1)S(1)}, bf16[2080,256]{1,0:T(8,128)(2,1)S(1)}, u32[]{:S(2)}, u32[]{:S(2)}) collective-permute-start(bf16[2080,256]{1,0:T(8,128)(2,1)S(1)} %get-tuple-element.45), channel_id=1, source_target_pairs={{0,4},{4,0},{1,5},{5,1},{2,6},{6,2},{3,7},{7,3},{8,12},{12,8},{9,1... | collective-permute-start | bytes 3194888 | tf_op jit(solution)/shard_map/ppermute | solution.py:643
  3.6 9.5 %collective-permute-start.2 = (bf16[512,256]{1,0:T(8,128)(2,1)S(1)}, bf16[512,256]{1,0:T(8,128)(2,1)S(1)}, u32[]{:S(2)}, u32[]{:S(2)}) collective-permute-start(bf16[512,256]{1,0:T(8,128)(2,1)S(1)} %get-tuple-element.46.refs_0_), channel_id=1, source_target_pairs={{0,8},{4,12},{8,0},{12,4},{16,24},{20,28},{24,16},{28,20},{1,9},{5... | collective-permute-start | bytes 786440 | tf_op jit(solution)/shard_map/ppermute | solution.py:651
  6.5 8.5 %collective-permute-start.3 = (bf16[512,256]{1,0:T(8,128)(2,1)S(1)}, bf16[512,256]{1,0:T(8,128)(2,1)S(1)}, u32[]{:S(2)}, u32[]{:S(2)}) collective-permute-start(bf16[512,256]{1,0:T(8,128)(2,1)S(1)} %get-tuple-element.62), channel_id=1, source_target_pairs={{0,20},{4,16},{8,28},{12,24},{16,4},{20,0},{24,12},{28,8},{1,21},{... | collective-permute-start | bytes 786440 | tf_op jit(solution)/shard_map/ppermute | solution.py:651
  11.7 10.6 %copy-start = (bf16[1,512,4096]{2,1,0:T(8,128)(2,1)S(1)}, bf16[1,512,4096]{2,1,0:T(8,128)(2,1)}, u32[]{:S(2)}) copy-start(bf16[1,512,4096]{2,1,0:T(8,128)(2,1)} %param.12) | copy-start | bytes 12582916
  11.7 9.7 %collective-permute-start.4 = (bf16[512,256]{1,0:T(8,128)(2,1)S(1)}, bf16[512,256]{1,0:T(8,128)(2,1)S(1)}, u32[]{:S(2)}, u32[]{:S(2)}) collective-permute-start(bf16[512,256]{1,0:T(8,128)(2,1)S(1)} %get-tuple-element.62), channel_id=1, source_target_pairs={{0,12},{4,8},{8,4},{12,0},{16,28},{20,24},{24,20},{28,16},{1,13},{... | collective-permute-start | bytes 786440 | tf_op jit(solution)/shard_map/ppermute | solution.py:651
  13.0 9.2 %collective-permute-start.5 = (bf16[512,256]{1,0:T(8,128)(2,1)S(1)}, bf16[512,256]{1,0:T(8,128)(2,1)S(1)}, u32[]{:S(2)}, u32[]{:S(2)}) collective-permute-start(bf16[512,256]{1,0:T(8,128)(2,1)S(1)} %get-tuple-element.46.refs_0_), channel_id=1, source_target_pairs={{0,16},{4,20},{8,24},{12,28},{16,0},{20,4},{24,8},{28,12},{1,17},{... | collective-permute-start | bytes 786440 | tf_op jit(solution)/shard_map/ppermute | solution.py:651
  15.0 11.4 %collective-permute-start.6 = (bf16[512,256]{1,0:T(8,128)(2,1)S(1)}, bf16[512,256]{1,0:T(8,128)(2,1)S(1)}, u32[]{:S(2)}, u32[]{:S(2)}) collective-permute-start(bf16[512,256]{1,0:T(8,128)(2,1)S(1)} %collective-permute-done.2.refs_2_), channel_id=1, source_target_pairs={{0,16},{4,20},{8,24},{12,28},{16,0},{20,4},{24,8},{28,12},{1,17},{... | collective-permute-start | bytes 786440 | tf_op jit(solution)/shard_map/ppermute | solution.py:651
  16.6 9.8 %collective-permute-start.7 = (bf16[512,256]{1,0:T(8,128)(2,1)S(1)}, bf16[512,256]{1,0:T(8,128)(2,1)S(1)}, u32[]{:S(2)}, u32[]{:S(2)}) collective-permute-start(bf16[512,256]{1,0:T(8,128)(2,1)S(1)} %collective-permute-done.3.refs_3_), channel_id=1, source_target_pairs={{0,8},{4,12},{8,0},{12,4},{16,24},{20,28},{24,16},{28,20},{1,9},{5... | collective-permute-start | bytes 786440 | tf_op jit(solution)/shard_map/ppermute | solution.py:651
  30.9 3.5 %collective-permute-start.8 = (bf16[1536,256]{1,0:T(8,128)(2,1)S(1)}, bf16[1536,256]{1,0:T(8,128)(2,1)S(1)}, u32[]{:S(2)}, u32[]{:S(2)}) collective-permute-start(bf16[1536,256]{1,0:T(8,128)(2,1)S(1)} %get-tuple-element.66.grads), channel_id=1, source_target_pairs={{0,4},{4,0},{1,5},{5,1},{2,6},{6,2},{3,7},{7,3},{8,12},{12,8},{9,1... | collective-permute-start | bytes 2359304 | tf_op jit(solution)/shard_map/ppermute | solution.py:643
  30.9 9.9 %collective-permute-start.10 = (bf16[2,256,256]{2,1,0:T(8,128)(2,1)S(1)}, bf16[2,256,256]{2,1,0:T(8,128)(2,1)S(1)}, u32[]{:S(2)}, u32[]{:S(2)}) collective-permute-start(bf16[2,256,256]{2,1,0:T(8,128)(2,1)S(1)} %get-tuple-element.71), channel_id=1, source_target_pairs={{0,8},{4,12},{8,0},{12,4},{16,24},{20,28},{24,16},{28,20},{1,9},{5... | collective-permute-start | bytes 786440 | tf_op jit(solution)/shard_map/ppermute | solution.py:651
  32.5 9.1 %collective-permute-start.11 = (bf16[2,256,256]{2,1,0:T(8,128)(2,1)S(1)}, bf16[2,256,256]{2,1,0:T(8,128)(2,1)S(1)}, u32[]{:S(2)}, u32[]{:S(2)}) collective-permute-start(bf16[2,256,256]{2,1,0:T(8,128)(2,1)S(1)} %get-tuple-element.72), channel_id=1, source_target_pairs={{0,16},{4,20},{8,24},{12,28},{16,0},{20,4},{24,8},{28,12},{1,17},{... | collective-permute-start | bytes 786440 | tf_op jit(solution)/shard_map/ppermute | solution.py:651
  37.1 8.2 %collective-permute-start.9 = (bf16[256,512]{1,0:T(8,128)(2,1)S(1)}, bf16[256,512]{1,0:T(8,128)(2,1)S(1)}, u32[]{:S(2)}, u32[]{:S(2)}) collective-permute-start(bf16[256,512]{1,0:T(8,128)(2,1)S(1)} %get-tuple-element.70.after), channel_id=1, source_target_pairs={{0,8},{4,12},{8,0},{12,4},{16,24},{20,28},{24,16},{28,20},{1,9},{5... | collective-permute-start | bytes 786440 | tf_op jit(solution)/shard_map/ppermute | solution.py:651
  37.5 14.3 %collective-permute-start.12 = (bf16[256,512]{1,0:T(8,128)(2,1)S(1)}, bf16[256,512]{1,0:T(8,128)(2,1)S(1)}, u32[]{:S(2)}, u32[]{:S(2)}) collective-permute-start(bf16[256,512]{1,0:T(8,128)(2,1)S(1)} %get-tuple-element.77), channel_id=1, source_target_pairs={{0,16},{4,20},{8,24},{12,28},{16,0},{20,4},{24,8},{28,12},{1,17},{... | collective-permute-start | bytes 786440 | tf_op jit(solution)/shard_map/ppermute | solution.py:651
  42.3 7.8 %collective-permute-start.13 = (bf16[256,256]{1,0:T(8,128)(2,1)S(1)}, bf16[256,256]{1,0:T(8,128)(2,1)S(1)}, u32[]{:S(2)}, u32[]{:S(2)}) collective-permute-start(bf16[256,256]{1,0:T(8,128)(2,1)S(1)} %get-tuple-element.78), channel_id=1, source_target_pairs={{0,16},{4,20},{8,24},{12,28},{16,0},{20,4},{24,8},{28,12},{1,17},{... | collective-permute-start | bytes 393224 | tf_op jit(solution)/shard_map/ppermute | solution.py:651
  44.2 6.0 %collective-permute-start.14 = (bf16[256,256]{1,0:T(8,128)(2,1)S(1)}, bf16[256,256]{1,0:T(8,128)(2,1)S(1)}, u32[]{:S(2)}, u32[]{:S(2)}) collective-permute-start(bf16[256,256]{1,0:T(8,128)(2,1)S(1)} %get-tuple-element.79), channel_id=1, source_target_pairs={{0,8},{4,12},{8,0},{12,4},{16,24},{20,28},{24,16},{28,20},{1,9},{5... | collective-permute-start | bytes 393224 | tf_op jit(solution)/shard_map/ppermute | solution.py:651
  44.4 7.3 %collective-permute-start.15 = (bf16[256,256]{1,0:T(8,128)(2,1)S(1)}, bf16[256,256]{1,0:T(8,128)(2,1)S(1)}, u32[]{:S(2)}, u32[]{:S(2)}) collective-permute-start(bf16[256,256]{1,0:T(8,128)(2,1)S(1)} %get-tuple-element.80), channel_id=1, source_target_pairs={{0,20},{4,16},{8,28},{12,24},{16,4},{20,0},{24,12},{28,8},{1,21},{... | collective-permute-start | bytes 393224 | tf_op jit(solution)/shard_map/ppermute | solution.py:651
  45.3 6.5 %collective-permute-start.16 = (bf16[256,256]{1,0:T(8,128)(2,1)S(1)}, bf16[256,256]{1,0:T(8,128)(2,1)S(1)}, u32[]{:S(2)}, u32[]{:S(2)}) collective-permute-start(bf16[256,256]{1,0:T(8,128)(2,1)S(1)} %get-tuple-element.81), channel_id=1, source_target_pairs={{0,12},{4,8},{8,4},{12,0},{16,28},{20,24},{24,20},{28,16},{1,13},{... | collective-permute-start | bytes 393224 | tf_op jit(solution)/shard_map/ppermute | solution.py:651

commit v6 on v5

--- a/solution.py
+++ b/solution.py
@@ -660,10 +660,10 @@
         theirs = swap(mine)
         x_one = send(kept, 1, 0)
         y_one = send(given, 2, 1)
-        y_two = send(kept, 2, 0)
+        x_two = send(given, 1, 1)
         maps = prepare(place, 0, tokens, width, own, (gates,))
-        late, *maps = lax.optimization_barrier((given, *maps))
-        x_two = send(late, 1, 1)
+        late, *maps = lax.optimization_barrier((kept, *maps))
+        y_two = send(late, 2, 0)
         x_one, y_one, *maps = lax.optimization_barrier((x_one, y_one, *maps))
         far_one = send(x_one, 2, 0)
         far_two = send(y_one, 1, 0)

time: 53.5 us -> 53.6 us (level)
  waiting for transfers between devices: 8.92 us -> 10.9 us
  starting transfers between devices: 18 us -> 16.1 us
    ppermute x14, waiting for transfers between devices: 8.91 us -> 10.9 us  [send(): return lax.ppermute(block, GROUP, pairs)]
    ppermute x14, starting transfers between devices: 17.4 us -> 15.5 us  [send(): return lax.ppermute(block, GROUP, pairs)]
  transfers between devices with their start and end apart: 17 -> 17, of which waited for: 9 -> 10; matrix products, arithmetic and copies ran while one was open for 0% -> 0% of each run, Pallas kernels for 32% -> 32%
where the time goes in v6:
time: 53.6 us; the launch traced here: 53.4 us
  Pallas kernels  25.6 us (48%)
  starting transfers between devices  16.1 us (30%)
  waiting for transfers between devices  10.9 us (20%)
  between operations  0.73 us (1%)
    pallas_call x7, Pallas kernels, kernel_call(): pl.pallas_call(kernel, grid_spec=pltpu.PrefetchScalarGridSpec(num_scalar_...  21.8 us
    ppermute x14, starting transfers between devices, send(): return lax.ppermute(block, GROUP, pairs)  15.5 us
    ppermute x14, waiting for transfers between devices, send(): return lax.ppermute(block, GROUP, pairs)  10.9 us
    pallas_call x1, Pallas kernels, pack(): pl.pallas_call(pack_kernel, grid_spec=pltpu.PrefetchScalarGridSpec(num_sc...  2.25 us
    pallas_call x1, Pallas kernels, finish(): pl.pallas_call(finish_kernel, grid_spec=pltpu.PrefetchScalarGridSpec(num_...  1.57 us
  transfers between devices with their start and end apart: 17, of which 10 were waited for; matrix products, arithmetic and copies ran while one was open for 0% of the time, Pallas kernels for 32%

profile of v6, /device:TPU:0, one launch (start us, length us, event | category | flops | bytes accessed | tf_op | source)
XLA Modules:
  0.0 53.4 jit_solution(5270925198609679072)
XLA Ops:
  0.7 2.2 %pack.1 = (bf16[512,256]{1,0:T(8,128)(2,1)S(1)}, bf16[512,256]{1,0:T(8,128)(2,1)S(1)}, bf16[3,512,256]{2,1,0:T(8,128)(2,1)S(1)}, bf16[2080,256]{1,0:T(8,128)(2,1)S(1)}, f32[2,4,512]{2,1,0:T(4,128)S(1)}) custom-call(s32[2]{0:T(128)S(1)} %pad_add_fusion.place, bf16[1,512,512]{2,1,0:T(8,128)(2,1)} %queries.1, bf16[1,512,512]{2,1,0:T(8,128)(2,1)} %keys.1, ...), custom_call_target="tpu_custom_call" | custom-call | flops 11000000 | bytes 30000 | tf_op jit(solution)/shard_map/pack/pallas_call | solution.py:149
  3.6 2.9 %collective-permute-start.2 = (bf16[512,256]{1,0:T(8,128)(2,1)S(1)}, bf16[512,256]{1,0:T(8,128)(2,1)S(1)}, u32[]{:S(2)}, u32[]{:S(2)}) collective-permute-start(bf16[512,256]{1,0:T(8,128)(2,1)S(1)} %get-tuple-element.62.refs_0_), channel_id=1, source_target_pairs={{0,8},{4,12},{8,0},{12,4},{16,24},{20,28},{24,16},{28,20},{1,9},{5... | collective-permute-start | bytes 786440 | tf_op jit(solution)/shard_map/ppermute | solution.py:651
  6.5 0.9 %collective-permute-start.3 = (bf16[512,256]{1,0:T(8,128)(2,1)S(1)}, bf16[512,256]{1,0:T(8,128)(2,1)S(1)}, u32[]{:S(2)}, u32[]{:S(2)}) collective-permute-start(bf16[512,256]{1,0:T(8,128)(2,1)S(1)} %get-tuple-element.47), channel_id=1, source_target_pairs={{0,20},{4,16},{8,28},{12,24},{16,4},{20,0},{24,12},{28,8},{1,21},{... | collective-permute-start | bytes 786440 | tf_op jit(solution)/shard_map/ppermute | solution.py:651
  7.4 4.3 %prepare.2 = (bf16[2,4,2,256,256]{4,3,2,1,0:T(8,128)(2,1)S(1)}, bf16[2,4,2,256,256]{4,3,2,1,0:T(8,128)(2,1)S(1)}, bf16[2,4,2,256,256]{4,3,2,1,0:T(8,128)(2,1)S(1)}) custom-call(s32[2]{0:T(128)S(1)} %pad_add_fusion.place, bf16[3,512,256]{2,1,0:T(8,128)(2,1)S(1)} %get-tuple-element.44.stack.own, f32[2,4,512]{2,1,0:T(4,128)S(1)} %get-tuple-element.48.refs_0_), custom_call_target="tpu_custom_call" | custom-call | flops 11000000 | bytes 30000 | tf_op jit(solution)/shard_map/prepare/pallas_call | solution.py:35
  11.7 0.7 %collective-permute-start.5 = (bf16[512,256]{1,0:T(8,128)(2,1)S(1)}, bf16[512,256]{1,0:T(8,128)(2,1)S(1)}, u32[]{:S(2)}, u32[]{:S(2)}) collective-permute-start(bf16[512,256]{1,0:T(8,128)(2,1)S(1)} %get-tuple-element.62.refs_0_), channel_id=1, source_target_pairs={{0,16},{4,20},{8,24},{12,28},{16,0},{20,4},{24,8},{28,12},{1,17},{... | collective-permute-start | bytes 786440 | tf_op jit(solution)/shard_map/ppermute | solution.py:651
  12.4 0.7 %collective-permute-done.2.refs_2_ = bf16[512,256]{1,0:T(8,128)(2,1)S(1)} collective-permute-done((bf16[512,256]{1,0:T(8,128)(2,1)S(1)}, bf16[512,256]{1,0:T(8,128)(2,1)S(1)}, u32[]{:S(2)}, u32[]{:S(2)}) %collective-permute-start.2) | collective-permute-done | bytes 262176 | tf_op jit(solution)/shard_map/ppermute | solution.py:651
  13.6 1.4 %collective-permute-done.3.refs_3_ = bf16[512,256]{1,0:T(8,128)(2,1)S(1)} collective-permute-done((bf16[512,256]{1,0:T(8,128)(2,1)S(1)}, bf16[512,256]{1,0:T(8,128)(2,1)S(1)}, u32[]{:S(2)}, u32[]{:S(2)}) %collective-permute-start.3) | collective-permute-done | bytes 262176 | tf_op jit(solution)/shard_map/ppermute | solution.py:651
  15.0 1.6 %collective-permute-start.6 = (bf16[512,256]{1,0:T(8,128)(2,1)S(1)}, bf16[512,256]{1,0:T(8,128)(2,1)S(1)}, u32[]{:S(2)}, u32[]{:S(2)}) collective-permute-start(bf16[512,256]{1,0:T(8,128)(2,1)S(1)} %collective-permute-done.2.refs_2_), channel_id=1, source_target_pairs={{0,16},{4,20},{8,24},{12,28},{16,0},{20,4},{24,8},{28,12},{1,17},{... | collective-permute-start | bytes 786440 | tf_op jit(solution)/shard_map/ppermute | solution.py:651
  17.1 4.3 %prepare.3 = (bf16[2,4,2,256,256]{4,3,2,1,0:T(8,128)(2,1)S(1)}, bf16[2,4,2,256,256]{4,3,2,1,0:T(8,128)(2,1)S(1)}, bf16[2,4,2,256,256]{4,3,2,1,0:T(8,128)(2,1)S(1)}) custom-call(s32[2]{0:T(128)S(1)} %pad_add_fusion.place, bf16[2080,256]{1,0:T(8,128)(2,1)S(1)} %collective-permute-done.1.stack.refs_1_, ...), custom_call_target="tpu_custom_call", output_to_operand_aliasing={{0}: (2, {}), {1}: (3, {}), {2}: (4, {})} | custom-call | flops 11000000 | bytes 30000 | tf_op jit(solution)/shard_map/prepare/pallas_call | solution.py:35
  21.5 4.0 %read_values.1 = (f32[1024,256]{1,0:T(8,128)S(1)}, bf16[512,256]{1,0:T(8,128)(2,1)S(1)}, bf16[512,256]{1,0:T(8,128)(2,1)S(1)}, f32[2,128,128]{2,1,0:T(8,128)}) custom-call(s32[2]{0:T(128)S(1)} %pad_add_fusion.place, bf16[512,4096]{1,0:T(8,128)(2,1)S(1)} %bitcast.5, bf16[512,4096]{1,0:T(8,128)(2,1)S(1)} %collective-permute-done.theirs, ...), custom_call_target="tpu_custom_call" | custom-call | flops 11000000 | bytes 30000 | tf_op jit(solution)/shard_map/read_values/pallas_call | solution.py:35
  25.5 0.8 %collective-permute-done.6.refs_0_ = bf16[512,256]{1,0:T(8,128)(2,1)S(1)} collective-permute-done((bf16[512,256]{1,0:T(8,128)(2,1)S(1)}, bf16[512,256]{1,0:T(8,128)(2,1)S(1)}, u32[]{:S(2)}, u32[]{:S(2)}) %collective-permute-start.6) | collective-permute-done | bytes 262176 | tf_op jit(solution)/shard_map/ppermute | solution.py:651
  26.3 0.9 %collective-permute-done.7.refs_1_ = bf16[512,256]{1,0:T(8,128)(2,1)S(1)} collective-permute-done((bf16[512,256]{1,0:T(8,128)(2,1)S(1)}, bf16[512,256]{1,0:T(8,128)(2,1)S(1)}, u32[]{:S(2)}, u32[]{:S(2)}) %collective-permute-start.7) | collective-permute-done | bytes 262176 | tf_op jit(solution)/shard_map/ppermute | solution.py:651
  27.3 4.5 %recur.1 = (bf16[1536,256]{1,0:T(8,128)(2,1)S(1)}, f32[2,128,128]{2,1,0:T(8,128)}, f32[2,128,128]{2,1,0:T(8,128)}, bf16[2,256,256]{2,1,0:T(8,128)(2,1)S(1)}, bf16[2,256,256]{2,1,0:T(8,128)(2,1)S(1)}) custom-call(s32[2]{0:T(128)S(1)} %pad_add_fusion.place, bf16[512,4096]{1,0:T(8,128)(2,1)S(1)} %bitcast.6, bf16[512,4096]{1,0:T(8,128)(2,1)S(1)} %collective-permute-done.theirs, ...), custom_call_target="tpu_custom_call" | custom-call | flops 11000000 | bytes 30000 | tf_op jit(solution)/shard_map/recur/pallas_call | solution.py:35
  31.8 1.0 %collective-permute-start.10 = (bf16[2,256,256]{2,1,0:T(8,128)(2,1)S(1)}, bf16[2,256,256]{2,1,0:T(8,128)(2,1)S(1)}, u32[]{:S(2)}, u32[]{:S(2)}) collective-permute-start(bf16[2,256,256]{2,1,0:T(8,128)(2,1)S(1)} %get-tuple-element.71), channel_id=1, source_target_pairs={{0,8},{4,12},{8,0},{12,4},{16,24},{20,28},{24,16},{28,20},{1,9},{5... | collective-permute-start | bytes 786440 | tf_op jit(solution)/shard_map/ppermute | solution.py:651
  32.7 1.5 %collective-permute-start.11 = (bf16[2,256,256]{2,1,0:T(8,128)(2,1)S(1)}, bf16[2,256,256]{2,1,0:T(8,128)(2,1)S(1)}, u32[]{:S(2)}, u32[]{:S(2)}) collective-permute-start(bf16[2,256,256]{2,1,0:T(8,128)(2,1)S(1)} %get-tuple-element.72), channel_id=1, source_target_pairs={{0,16},{4,20},{8,24},{12,28},{16,0},{20,4},{24,8},{28,12},{1,17},{... | collective-permute-start | bytes 786440 | tf_op jit(solution)/shard_map/ppermute | solution.py:651
  34.3 2.7 %near.1 = (bf16[256,512]{1,0:T(8,128)(2,1)S(1)}, bf16[256,512]{1,0:T(8,128)(2,1)S(1)}, f32[512,512]{1,0:T(8,128)S(1)}, bf16[512,512]{1,0:T(8,128)(2,1)}) custom-call(s32[2]{0:T(128)S(1)} %pad_add_fusion.place, bf16[512,4096]{1,0:T(8,128)(2,1)S(1)} %bitcast.7, bf16[512,4096]{1,0:T(8,128)(2,1)S(1)} %collective-permute-done.theirs, ...), custom_call_target="tpu_custom_call" | custom-call | flops 11000000 | bytes 30000 | tf_op jit(solution)/shard_map/near/pallas_call | solution.py:35
  36.9 1.4 %collective-permute-start.9 = (bf16[256,512]{1,0:T(8,128)(2,1)S(1)}, bf16[256,512]{1,0:T(8,128)(2,1)S(1)}, u32[]{:S(2)}, u32[]{:S(2)}) collective-permute-start(bf16[256,512]{1,0:T(8,128)(2,1)S(1)} %get-tuple-element.70.after), channel_id=1, source_target_pairs={{0,8},{4,12},{8,0},{12,4},{16,24},{20,28},{24,16},{28,20},{1,9},{5... | collective-permute-start | bytes 786440 | tf_op jit(solution)/shard_map/ppermute | solution.py:651
  38.9 1.4 %keep.1 = (f32[2,256,256]{2,1,0:T(8,128)S(1)}, f32[2,256,256]{2,1,0:T(8,128)S(1)}) custom-call(s32[2]{0:T(128)S(1)} %pad_add_fusion.place, bf16[512,4096]{1,0:T(8,128)(2,1)S(1)} %bitcast.8, bf16[512,4096]{1,0:T(8,128)(2,1)S(1)} %collective-permute-done.theirs, bf16[1536,256]{1,0:T(8,128)(2,1)S(1)} %get-tuple-element.66.grads), custom_call_target="tpu_custom_call" | custom-call | flops 11000000 | bytes 30000 | tf_op jit(solution)/shard_map/keep/pallas_call | solution.py:35
  41.7 2.1 %collective-permute-start.13 = (bf16[256,256]{1,0:T(8,128)(2,1)S(1)}, bf16[256,256]{1,0:T(8,128)(2,1)S(1)}, u32[]{:S(2)}, u32[]{:S(2)}) collective-permute-start(bf16[256,256]{1,0:T(8,128)(2,1)S(1)} %get-tuple-element.78), channel_id=1, source_target_pairs={{0,16},{4,20},{8,24},{12,28},{16,0},{20,4},{24,8},{28,12},{1,17},{... | collective-permute-start | bytes 393224 | tf_op jit(solution)/shard_map/ppermute | solution.py:651
  43.8 1.7 %collective-permute-start.14 = (bf16[256,256]{1,0:T(8,128)(2,1)S(1)}, bf16[256,256]{1,0:T(8,128)(2,1)S(1)}, u32[]{:S(2)}, u32[]{:S(2)}) collective-permute-start(bf16[256,256]{1,0:T(8,128)(2,1)S(1)} %get-tuple-element.79), channel_id=1, source_target_pairs={{0,8},{4,12},{8,0},{12,4},{16,24},{20,28},{24,16},{28,20},{1,9},{5... | collective-permute-start | bytes 393224 | tf_op jit(solution)/shard_map/ppermute | solution.py:651
  45.5 1.0 %collective-permute-done.9.near_x = bf16[256,512]{1,0:T(8,128)(2,1)S(1)} collective-permute-done((bf16[256,512]{1,0:T(8,128)(2,1)S(1)}, bf16[256,512]{1,0:T(8,128)(2,1)S(1)}, u32[]{:S(2)}, u32[]{:S(2)}) %collective-permute-start.9) | collective-permute-done | bytes 262176 | tf_op jit(solution)/shard_map/ppermute | solution.py:651
  46.5 3.5 %collective-permute-done.13.top_same = bf16[256,256]{1,0:T(8,128)(2,1)S(1)} collective-permute-done((bf16[256,256]{1,0:T(8,128)(2,1)S(1)}, bf16[256,256]{1,0:T(8,128)(2,1)S(1)}, u32[]{:S(2)}, u32[]{:S(2)}) %collective-permute-start.13) | collective-permute-done | bytes 131104 | tf_op jit(solution)/shard_map/ppermute | solution.py:651
  50.0 1.4 %collective-permute-done.15.top_cross = bf16[256,256]{1,0:T(8,128)(2,1)S(1)} collective-permute-done((bf16[256,256]{1,0:T(8,128)(2,1)S(1)}, bf16[256,256]{1,0:T(8,128)(2,1)S(1)}, u32[]{:S(2)}, u32[]{:S(2)}) %collective-permute-start.15) | collective-permute-done | bytes 131104 | tf_op jit(solution)/shard_map/ppermute | solution.py:651
  51.8 1.6 %finish.1 = f32[512,512]{1,0:T(8,128)} custom-call(s32[2]{0:T(128)S(1)} %pad_add_fusion.place, f32[512,512]{1,0:T(8,128)S(1)} %get-tuple-element.69.own, bf16[256,512]{1,0:T(8,128)(2,1)S(1)} %collective-permute-done.9.near_x, bf16[256,512]{1,0:T(8,128)(2,1)S(1)} %collective-permute-done.12.near_y, bf16[256,256]{1,0:T(8,128)(2,1)S(1)} %collective-permute-done.13.top_same, ...), custom_call_target="tpu_custom_call" | custom-call | flops 11000000 | bytes 30000 | tf_op jit(solution)/shard_map/finish/pallas_call | solution.py:610
  (22 shorter events, 4.2 us)
Async XLA Ops:
  3.0 18.5 %collective-permute-start = (bf16[512,4096]{1,0:T(8,128)(2,1)}, bf16[512,4096]{1,0:T(8,128)(2,1)S(1)}, u32[]{:S(2)}, u32[]{:S(2)}) collective-permute-start(bf16[512,4096]{1,0:T(8,128)(2,1)} %bitcast.4), channel_id=1, source_target_pairs={{0,4},{4,0},{1,5},{5,1},{2,6},{6,2},{3,7},{7,3},{8,12},{12,8},{9,1... | collective-permute-start | bytes 12582920 | tf_op jit(solution)/shard_map/ppermute | solution.py:643
  3.5 13.1 %collective-permute-start.1 = (bf16[2080,256]{1,0:T(8,128)(2,1)S(1)}, bf16[2080,256]{1,0:T(8,128)(2,1)S(1)}, u32[]{:S(2)}, u32[]{:S(2)}) collective-permute-start(bf16[2080,256]{1,0:T(8,128)(2,1)S(1)} %get-tuple-element.45), channel_id=1, source_target_pairs={{0,4},{4,0},{1,5},{5,1},{2,6},{6,2},{3,7},{7,3},{8,12},{12,8},{9,1... | collective-permute-start | bytes 3194888 | tf_op jit(solution)/shard_map/ppermute | solution.py:643
  3.6 9.5 %collective-permute-start.2 = (bf16[512,256]{1,0:T(8,128)(2,1)S(1)}, bf16[512,256]{1,0:T(8,128)(2,1)S(1)}, u32[]{:S(2)}, u32[]{:S(2)}) collective-permute-start(bf16[512,256]{1,0:T(8,128)(2,1)S(1)} %get-tuple-element.62.refs_0_), channel_id=1, source_target_pairs={{0,8},{4,12},{8,0},{12,4},{16,24},{20,28},{24,16},{28,20},{1,9},{5... | collective-permute-start | bytes 786440 | tf_op jit(solution)/shard_map/ppermute | solution.py:651
  6.5 8.5 %collective-permute-start.3 = (bf16[512,256]{1,0:T(8,128)(2,1)S(1)}, bf16[512,256]{1,0:T(8,128)(2,1)S(1)}, u32[]{:S(2)}, u32[]{:S(2)}) collective-permute-start(bf16[512,256]{1,0:T(8,128)(2,1)S(1)} %get-tuple-element.47), channel_id=1, source_target_pairs={{0,20},{4,16},{8,28},{12,24},{16,4},{20,0},{24,12},{28,8},{1,21},{... | collective-permute-start | bytes 786440 | tf_op jit(solution)/shard_map/ppermute | solution.py:651
  11.7 9.8 %copy-start = (bf16[1,512,4096]{2,1,0:T(8,128)(2,1)S(1)}, bf16[1,512,4096]{2,1,0:T(8,128)(2,1)}, u32[]{:S(2)}) copy-start(bf16[1,512,4096]{2,1,0:T(8,128)(2,1)} %param.12) | copy-start | bytes 12582916
  11.7 9.7 %collective-permute-start.5 = (bf16[512,256]{1,0:T(8,128)(2,1)S(1)}, bf16[512,256]{1,0:T(8,128)(2,1)S(1)}, u32[]{:S(2)}, u32[]{:S(2)}) collective-permute-start(bf16[512,256]{1,0:T(8,128)(2,1)S(1)} %get-tuple-element.62.refs_0_), channel_id=1, source_target_pairs={{0,16},{4,20},{8,24},{12,28},{16,0},{20,4},{24,8},{28,12},{1,17},{... | collective-permute-start | bytes 786440 | tf_op jit(solution)/shard_map/ppermute | solution.py:651
  13.0 8.4 %collective-permute-start.4 = (bf16[512,256]{1,0:T(8,128)(2,1)S(1)}, bf16[512,256]{1,0:T(8,128)(2,1)S(1)}, u32[]{:S(2)}, u32[]{:S(2)}) collective-permute-start(bf16[512,256]{1,0:T(8,128)(2,1)S(1)} %get-tuple-element.47), channel_id=1, source_target_pairs={{0,12},{4,8},{8,4},{12,0},{16,28},{20,24},{24,20},{28,16},{1,13},{... | collective-permute-start | bytes 786440 | tf_op jit(solution)/shard_map/ppermute | solution.py:651
  15.0 11.3 %collective-permute-start.6 = (bf16[512,256]{1,0:T(8,128)(2,1)S(1)}, bf16[512,256]{1,0:T(8,128)(2,1)S(1)}, u32[]{:S(2)}, u32[]{:S(2)}) collective-permute-start(bf16[512,256]{1,0:T(8,128)(2,1)S(1)} %collective-permute-done.2.refs_2_), channel_id=1, source_target_pairs={{0,16},{4,20},{8,24},{12,28},{16,0},{20,4},{24,8},{28,12},{1,17},{... | collective-permute-start | bytes 786440 | tf_op jit(solution)/shard_map/ppermute | solution.py:651
  16.6 10.6 %collective-permute-start.7 = (bf16[512,256]{1,0:T(8,128)(2,1)S(1)}, bf16[512,256]{1,0:T(8,128)(2,1)S(1)}, u32[]{:S(2)}, u32[]{:S(2)}) collective-permute-start(bf16[512,256]{1,0:T(8,128)(2,1)S(1)} %collective-permute-done.3.refs_3_), channel_id=1, source_target_pairs={{0,8},{4,12},{8,0},{12,4},{16,24},{20,28},{24,16},{28,20},{1,9},{5... | collective-permute-start | bytes 786440 | tf_op jit(solution)/shard_map/ppermute | solution.py:651
  31.8 2.5 %collective-permute-start.8 = (bf16[1536,256]{1,0:T(8,128)(2,1)S(1)}, bf16[1536,256]{1,0:T(8,128)(2,1)S(1)}, u32[]{:S(2)}, u32[]{:S(2)}) collective-permute-start(bf16[1536,256]{1,0:T(8,128)(2,1)S(1)} %get-tuple-element.66.grads), channel_id=1, source_target_pairs={{0,4},{4,0},{1,5},{5,1},{2,6},{6,2},{3,7},{7,3},{8,12},{12,8},{9,1... | collective-permute-start | bytes 2359304 | tf_op jit(solution)/shard_map/ppermute | solution.py:643
  31.8 9.1 %collective-permute-start.10 = (bf16[2,256,256]{2,1,0:T(8,128)(2,1)S(1)}, bf16[2,256,256]{2,1,0:T(8,128)(2,1)S(1)}, u32[]{:S(2)}, u32[]{:S(2)}) collective-permute-start(bf16[2,256,256]{2,1,0:T(8,128)(2,1)S(1)} %get-tuple-element.71), channel_id=1, source_target_pairs={{0,8},{4,12},{8,0},{12,4},{16,24},{20,28},{24,16},{28,20},{1,9},{5... | collective-permute-start | bytes 786440 | tf_op jit(solution)/shard_map/ppermute | solution.py:651
  32.7 8.3 %collective-permute-start.11 = (bf16[2,256,256]{2,1,0:T(8,128)(2,1)S(1)}, bf16[2,256,256]{2,1,0:T(8,128)(2,1)S(1)}, u32[]{:S(2)}, u32[]{:S(2)}) collective-permute-start(bf16[2,256,256]{2,1,0:T(8,128)(2,1)S(1)} %get-tuple-element.72), channel_id=1, source_target_pairs={{0,16},{4,20},{8,24},{12,28},{16,0},{20,4},{24,8},{28,12},{1,17},{... | collective-permute-start | bytes 786440 | tf_op jit(solution)/shard_map/ppermute | solution.py:651
  36.9 9.5 %collective-permute-start.9 = (bf16[256,512]{1,0:T(8,128)(2,1)S(1)}, bf16[256,512]{1,0:T(8,128)(2,1)S(1)}, u32[]{:S(2)}, u32[]{:S(2)}) collective-permute-start(bf16[256,512]{1,0:T(8,128)(2,1)S(1)} %get-tuple-element.70.after), channel_id=1, source_target_pairs={{0,8},{4,12},{8,0},{12,4},{16,24},{20,28},{24,16},{28,20},{1,9},{5... | collective-permute-start | bytes 786440 | tf_op jit(solution)/shard_map/ppermute | solution.py:651
  38.3 13.0 %collective-permute-start.12 = (bf16[256,512]{1,0:T(8,128)(2,1)S(1)}, bf16[256,512]{1,0:T(8,128)(2,1)S(1)}, u32[]{:S(2)}, u32[]{:S(2)}) collective-permute-start(bf16[256,512]{1,0:T(8,128)(2,1)S(1)} %get-tuple-element.77), channel_id=1, source_target_pairs={{0,16},{4,20},{8,24},{12,28},{16,0},{20,4},{24,8},{28,12},{1,17},{... | collective-permute-start | bytes 786440 | tf_op jit(solution)/shard_map/ppermute | solution.py:651
  41.7 8.3 %collective-permute-start.13 = (bf16[256,256]{1,0:T(8,128)(2,1)S(1)}, bf16[256,256]{1,0:T(8,128)(2,1)S(1)}, u32[]{:S(2)}, u32[]{:S(2)}) collective-permute-start(bf16[256,256]{1,0:T(8,128)(2,1)S(1)} %get-tuple-element.78), channel_id=1, source_target_pairs={{0,16},{4,20},{8,24},{12,28},{16,0},{20,4},{24,8},{28,12},{1,17},{... | collective-permute-start | bytes 393224 | tf_op jit(solution)/shard_map/ppermute | solution.py:651
  43.8 6.2 %collective-permute-start.14 = (bf16[256,256]{1,0:T(8,128)(2,1)S(1)}, bf16[256,256]{1,0:T(8,128)(2,1)S(1)}, u32[]{:S(2)}, u32[]{:S(2)}) collective-permute-start(bf16[256,256]{1,0:T(8,128)(2,1)S(1)} %get-tuple-element.79), channel_id=1, source_target_pairs={{0,8},{4,12},{8,0},{12,4},{16,24},{20,28},{24,16},{28,20},{1,9},{5... | collective-permute-start | bytes 393224 | tf_op jit(solution)/shard_map/ppermute | solution.py:651
  45.5 5.9 %collective-permute-start.15 = (bf16[256,256]{1,0:T(8,128)(2,1)S(1)}, bf16[256,256]{1,0:T(8,128)(2,1)S(1)}, u32[]{:S(2)}, u32[]{:S(2)}) collective-permute-start(bf16[256,256]{1,0:T(8,128)(2,1)S(1)} %get-tuple-element.80), channel_id=1, source_target_pairs={{0,20},{4,16},{8,28},{12,24},{16,4},{20,0},{24,12},{28,8},{1,21},{... | collective-permute-start | bytes 393224 | tf_op jit(solution)/shard_map/ppermute | solution.py:651
  46.5 5.3 %collective-permute-start.16 = (bf16[256,256]{1,0:T(8,128)(2,1)S(1)}, bf16[256,256]{1,0:T(8,128)(2,1)S(1)}, u32[]{:S(2)}, u32[]{:S(2)}) collective-permute-start(bf16[256,256]{1,0:T(8,128)(2,1)S(1)} %get-tuple-element.81), channel_id=1, source_target_pairs={{0,12},{4,8},{8,4},{12,0},{16,28},{20,24},{24,20},{28,16},{1,13},{... | collective-permute-start | bytes 393224 | tf_op jit(solution)/shard_map/ppermute | solution.py:651
